TPU v7x, 32 devices: a whole 2x2x4 slice. The times are simulated.
32 devices in a mesh: section: 2 (over core), tensor: 4 (over y, x), dp: 4 (over z).
Axes of the slice: x: 2, y: 2, z: 4, core: 2. Of those that a mesh axis runs over, the one named last changes fastest.
Arguments:
- inputs: bfloat16 [8, 1024, 768], P('dp', 'tensor'), may hold values from -6 to 6
- lengths: int32 [8], P('dp'), may hold values from 512 to 1024, as said below
- gains: bfloat16 [2, 2, 768], P('section', None, 'dp'), may hold values from 0.099609375 to 1.8984375
- w_qkv: bfloat16 [2, 768, 3, 768], P('section', 'dp', None, 'tensor'), may hold values from -0.21875 to 0.21875
- w_out: bfloat16 [2, 768, 768], P('section', 'tensor', 'dp'), may hold values from -1.75 to 1.75
- w_up: bfloat16 [2, 768, 3072], P('section', 'dp', 'tensor'), may hold values from -0.21875 to 0.21875
- w_down: bfloat16 [2, 3072, 768], P('section', 'tensor', 'dp'), may hold values from -0.109375 to 0.109375
- cotangent: bfloat16 [8, 1024, 768], P('dp', 'tensor'), may hold values from -6 to 6
Outputs:
- activations: bfloat16 [2, 8, 1024, 768], P('section', 'dp', 'tensor')
- input_grads: bfloat16 [2, 8, 1024, 768], P('section', 'dp', 'tensor')
- gain_grads: float32 [2, 2, 768], P('section', None, ('tensor', 'dp'))
- qkv_grads: float32 [2, 768, 3, 768], P('section', 'dp', None, 'tensor')
- out_grads: float32 [2, 768, 768], P('section', 'tensor', 'dp')
- up_grads: float32 [2, 768, 3072], P('section', 'dp', 'tensor')
- down_grads: float32 [2, 3072, 768], P('section', 'tensor', 'dp')
Inputs may be any that keep to these rules, and one draw needn't show every extreme that they name: `lengths`: each entry is the first document's length in a bucket of 1024 positions, either 1024 // 2 or 1024; the rest of the bucket is a second document. Among the 2 buckets of each data group one holds a single document and another holds two.
All inputs are finite; a program needn't handle non-finite values.
Results may differ from a plain program's by a relative error of at most 0.038.
Values may be sent and summed in bfloat16 or wider, within the bound.
A program may use at most 192 MiB of HBM per device.

v0:
```python
import jax
import jax.numpy as jnp
from jax import lax
from jax.sharding import PartitionSpec as P

HEAD = 64


epsilon = 1e-05


def from_behind(value, axis, by):
    length = lax.axis_size(axis)
    pairs = [(i, i + by) for i in range(length) if 0 <= i + by < length]
    return lax.ppermute(value, axis, pairs)


def normalize(row_block, gain_row):
    centre = row_block - jnp.mean(row_block, axis=-1, keepdims=True)
    spread = jnp.mean(centre * centre, axis=-1, keepdims=True)
    return centre * lax.rsqrt(spread + epsilon) * gain_row


def smooth_gelu(value_rows):
    return jax.nn.gelu(value_rows, approximate=True)


def score_terms(scores, cog_share):
    radius = jnp.sqrt(scores * scores + 1.0)
    magnitude = cog_share * radius + (1.0 - cog_share) * scores
    direction = cog_share * scores / radius + (1.0 - cog_share)
    return (radius, magnitude, direction)


def visible_pairs(first_len, row_start, row_total, key_total):
    query_pos = row_start + lax.broadcasted_iota(jnp.int32, (row_total, key_total), 0)
    key_pos = lax.broadcasted_iota(jnp.int32, (row_total, key_total), 1)
    return (key_pos <= query_pos) & ((query_pos >= first_len) == (key_pos >= first_len))


def contract_rows(left, right):
    return lax.dot_general(
        left, right, (((0,), (0,)), ((), ())), preferred_element_type=jnp.float32
    )


def contract_cols(left, right):
    return lax.dot_general(
        left, right, (((1,), (1,)), ((), ())), preferred_element_type=jnp.float32
    )


def gathered_rows(local_piece):
    return lax.all_gather(local_piece, "tensor", axis=0, tiled=True)


def gathered_grads(local_piece):
    return lax.all_gather(local_piece, "tensor", axis=0, tiled=True)


def summed_branch(term_fn, local_rows):
    return lax.psum_scatter(
        term_fn(jnp.int32(0), lax.axis_size("tensor") * local_rows).astype(jnp.bfloat16),
        "tensor",
        scatter_dimension=0,
        tiled=True,
    ).astype(jnp.float32)


def summed_grads(term_fn, local_rows):
    return lax.psum_scatter(
        term_fn(jnp.int32(0), lax.axis_size("tensor") * local_rows).astype(jnp.bfloat16),
        "tensor",
        scatter_dimension=0,
        tiled=True,
    ).astype(jnp.float32)


def attend(query_rows, key_rows, value_rows, first_len, cog_share):
    row_count = query_rows.shape[0]
    block_rows = min(512, row_count)
    score_scale = query_rows.shape[-1] ** (-0.5)
    out_blocks = []
    log_blocks = []
    for block_index in range(row_count // block_rows):
        row_start = block_index * block_rows
        row_end = row_start + block_rows
        scores = (
            jnp.einsum(
                "qhd,khd->hqk",
                query_rows[row_start:row_end],
                key_rows[:row_end],
                preferred_element_type=jnp.float32,
            )
            * score_scale
        )
        radius, magnitude, direction = score_terms(scores, cog_share)
        visible = visible_pairs(first_len, row_start, block_rows, row_end)[None]
        masked_mag = jnp.where(visible, magnitude, -1e30)
        row_max = jnp.max(masked_mag, axis=-1, keepdims=True)
        weights = jnp.exp(masked_mag - row_max)
        weight_sum = jnp.sum(weights, axis=-1, keepdims=True)
        probabilities = (direction * weights / weight_sum).astype(jnp.bfloat16)
        out_rows = jnp.einsum(
            "hqk,khd->qhd", probabilities, value_rows[:row_end], preferred_element_type=jnp.float32
        )
        out_blocks.append(out_rows.astype(jnp.bfloat16))
        log_blocks.append((row_max + jnp.log(weight_sum))[..., 0])
    return (jnp.concatenate(out_blocks, axis=0), jnp.concatenate(log_blocks, axis=1))


def attend_back(query_rows, key_rows, value_rows, attn_grad, log_totals, first_len, cog_share):
    row_count, heads_local, head_size = query_rows.shape
    block_rows = min(512, row_count)
    score_scale = head_size ** (-0.5)
    query_blocks = []
    key_grad = jnp.zeros((row_count, heads_local, head_size), jnp.float32)
    value_grad = jnp.zeros((row_count, heads_local, head_size), jnp.float32)
    for block_index in range(row_count // block_rows):
        row_start = block_index * block_rows
        row_end = row_start + block_rows
        query_block = query_rows[row_start:row_end]
        grad_block = attn_grad[row_start:row_end]
        scores = (
            jnp.einsum(
                "qhd,khd->hqk", query_block, key_rows[:row_end], preferred_element_type=jnp.float32
            )
            * score_scale
        )
        radius, magnitude, direction = score_terms(scores, cog_share)
        visible = visible_pairs(first_len, row_start, block_rows, row_end)[None]
        weights = jnp.exp(
            jnp.where(visible, magnitude, -1e30) - log_totals[:, row_start:row_end, None]
        )
        signed = direction * weights
        prob_grad = jnp.einsum(
            "qhd,khd->hqk", grad_block, value_rows[:row_end], preferred_element_type=jnp.float32
        )
        row_inner = jnp.sum(signed * prob_grad, axis=-1, keepdims=True)
        score_grad = weights * (
            direction * (direction * prob_grad - row_inner)
            + cog_share * prob_grad / (radius * radius * radius)
        )
        score_grad = score_grad.astype(jnp.bfloat16)
        query_blocks.append(
            jnp.einsum(
                "hqk,khd->qhd", score_grad, key_rows[:row_end], preferred_element_type=jnp.float32
            )
            * score_scale
        )
        key_grad = key_grad.at[:row_end].add(
            jnp.einsum("hqk,qhd->khd", score_grad, query_block, preferred_element_type=jnp.float32)
            * score_scale
        )
        value_grad = value_grad.at[:row_end].add(
            jnp.einsum(
                "hqk,qhd->khd",
                signed.astype(jnp.bfloat16),
                grad_block,
                preferred_element_type=jnp.float32,
            )
        )
    return (jnp.concatenate(query_blocks, axis=0), key_grad, value_grad)


def block_forward(row_block, first_len, cog_share, layer_weights):
    gain_pair, qkv_weight, out_weight, up_weight, down_weight = layer_weights
    local_rows = row_block.shape[0]
    heads_local = out_weight.shape[0] // HEAD
    norm_one = normalize(row_block, gain_pair[0]).astype(jnp.bfloat16)
    norm_all = gathered_rows(norm_one)
    row_count = norm_all.shape[0]
    packed = jnp.dot(norm_all, qkv_weight, preferred_element_type=jnp.float32).astype(jnp.bfloat16)
    packed = packed.reshape(row_count, 3, heads_local, HEAD)
    attn_rows, log_totals = attend(packed[:, 0], packed[:, 1], packed[:, 2], first_len, cog_share)
    attn_rows = attn_rows.reshape(row_count, -1)

    def attn_term(row_start, row_total):
        return jnp.dot(attn_rows, out_weight, preferred_element_type=jnp.float32)

    middle = row_block + summed_branch(attn_term, local_rows)
    norm_two = normalize(middle, gain_pair[1]).astype(jnp.bfloat16)
    norm_all_two = gathered_rows(norm_two)
    hidden_pre = jnp.dot(norm_all_two, up_weight, preferred_element_type=jnp.float32)
    hidden = smooth_gelu(hidden_pre).astype(jnp.bfloat16)

    def mlp_term(row_start, row_total):
        return jnp.dot(hidden, down_weight, preferred_element_type=jnp.float32)

    result = middle + summed_branch(mlp_term, local_rows)
    norm_kept = (norm_all, norm_all_two)
    return (
        result,
        (row_block, middle, norm_kept[0], norm_kept[1], packed, attn_rows, log_totals, hidden_pre),
    )


def block_backward(grad_rows_in, kept_state, first_len, cog_share, layer_weights):
    gain_pair, qkv_weight, out_weight, up_weight, down_weight = layer_weights
    row_block, middle, norm_first, norm_second, packed, attn_rows, log_totals, hidden_pre = (
        kept_state
    )
    local_rows = row_block.shape[0]
    row_count = norm_first.shape[0]
    heads_local = out_weight.shape[0] // HEAD
    mlp_grad = gathered_grads(grad_rows_in.astype(jnp.bfloat16))
    hidden = smooth_gelu(hidden_pre).astype(jnp.bfloat16)
    down_grad = contract_rows(hidden, mlp_grad)
    hidden_grad = contract_cols(mlp_grad, down_weight)
    gelu_pull = jax.vjp(smooth_gelu, hidden_pre)[1]
    pre_grad = gelu_pull(hidden_grad)[0].astype(jnp.bfloat16)
    up_grad = contract_rows(norm_second, pre_grad)
    second_pull = jax.vjp(normalize, middle, gain_pair[1])[1]

    def up_term(row_start, row_total):
        return contract_cols(pre_grad, up_weight)

    norm_two_grad = summed_grads(up_term, local_rows)
    middle_part, second_gain = second_pull(norm_two_grad)
    middle_grad = grad_rows_in + middle_part
    branch_grad = gathered_grads(middle_grad.astype(jnp.bfloat16))
    out_grad = contract_rows(attn_rows, branch_grad)
    attn_grad = contract_cols(branch_grad, out_weight).astype(jnp.bfloat16)
    query_grad, key_grad, value_grad = attend_back(
        packed[:, 0],
        packed[:, 1],
        packed[:, 2],
        attn_grad.reshape(row_count, heads_local, HEAD),
        log_totals,
        first_len,
        cog_share,
    )
    packed_grad = (
        jnp.stack([query_grad, key_grad, value_grad], axis=1)
        .astype(jnp.bfloat16)
        .reshape(row_count, -1)
    )
    qkv_grad = contract_rows(norm_first, packed_grad)

    def qkv_term(row_start, row_total):
        return contract_cols(packed_grad, qkv_weight)

    first_pull = jax.vjp(normalize, row_block, gain_pair[0])[1]
    row_part, first_gain = first_pull(summed_grads(qkv_term, local_rows))
    return (
        middle_grad + row_part,
        (qkv_grad, out_grad, up_grad, down_grad),
        jnp.stack([first_gain, second_gain]),
    )


def shards(inputs, lengths, gains, w_qkv, w_out, w_up, w_down, cotangent):
    gathered = (
        lax.all_gather(gains, "dp", axis=2, tiled=True),
        lax.all_gather(w_qkv, "dp", axis=1, tiled=True),
        lax.all_gather(w_out, "dp", axis=2, tiled=True),
        lax.all_gather(w_up, "dp", axis=1, tiled=True),
        lax.all_gather(w_down, "dp", axis=2, tiled=True),
    )
    model_width = gathered[1].shape[1]
    up_use = gathered[3][0]
    down_use = gathered[4][0]
    layer_weights = (
        gathered[0][0].astype(jnp.float32),
        gathered[1][0].reshape(model_width, -1),
        gathered[2][0],
        up_use,
        down_use,
    )
    leading = lax.axis_index("section") == 0
    cog_share = leading.astype(jnp.float32)
    bucket_count, local_rows, feature_count = inputs.shape
    blank_rows = jnp.zeros((local_rows, feature_count), jnp.bfloat16)
    ahead_rows = blank_rows
    behind = blank_rows
    stashed = []
    produced = []
    returned = []
    grad_total = None
    gain_total = jnp.zeros((2, feature_count), jnp.float32)
    for moment in range(bucket_count + 2):
        if moment <= bucket_count:
            own_rows = inputs[moment] if moment < bucket_count else blank_rows
            start_rows = jnp.where(leading, own_rows, ahead_rows)
            first_len = jnp.where(
                leading, lengths[min(moment, bucket_count - 1)], lengths[max(moment - 1, 0)]
            )
            result, kept_state = block_forward(
                start_rows.astype(jnp.float32), first_len, cog_share, layer_weights
            )
            sent_rows = result.astype(jnp.bfloat16)
            stashed.append((kept_state, first_len))
            produced.append(sent_rows)
            if moment < bucket_count:
                ahead_rows = from_behind(sent_rows, "section", 1)
        if moment >= 1:
            chosen = jax.tree.map(
                lambda earlier, lagging: jnp.where(leading, earlier, lagging),
                stashed[max(moment - 2, 0)],
                stashed[min(moment, bucket_count)],
            )
            incoming = cotangent[moment - 1] if moment - 1 < bucket_count else blank_rows
            grad_start = jnp.where(leading, behind, incoming).astype(jnp.float32)
            live_flag = jnp.where(leading, moment >= 2, moment <= bucket_count).astype(jnp.float32)
            grad_rows_out, layer_grads, gain_part = block_backward(
                grad_start, chosen[0], chosen[1], cog_share, layer_weights
            )
            gain_total = gain_total + live_flag * gain_part
            qkv_part = layer_grads[0].reshape(1, model_width, 3, -1) * live_flag
            out_part = layer_grads[1][None] * live_flag
            up_part = layer_grads[2][None] * live_flag
            down_part = layer_grads[3][None] * live_flag
            grad_back = grad_rows_out.astype(jnp.bfloat16)
            returned.append(grad_back)
            if moment <= bucket_count:
                behind = from_behind(grad_back, "section", -1)
            shard_grads = (qkv_part, out_part, up_part, down_part)
            if grad_total is None:
                grad_total = shard_grads
            else:
                grad_total = jax.tree.map(jnp.add, grad_total, shard_grads)
    grad_total = (
        lax.psum_scatter(
            grad_total[0].astype(jnp.bfloat16), "dp", scatter_dimension=1, tiled=True
        ).astype(jnp.float32),
        lax.psum_scatter(
            grad_total[1].astype(jnp.bfloat16), "dp", scatter_dimension=2, tiled=True
        ).astype(jnp.float32),
        lax.psum_scatter(
            grad_total[2].astype(jnp.bfloat16), "dp", scatter_dimension=1, tiled=True
        ).astype(jnp.float32),
        lax.psum_scatter(
            grad_total[3].astype(jnp.bfloat16), "dp", scatter_dimension=2, tiled=True
        ).astype(jnp.float32),
    )
    activations = jnp.stack(
        [
            jnp.where(leading, produced[bucket_slot], produced[bucket_slot + 1])
            for bucket_slot in range(bucket_count)
        ]
    )[None]
    input_grads = jnp.stack(
        [
            jnp.where(leading, returned[bucket_slot + 1], returned[bucket_slot])
            for bucket_slot in range(bucket_count)
        ]
    )[None]
    gain_shard = lax.psum_scatter(
        gain_total[None], ("tensor", "dp"), scatter_dimension=2, tiled=True
    )
    return (
        activations,
        input_grads,
        gain_shard,
        grad_total[0],
        grad_total[1],
        grad_total[2],
        grad_total[3],
    )


def solution(mesh):
    in_specs = (
        P("dp", "tensor", None),
        P("dp"),
        P("section", None, "dp"),
        P("section", "dp", None, "tensor"),
        P("section", "tensor", "dp"),
        P("section", "dp", "tensor"),
        P("section", "tensor", "dp"),
        P("dp", "tensor", None),
    )
    out_specs = (
        P("section", "dp", "tensor", None),
        P("section", "dp", "tensor", None),
        P("section", None, ("tensor", "dp")),
        P("section", "dp", None, "tensor"),
        P("section", "tensor", "dp"),
        P("section", "dp", "tensor"),
        P("section", "tensor", "dp"),
    )
    return jax.shard_map(shards, mesh=mesh, in_specs=in_specs, out_specs=out_specs, check_vma=False)
```

profile of v0, /device:TPU:0, one launch (start us, length us, event | category | flops | bytes accessed | tf_op | source)
XLA Modules:
  0.0 1321.3 jit_solution(9142517071162860806)
XLA Ops:
  11.4 16.2 %all_gather.51 = bf16[1,2,768]{1,0,2:T(2,128)(2,1)S(1)} all-gather(bf16[1,2,192]{1,0,2:T(2,128)(2,1)S(1)} %copy.62), channel_id=1, replica_groups=mesh['section'=2,'tensor'=4,'dp'=4] {'dp'}, dimensions={2}, use_global_device_ids=true | all-gather | bytes 3840 | tf_op jit(solution)/shard_map/all_gather | solution.py:254
  38.4 28.6 %all_gather.53 = bf16[1,768,3,192]{3,2,0,1:T(4,128)(2,1)S(1)} all-gather(bf16[1,192,3,192]{3,2,0,1:T(4,128)(2,1)S(1)} %copy.63), channel_id=1, replica_groups=mesh['section'=2,'tensor'=4,'dp'=4] {'dp'}, dimensions={1}, use_global_device_ids=true | all-gather | bytes 1105920 | tf_op jit(solution)/shard_map/all_gather | solution.py:255
  69.2 17.2 %all_gather.54 = bf16[1,192,768]{1,0,2:T(2,128)(2,1)S(1)} all-gather(bf16[1,192,192]{1,0,2:T(2,128)(2,1)S(1)} %copy.66), channel_id=1, replica_groups=mesh['section'=2,'tensor'=4,'dp'=4] {'dp'}, dimensions={2}, use_global_device_ids=true | all-gather | bytes 368640 | tf_op jit(solution)/shard_map/all_gather | solution.py:256
  113.8 6.1 fusion.282
  122.3 31.0 %reduce-scatter.26.cloned.1.call-done = bf16[256,768]{1,0:T(8,128)(2,1)} async-done(((bf16[1024,768]{1,0:T(8,128)(2,1)}), bf16[256,768]{1,0:T(8,128)(2,1)}) %reduce-scatter.26.cloned.1.call-update) | async-done | bytes 393232 | tf_op jit(solution)/shard_map/reduce_scatter | solution.py:62
  158.6 30.1 %all-gather.18.cloned.1.call-done = bf16[1024,768]{1,0:T(8,128)(2,1)} async-done(((bf16[256,768]{1,0:T(8,128)(2,1)}), bf16[1024,768]{1,0:T(8,128)(2,1)}) %all-gather.18.cloned.1.call-update) | async-done | bytes 1572880 | tf_op jit(solution)/shard_map/all_gather | solution.py:54
  193.5 26.9 %all-gather.22.cloned.1.call-done = bf16[1,768,768]{1,2,0:T(8,128)(2,1)} async-done(((bf16[1,768,192]{1,2,0:T(8,128)(2,1)}), bf16[1,768,768]{1,2,0:T(8,128)(2,1)}) %all-gather.22.cloned.1.call-update) | async-done | bytes 1179664 | tf_op jit(solution)/shard_map/all_gather | solution.py:258
  220.3 5.4 convolution_convert_fusion.10
  225.8 30.2 %reduce-scatter.28.cloned.1.call-done = bf16[256,768]{1,0:T(8,128)(2,1)} async-done(((bf16[1024,768]{1,0:T(8,128)(2,1)}), bf16[256,768]{1,0:T(8,128)(2,1)}) %reduce-scatter.28.cloned.1.call-update) | async-done | bytes 393232 | tf_op jit(solution)/shard_map/reduce_scatter | solution.py:62
  262.0 30.6 %all-gather.24.cloned.1.call-done = bf16[1024,768]{1,0:T(8,128)(2,1)} async-done(((bf16[256,768]{1,0:T(8,128)(2,1)}), bf16[1024,768]{1,0:T(8,128)(2,1)}) %all-gather.24.cloned.1.call-update) | async-done | bytes 1572880 | tf_op jit(solution)/shard_map/all_gather | solution.py:54
  312.6 6.0 fusion.283
  320.5 30.9 %reduce-scatter.30.cloned.1.call-done = bf16[256,768]{1,0:T(8,128)(2,1)} async-done(((bf16[1024,768]{1,0:T(8,128)(2,1)}), bf16[256,768]{1,0:T(8,128)(2,1)}) %reduce-scatter.30.cloned.1.call-update) | async-done | bytes 393232 | tf_op jit(solution)/shard_map/reduce_scatter | solution.py:62
  358.2 28.7 %all-gather.26.cloned.1.call-done = bf16[1024,768]{1,0:T(8,128)(2,1)} async-done(((bf16[256,768]{1,0:T(8,128)(2,1)}), bf16[1024,768]{1,0:T(8,128)(2,1)}) %all-gather.26.cloned.1.call-update) | async-done | bytes 1572880 | tf_op jit(solution)/shard_map/all_gather | solution.py:54
  391.7 28.5 %all-gather.42.cloned.1.call-done = bf16[1,1024,768]{2,1,0:T(8,128)(2,1)} async-done(((bf16[1,256,768]{2,1,0:T(8,128)(2,1)}), bf16[1,1024,768]{2,1,0:T(8,128)(2,1)}) %all-gather.42.cloned.1.call-update) | async-done | bytes 1572880 | tf_op jit(solution)/shard_map/all_gather | solution.py:58
  420.2 5.7 fusion.36
  429.7 5.4 convolution_convert_fusion.8
  435.4 25.2 %reduce-scatter.38.cloned.1.call-done = bf16[256,768]{1,0:T(8,128)(2,1)} async-done(((bf16[1024,768]{1,0:T(8,128)(2,1)}), bf16[256,768]{1,0:T(8,128)(2,1)}) %reduce-scatter.38.cloned.1.call-update) | async-done | bytes 393232 | tf_op jit(solution)/shard_map/reduce_scatter | solution.py:71
  465.9 37.5 %reduce-scatter.32.cloned.1.call-done = bf16[256,768]{1,0:T(8,128)(2,1)} async-done(((bf16[1024,768]{1,0:T(8,128)(2,1)}), bf16[256,768]{1,0:T(8,128)(2,1)}) %reduce-scatter.32.cloned.1.call-update) | async-done | bytes 393232 | tf_op jit(solution)/shard_map/reduce_scatter | solution.py:62
  517.8 23.1 %all-gather.28.cloned.1.call-done = bf16[1024,768]{1,0:T(8,128)(2,1)} async-done(((bf16[256,768]{1,0:T(8,128)(2,1)}), bf16[1024,768]{1,0:T(8,128)(2,1)}) %all-gather.28.cloned.1.call-update) | async-done | bytes 1572880 | tf_op jit(solution)/shard_map/all_gather | solution.py:54
  562.0 5.3 fusion.105
  567.3 7.3 fusion.95
  579.8 9.2 fusion.21
  589.1 12.7 fusion.20
  618.5 8.3 fusion.284
  629.5 14.7 %reduce-scatter.40.cloned.1.call-done = bf16[256,768]{1,0:T(8,128)(2,1)} async-done(((bf16[1024,768]{1,0:T(8,128)(2,1)}), bf16[256,768]{1,0:T(8,128)(2,1)}) %reduce-scatter.40.cloned.1.call-update) | async-done | bytes 393232 | tf_op jit(solution)/shard_map/reduce_scatter | solution.py:71
  646.2 31.8 %reduce-scatter.34.cloned.1.call-done = bf16[256,768]{1,0:T(8,128)(2,1)} async-done(((bf16[1024,768]{1,0:T(8,128)(2,1)}), bf16[256,768]{1,0:T(8,128)(2,1)}) %reduce-scatter.34.cloned.1.call-update) | async-done | bytes 393232 | tf_op jit(solution)/shard_map/reduce_scatter | solution.py:62
  690.4 23.0 %all-gather.30.cloned.1.call-done = bf16[1024,768]{1,0:T(8,128)(2,1)} async-done(((bf16[256,768]{1,0:T(8,128)(2,1)}), bf16[1024,768]{1,0:T(8,128)(2,1)}) %all-gather.30.cloned.1.call-update) | async-done | bytes 1572880 | tf_op jit(solution)/shard_map/all_gather | solution.py:54
  718.3 28.5 %all-gather.34.cloned.1.call-done = bf16[1024,768]{1,0:T(8,128)(2,1)} async-done(((bf16[256,768]{1,0:T(8,128)(2,1)}), bf16[1024,768]{1,0:T(8,128)(2,1)}) %all-gather.34.cloned.1.call-update) | async-done | bytes 1572880 | tf_op jit(solution)/shard_map/all_gather | solution.py:58
  746.8 5.7 fusion.43
  757.1 30.3 %reduce-scatter.42.cloned.1.call-done = bf16[256,768]{1,0:T(8,128)(2,1)} async-done(((bf16[1024,768]{1,0:T(8,128)(2,1)}), bf16[256,768]{1,0:T(8,128)(2,1)}) %reduce-scatter.42.cloned.1.call-update) | async-done | bytes 393232 | tf_op jit(solution)/shard_map/reduce_scatter | solution.py:71
  794.8 6.7 fusion.106
  801.5 8.8 fusion.22
  810.3 13.2 all-gather.36.cloned.1.call-done
  826.3 8.4 fusion.94
  841.1 14.8 %fusion.19 = bf16[3,512,1024]{2,1,0:T(8,128)(2,1)} fusion(f32[3,512,1024]{2,1,0:T(8,128)} %get-tuple-element.330, f32[3,512]{1,0:T(4,128)S(1)} %get-tuple-element.296, f32[]{:T(128)S(6)} %mul.1122, f32[]{:T(128)S(6)} %convert_element_type.371, f32[]{:T(128)S(6)} %sub.130, f32[]{:T(128)S(6)} %mul.1115, pred[512,1024]{1,0:T(8,128)(4,1)} %get-tuple-element.300, ...), kind=kOutput, calls=%fused_computation.46 | convolution fusion | flops 437258752 | bytes 17438736 | tf_op jit(solution)/shard_map/sub | solution.py:141
  868.4 31.0 %reduce-scatter.44.cloned.1.call-done = bf16[256,768]{1,0:T(8,128)(2,1)} async-done(((bf16[1024,768]{1,0:T(8,128)(2,1)}), bf16[256,768]{1,0:T(8,128)(2,1)}) %reduce-scatter.44.cloned.1.call-update) | async-done | bytes 393232 | tf_op jit(solution)/shard_map/reduce_scatter | solution.py:71
  909.4 30.7 %all-gather.38.cloned.1.call-done = bf16[1024,768]{1,0:T(8,128)(2,1)} async-done(((bf16[256,768]{1,0:T(8,128)(2,1)}), bf16[1024,768]{1,0:T(8,128)(2,1)}) %all-gather.38.cloned.1.call-update) | async-done | bytes 1572880 | tf_op jit(solution)/shard_map/all_gather | solution.py:58
  940.1 5.6 fusion.50
  962.4 19.4 %reduce-scatter.46.cloned.1.call-done = bf16[256,768]{1,0:T(8,128)(2,1)} async-done(((bf16[1024,768]{1,0:T(8,128)(2,1)}), bf16[256,768]{1,0:T(8,128)(2,1)}) %reduce-scatter.46.cloned.1.call-update) | async-done | bytes 393232 | tf_op jit(solution)/shard_map/reduce_scatter | solution.py:71
  986.0 11.6 fusion.23
  1003.9 5.8 copy.99
  1011.2 6.6 fusion.107
  1030.0 12.9 fusion.18
  1042.9 7.2 fusion.93
  1094.3 24.9 %reduce-scatter.54.cloned.1.call-done = bf16[192,576]{1,0:T(8,128)(2,1)} async-done(((bf16[768,576]{1,0:T(8,128)(2,1)}), bf16[192,576]{1,0:T(8,128)(2,1)}) %reduce-scatter.54.cloned.1.call-update) | async-done | bytes 221200
  1121.6 30.1 %reduce-scatter.48.cloned.1.call-done = bf16[256,768]{1,0:T(8,128)(2,1)} async-done(((bf16[1024,768]{1,0:T(8,128)(2,1)}), bf16[256,768]{1,0:T(8,128)(2,1)}) %reduce-scatter.48.cloned.1.call-update) | async-done | bytes 393232 | tf_op jit(solution)/shard_map/reduce_scatter | solution.py:71
  1155.9 29.7 %reduce-scatter.36.cloned.1.call-done = bf16[256,768]{1,0:T(8,128)(2,1)} async-done(((bf16[1024,768]{1,0:T(8,128)(2,1)}), bf16[256,768]{1,0:T(8,128)(2,1)}) %reduce-scatter.36.cloned.1.call-update) | async-done | bytes 393232 | tf_op jit(solution)/shard_map/reduce_scatter | solution.py:62
  1189.4 122.4 %reduce-scatter.52.cloned.1.call-done = f32[48,2]{1,0:T(8,128)} async-done(((f32[768,2]{1,0:T(8,128)}), f32[48,2]{1,0:T(8,128)}) %reduce-scatter.52.cloned.1.call-update) | async-done | bytes 400
  (581 shorter events, 318.7 us)
Async XLA Ops:
  8.0 85.9 %all-gather.16.cloned.1.call-start = ((), (), s32[]{:S(2)}) async-start(), calls=%async_computation.17 | async-start | bytes 1966080 | tf_op jit(solution)/shard_map/all_gather | solution.py:54
  32.6 36.4 %copy-start.82 = (bf16[1,192,192]{2,1,0:T(8,128)(2,1)S(1)}, bf16[1,192,192]{2,1,0:T(8,128)(2,1)}, u32[]{:S(2)}) copy-start(bf16[1,192,192]{2,1,0:T(8,128)(2,1)} %param.48) | copy-start | bytes 221188
  33.6 119.7 %reduce-scatter.26.cloned.1.call-start = ((), (), s32[]{:S(2)}) async-start(), calls=%async_computation.18 | async-start | bytes 1966080 | tf_op jit(solution)/shard_map/reduce_scatter | solution.py:62
  86.9 428.1 %copy-start.23 = (bf16[1,192,768]{2,1,0:T(8,128)(2,1)}, bf16[1,192,768]{2,1,0:T(8,128)(2,1)S(1)}, u32[]{:S(2)}) copy-start(bf16[1,192,768]{2,1,0:T(8,128)(2,1)S(1)} %copy.67) | copy-start | bytes 884740
  119.9 37.9 %copy-start.18 = (bf16[1024,3,64]{0,2,1:T(8,128)(2,1)}, bf16[1024,3,64]{0,2,1:T(8,128)(2,1)S(1)}, u32[]{:S(2)}) copy-start(bf16[1024,3,64]{0,2,1:T(8,128)(2,1)S(1)} %pad_maximum_fusion) | copy-start | bytes 1179652
  121.7 36.9 %all-gather.20.cloned.1.call-start = ((), (), s32[]{:S(2)}) async-start(), calls=%async_computation.20 | async-start | bytes 1474560 | tf_op jit(solution)/shard_map/all_gather | solution.py:257
  122.3 66.4 %all-gather.18.cloned.1.call-start = ((), (), s32[]{:S(2)}) async-start(), calls=%async_computation.19 | async-start | bytes 1966080 | tf_op jit(solution)/shard_map/all_gather | solution.py:54
  157.8 62.6 %all-gather.22.cloned.1.call-start = ((), (), s32[]{:S(2)}) async-start(), calls=%async_computation.21 | async-start | bytes 1474560 | tf_op jit(solution)/shard_map/all_gather | solution.py:258
  158.4 97.7 %reduce-scatter.28.cloned.1.call-start = ((), (), s32[]{:S(2)}) async-start(), calls=%async_computation.22 | async-start | bytes 1966080 | tf_op jit(solution)/shard_map/reduce_scatter | solution.py:62
  193.5 62.5 %copy-start.6 = (bf16[256,768]{1,0:T(8,128)(2,1)S(1)}, bf16[256,768]{1,0:T(8,128)(2,1)}, u32[]{:S(2)}) copy-start(bf16[256,768]{1,0:T(8,128)(2,1)} %reduce-scatter.26.cloned.1.call-done) | copy-start | bytes 1179652
  225.7 66.9 %all-gather.24.cloned.1.call-start = ((), (), s32[]{:S(2)}) async-start(), calls=%async_computation.23 | async-start | bytes 1966080 | tf_op jit(solution)/shard_map/all_gather | solution.py:54
  257.2 3.1 collective-permute-start
  260.5 422.5 %copy-start = (bf16[256,768]{1,0:T(8,128)(2,1)}, bf16[256,768]{1,0:T(8,128)(2,1)S(1)}, u32[]{:S(2)}) copy-start(bf16[256,768]{1,0:T(8,128)(2,1)S(1)} %get-tuple-element.269) | copy-start | bytes 1179652
  261.8 89.7 %reduce-scatter.30.cloned.1.call-start = ((), (), s32[]{:S(2)}) async-start(), calls=%async_computation.24 | async-start | bytes 1966080 | tf_op jit(solution)/shard_map/reduce_scatter | solution.py:62
  320.5 66.4 %all-gather.26.cloned.1.call-start = ((), (), s32[]{:S(2)}) async-start(), calls=%async_computation.25 | async-start | bytes 1966080 | tf_op jit(solution)/shard_map/all_gather | solution.py:54
  355.8 64.4 %all-gather.42.cloned.1.call-start = ((), (), s32[]{:S(2)}) async-start(), calls=%async_computation.43 | async-start | bytes 1966080 | tf_op jit(solution)/shard_map/all_gather | solution.py:58
  357.7 103.0 %reduce-scatter.38.cloned.1.call-start = ((), (), s32[]{:S(2)}) async-start(), calls=%async_computation.31 | async-start | bytes 1966080 | tf_op jit(solution)/shard_map/reduce_scatter | solution.py:71
  429.7 73.7 %reduce-scatter.32.cloned.1.call-start = ((), (), s32[]{:S(2)}) async-start(), calls=%async_computation.26 | async-start | bytes 1966080 | tf_op jit(solution)/shard_map/reduce_scatter | solution.py:62
  435.1 79.8 %all-gather.32.cloned.1.call-start = ((), (), s32[]{:S(2)}) async-start(), calls=%async_computation.32 | async-start | bytes 1966080 | tf_op jit(solution)/shard_map/all_gather | solution.py:58
  464.0 45.7 %copy-start.97 = (f32[256]{0:T(256)}, f32[256]{0:T(256)S(1)}, u32[]{:S(2)}) copy-start(f32[256]{0:T(256)S(1)} %negate_multiply_fusion.5) | copy-start | bytes 3076
  465.8 75.1 %all-gather.28.cloned.1.call-start = ((), (), s32[]{:S(2)}) async-start(), calls=%async_computation.27 | async-start | bytes 1966080 | tf_op jit(solution)/shard_map/all_gather | solution.py:54
  505.3 38.4 %copy-start.51 = (bf16[256,768]{1,0:T(8,128)(2,1)}, bf16[256,768]{1,0:T(8,128)(2,1)S(1)}, u32[]{:S(2)}) copy-start(bf16[256,768]{1,0:T(8,128)(2,1)S(1)} %get-tuple-element.263) | copy-start | bytes 1179652
  505.3 3.1 collective-permute-start.1
  509.8 134.5 %reduce-scatter.40.cloned.1.call-start = ((), (), s32[]{:S(2)}) async-start(), calls=%async_computation.33 | async-start | bytes 1966080 | tf_op jit(solution)/shard_map/reduce_scatter | solution.py:71
  613.3 64.7 %reduce-scatter.34.cloned.1.call-start = ((), (), s32[]{:S(2)}) async-start(), calls=%async_computation.28 | async-start | bytes 1966080 | tf_op jit(solution)/shard_map/reduce_scatter | solution.py:62
  629.4 83.9 %all-gather.30.cloned.1.call-start = ((), (), s32[]{:S(2)}) async-start(), calls=%async_computation.29 | async-start | bytes 1966080 | tf_op jit(solution)/shard_map/all_gather | solution.py:54
  682.3 64.5 %all-gather.34.cloned.1.call-start = ((), (), s32[]{:S(2)}) async-start(), calls=%async_computation.34 | async-start | bytes 1966080 | tf_op jit(solution)/shard_map/all_gather | solution.py:58
  684.9 3.6 collective-permute-start.2
  690.3 97.0 %reduce-scatter.42.cloned.1.call-start = ((), (), s32[]{:S(2)}) async-start(), calls=%async_computation.35 | async-start | bytes 1966080 | tf_op jit(solution)/shard_map/reduce_scatter | solution.py:71
  756.2 67.2 %all-gather.36.cloned.1.call-start = ((), (), s32[]{:S(2)}) async-start(), calls=%async_computation.36 | async-start | bytes 1966080 | tf_op jit(solution)/shard_map/all_gather | solution.py:58
  792.6 106.8 %reduce-scatter.44.cloned.1.call-start = ((), (), s32[]{:S(2)}) async-start(), calls=%async_computation.37 | async-start | bytes 1966080 | tf_op jit(solution)/shard_map/reduce_scatter | solution.py:71
  868.3 71.8 %all-gather.38.cloned.1.call-start = ((), (), s32[]{:S(2)}) async-start(), calls=%async_computation.38 | async-start | bytes 1966080 | tf_op jit(solution)/shard_map/all_gather | solution.py:58
  904.7 3.6 collective-permute-start.3
  908.3 76.2 %copy-start.34 = (bf16[256,768]{1,0:T(8,128)(2,1)}, bf16[256,768]{1,0:T(8,128)(2,1)S(1)}, u32[]{:S(2)}) copy-start(bf16[256,768]{1,0:T(8,128)(2,1)S(1)} %collective-permute-done.3) | copy-start | bytes 1179652
  909.2 72.6 %reduce-scatter.46.cloned.1.call-start = ((), (), s32[]{:S(2)}) async-start(), calls=%async_computation.39 | async-start | bytes 1966080 | tf_op jit(solution)/shard_map/reduce_scatter | solution.py:71
  950.8 76.9 %all-gather.40.cloned.1.call-start = ((), (), s32[]{:S(2)}) async-start(), calls=%async_computation.40 | async-start | bytes 1966080 | tf_op jit(solution)/shard_map/all_gather | solution.py:58
  985.5 98.5 %reduce-scatter.58.cloned.1.call-start = ((), (), s32[]{:S(2)}) async-start(), calls=%async_computation.47 | async-start | bytes 1474560
  1010.9 75.9 %reduce-scatter.50.cloned.1.call-start = ((), (), s32[]{:S(2)}) async-start(), calls=%async_computation.42 | async-start | bytes 1474560 | tf_op jit(solution)/shard_map/reduce_scatter | solution.py:329
  1027.7 64.9 %reduce-scatter.56.cloned.1.call-start = ((), (), s32[]{:S(2)}) async-start(), calls=%async_computation.46 | async-start | bytes 491520
  1063.1 56.1 %reduce-scatter.54.cloned.1.call-start = ((), (), s32[]{:S(2)}) async-start(), calls=%async_computation.45 | async-start | bytes 1228800
  1074.4 77.3 %reduce-scatter.48.cloned.1.call-start = ((), (), s32[]{:S(2)}) async-start(), calls=%async_computation.41 | async-start | bytes 1966080 | tf_op jit(solution)/shard_map/reduce_scatter | solution.py:71
  1078.7 106.9 %reduce-scatter.36.cloned.1.call-start = ((), (), s32[]{:S(2)}) async-start(), calls=%async_computation.30 | async-start | bytes 1966080 | tf_op jit(solution)/shard_map/reduce_scatter | solution.py:62
  1083.8 228.0 %reduce-scatter.52.cloned.1.call-start = ((), (), s32[]{:S(2)}) async-start(), calls=%async_computation.44 | async-start | bytes 417792
  1085.3 66.4 %copy-start.1 = (bf16[256,768]{1,0:T(8,128)(2,1)S(1)}, bf16[256,768]{1,0:T(8,128)(2,1)}, u32[]{:S(2)}) copy-start(bf16[256,768]{1,0:T(8,128)(2,1)} %copy-done) | copy-start | bytes 1179652
  1088.6 97.0 %copy-start.10 = (f32[256,768]{1,0:T(8,128)S(1)}, f32[256,768]{1,0:T(8,128)}, u32[]{:S(2)}) copy-start(f32[256,768]{1,0:T(8,128)} %copy-done.9) | copy-start | bytes 2359300
  1088.6 97.0 %copy-start.22 = (bf16[256,768]{1,0:T(8,128)(2,1)S(1)}, bf16[256,768]{1,0:T(8,128)(2,1)}, u32[]{:S(2)}) copy-start(bf16[256,768]{1,0:T(8,128)(2,1)} %reduce-scatter.34.cloned.1.call-done) | copy-start | bytes 1179652
  1088.6 97.0 %copy-start.35 = (bf16[256,768]{1,0:T(8,128)(2,1)S(1)}, bf16[256,768]{1,0:T(8,128)(2,1)}, u32[]{:S(2)}) copy-start(bf16[256,768]{1,0:T(8,128)(2,1)} %copy-done.34) | copy-start | bytes 1179652
  1088.6 97.0 %copy-start.101 = (f32[256]{0:T(256)S(1)}, f32[256]{0:T(256)}, u32[]{:S(2)}) copy-start(f32[256]{0:T(256)} %copy-done.100) | copy-start | bytes 3076
  (130 other events, 914.6 us)
Sparse Core Ops, SparseCore 0:
  33.7 32.7 all-gather.15
  121.8 31.4 reduce-scatter.25
  225.9 30.1 reduce-scatter.27
  355.9 30.9 all-gather.25
  389.2 30.9 all-gather.41
  465.9 32.6 all-gather.31
  509.9 30.9 all-gather.27
  682.4 30.9 all-gather.29
  715.8 30.9 all-gather.33
  756.4 30.8 reduce-scatter.41
  868.4 30.9 reduce-scatter.43
  985.7 30.9 all-gather.39
Sparse Core Ops, SparseCore 1:
  123.7 30.7 all-gather.19
  157.9 30.8 all-gather.17
  190.1 30.2 all-gather.21
  261.8 30.8 all-gather.23
  320.6 30.8 reduce-scatter.29
  429.8 30.8 reduce-scatter.37
  463.5 39.8 reduce-scatter.31
  613.3 30.8 reduce-scatter.39
  647.1 30.8 reduce-scatter.33
  792.7 30.8 all-gather.35
  909.2 30.8 all-gather.37
  950.9 30.8 reduce-scatter.45
  1011.0 29.2 reduce-scatter.57
  1042.6 27.8 reduce-scatter.49
  1073.3 19.2 reduce-scatter.55
  1095.0 24.2 reduce-scatter.53
  1122.2 29.4 reduce-scatter.47
  1154.7 30.8 reduce-scatter.35
  1190.2 121.6 reduce-scatter.51
where the time goes:
time: 1330 us; the launch traced here: 1320 us
  waiting for transfers between devices  765 us (58%)
  matrix products  313 us (24%)
  other arithmetic  98.1 us (7%)
  blocking collectives  62 us (5%)
  local copies, waits for them, and re-layouts  50 us (4%)
  between operations  22.6 us (2%)
    reduce_scatter x6, waiting for transfers between devices, summed_branch(): lax.psum_scatter(term_fn(jnp.int32(0), lax.axis_size('tensor') * local_ro...  191 us
    unnamed x35, waiting for transfers between devices  153 us
    reduce_scatter x6, waiting for transfers between devices, summed_grads(): lax.psum_scatter(term_fn(jnp.int32(0), lax.axis_size('tensor') * local_ro...  151 us
    all_gather x6, waiting for transfers between devices, gathered_rows(): return lax.all_gather(local_piece, 'tensor', axis=0, tiled=True)  136 us
    all_gather x6, waiting for transfers between devices, gathered_grads(): return lax.all_gather(local_piece, 'tensor', axis=0, tiled=True)  101 us
    sub x6, matrix products, attend_back(): direction * prob_grad - row_inner  63.3 us
    dot_general x6, matrix products, attend_back(): jnp.einsum('qhd,khd->hqk', query_block, key_rows[:row_end], preferred_ele...  48.3 us
    dot_general x12, matrix products, contract_cols(): lax.dot_general(left, right, (((1,), (1,)), ((), ())), preferred_element_...  41.8 us
  transfers between devices with their start and end apart: 35, of which 29 were waited for; matrix products, arithmetic and copies ran while one was open for 16% of the time, Pallas kernels for 0%

commit v1 on v0

v1 whole, which is shorter than its diff:
```python
import functools

import jax
import jax.numpy as jnp
from jax import lax
from jax.experimental import pallas as pl
from jax.experimental.pallas import tpu as pltpu
from jax.sharding import PartitionSpec as P

HEAD = 64
EPSILON = 1e-05
MASKED = -1e30
CHUNKS = 4
BF16 = jnp.bfloat16
F32 = jnp.float32
MESH = pl.DeviceIdType.MESH
TILE = 256


def nn(left, right):
    return lax.dot_general(left, right, (((1,), (0,)), ((), ())), preferred_element_type=F32)


def nt(left, right):
    return lax.dot_general(left, right, (((1,), (1,)), ((), ())), preferred_element_type=F32)


def tn(left, right):
    return lax.dot_general(left, right, (((0,), (0,)), ((), ())), preferred_element_type=F32)


def unit_rows(rows):
    centre = rows - jnp.mean(rows, axis=-1, keepdims=True)
    spread = jnp.mean(centre * centre, axis=-1, keepdims=True)
    scale = lax.rsqrt(spread + EPSILON)
    return centre * scale, scale


def norm_back(unit, scale, gain, grad):
    wide = grad * gain
    inner = jnp.mean(wide * unit, axis=-1, keepdims=True)
    return scale * (wide - jnp.mean(wide, axis=-1, keepdims=True) - unit * inner)


def gelu_parts(x):
    root = 0.7978845608028654
    square = x * x
    bend = jnp.tanh(root * x * (1.0 + 0.044715 * square))
    half = 0.5 + 0.5 * bend
    slope = half + 0.5 * x * (1.0 - bend * bend) * (root * (1.0 + 0.134145 * square))
    return x * half, slope


AG_NORM2 = (0, 1)
AG_MIDDLE = 2
AG_DA = (3, 4)
AG_DR = 5
RS_ATTN = (0, 1)
RS_MLP = (2, 3)
RS_DMLP = (4, 5)
RS_DATTN = (6, 7)


def block_kernel(
    inp,
    cot,
    w_in,
    gains,
    bias,
    acts,
    igr,
    grads,
    gain_out,
    W,
    X0,
    Y0,
    CT,
    DR,
    N1,
    N2,
    QKV,
    KT,
    VT,
    ATT,
    ATTT,
    LSE,
    PRE,
    HID,
    DPRE,
    DQKV,
    DA,
    DKV,
    DATH,
    DATT,
    DQT,
    MID,
    DMID,
    PART,
    RC,
    XS,
    RX,
    LAST,
    STG,
    w_sem,
    in_send,
    in_recv,
    ag_send,
    ag_recv,
    rs_send,
    rs_recv,
    out_send,
    out_recv,
    full_send,
    full_recv,
    stg_sem,
):
    s = lax.axis_index("section")
    t = lax.axis_index("tensor")
    z = lax.axis_index("dp")
    x = lax.rem(t, 2)
    y = lax.div(t, 2)
    rank = 2 * s + x
    t_x = 2 * y + 1 - x
    t_y = 2 * (1 - y) + x
    peer_c = (1 - s, t, z)
    peer_x = (s, t_x, z)
    rank_x = 2 * s + 1 - x
    chunk = X0.shape[0] // CHUNKS
    piece = chunk // 4
    half = CHUNKS // 2
    width = X0.shape[1]
    tiles = width // TILE
    heads = KT.shape[1]

    barrier = pltpu.get_barrier_semaphore()
    for other_s in range(2):
        for other in range(CHUNKS):

            @pl.when((s != other_s) | (t != other))
            def _():
                pl.semaphore_signal(
                    barrier, inc=1, device_id=(other_s, other, z), device_id_type=MESH
                )

    def remote(src, dst, send_sem, recv_sem, device):
        return pltpu.make_async_remote_copy(
            src_ref=src,
            dst_ref=dst,
            send_sem=send_sem,
            recv_sem=recv_sem,
            device_id=device,
            device_id_type=MESH,
        )

    def arrived(ref, sem):
        pltpu.make_async_copy(ref, ref, sem).wait()

    def rows_of(j):
        return pl.ds(pl.multiple_of(j * chunk, chunk), chunk)

    def piece_of(j, r):
        return pl.ds(pl.multiple_of(j * chunk + r * piece, piece), piece)

    def own_of(j):
        return pl.ds(pl.multiple_of(j * piece, piece), piece)

    def columns(n):
        return pl.ds(pl.multiple_of(n * TILE, TILE), TILE)

    weight_copies = [
        pltpu.make_async_copy(w_in.at[l], W.at[l], w_sem.at[l]) for l in range(2)
    ]
    for copy in weight_copies:
        copy.start()

    pl.semaphore_wait(barrier, 2 * CHUNKS - 1)

    def spread(source, target, which):
        pltpu.make_async_copy(
            source.at[y], target.at[rows_of(t)], in_recv.at[which, t]
        ).start()
        for other in range(CHUNKS):

            @pl.when(t != other)
            def _():
                remote(
                    source.at[other // 2],
                    target.at[rows_of(t)],
                    in_send.at[which, other],
                    in_recv.at[which, t],
                    (s, other, z),
                ).start()

    def spread_done(source, which):
        for other in range(CHUNKS):

            @pl.when(t != other)
            def _():
                arrived(source.at[other // 2], in_send.at[which, other])

    spread(inp, X0, 0)
    spread(cot, CT, 1)

    def gather_start(stage, ref, j):
        own = ref.at[piece_of(j, rank)]
        remote(own, own, ag_send.at[stage, 0, j], ag_recv.at[stage, 0, j], peer_x).start()
        remote(own, own, ag_send.at[stage, 1, j], ag_recv.at[stage, 1, j], peer_c).start()

    def gather_relay(stage, ref, j):
        theirs = ref.at[piece_of(j, rank_x)]
        arrived(theirs, ag_recv.at[stage, 0, j])
        remote(
            theirs, theirs, ag_send.at[stage, 2, j], ag_recv.at[stage, 2, j], peer_c
        ).start()

    def gather_wait(stage, ref, j):
        some = ref.at[piece_of(j, rank)]
        arrived(some, ag_recv.at[stage, 1, j])
        arrived(some, ag_recv.at[stage, 2, j])

    def sum_start(stage, b, j):
        half_rows = pl.ds(pl.multiple_of(j * chunk + (1 - s) * 2 * piece, 2 * piece), 2 * piece)
        remote(
            PART.at[b, half_rows],
            RC.at[b, j],
            rs_send.at[stage, 0, j],
            rs_recv.at[stage, 0, j],
            peer_c,
        ).start()

    def sum_pass(stage, b, j):
        arrived(RC.at[b, j], rs_recv.at[stage, 0, j])
        XS[b, j] = (
            PART[b, piece_of(j, rank_x), :].astype(F32)
            + RC[b, j, own_of(1 - x), :].astype(F32)
        ).astype(BF16)
        remote(
            XS.at[b, j], RX.at[b, j], rs_send.at[stage, 1, j], rs_recv.at[stage, 1, j], peer_x
        ).start()

    def sum_wait(stage, b, j):
        arrived(RX.at[b, j], rs_recv.at[stage, 1, j])
        total = (
            PART[b, piece_of(j, rank), :].astype(F32)
            + RC[b, j, own_of(x), :].astype(F32)
            + RX[b, j].astype(F32)
        )
        arrived(RC.at[b, j], rs_send.at[stage, 0, j])
        arrived(XS.at[b, j], rs_send.at[stage, 1, j])
        return total

    key_index = lax.broadcasted_iota(jnp.int32, (chunk, chunk), 0)
    query_index = lax.broadcasted_iota(jnp.int32, (chunk, chunk), 1)
    causal = key_index <= query_index

    def scores(l, st, i, j, diagonal):
        if l == 0:
            grown = st * st + 1.0
            inverse = lax.rsqrt(grown)
            magnitude = grown * inverse
            sign = st * inverse
        else:
            inverse, magnitude, sign = None, st, None
        if diagonal:
            magnitude = jnp.where(causal, magnitude, MASKED)
        else:
            apart = (j >= half) & (i < half)
            magnitude = magnitude + jnp.where(apart, bias[0:1, 0:chunk], 0.0)
        return inverse, magnitude, sign

    def attn_forward(l, j):
        rows = rows_of(j)
        source = X0 if l == 0 else Y0
        if l == 0:
            arrived(X0.at[rows], in_recv.at[0, j])
        else:
            gather_wait(AG_MIDDLE, Y0, j)

        @pl.loop(0, 4)
        def _(q):
            part = piece_of(j, q)
            unit, _ = unit_rows(source[part, :].astype(F32))
            N1[l, part, :] = (unit * gains[2 * l : 2 * l + 1, :]).astype(BF16)

        packed = nn(N1[l, rows, :], W[l, :, 0 : 3 * heads * HEAD]).astype(BF16)
        for h in range(heads):
            QKV[l, h, rows, :] = packed[:, h * HEAD : (h + 1) * HEAD] * jnp.asarray(
                HEAD**-0.5, BF16
            )
        for h in range(heads, 3 * heads):
            QKV[l, h, rows, :] = packed[:, h * HEAD : (h + 1) * HEAD]
        turned = packed[:, heads * HEAD :].astype(F32).T.astype(BF16)
        for h in range(heads):
            KT[l, h, :, rows] = turned[h * HEAD : (h + 1) * HEAD]
            VT[h, :, rows] = turned[(heads + h) * HEAD : (heads + h + 1) * HEAD]

        @pl.loop(0, heads)
        def _(h):
            query = QKV[l, h, rows, :]

            def block(i, carry, diagonal):
                top, total, out = carry
                keys = rows_of(i)
                st = nt(QKV[l, heads + h, keys, :], query)
                _, magnitude, sign = scores(l, st, i, j, diagonal)
                new_top = jnp.maximum(top, jnp.max(magnitude, axis=0, keepdims=True))
                weights = jnp.exp(magnitude - new_top)
                shrink = jnp.exp(top - new_top)
                total = total * shrink + jnp.sum(weights, axis=0, keepdims=True)
                signed = weights if l == 1 else sign * weights
                out = out * shrink + nn(VT[h, :, keys], signed.astype(BF16))
                return new_top, total, out

            carry = (
                jnp.full((1, chunk), MASKED, F32),
                jnp.zeros((1, chunk), F32),
                jnp.zeros((HEAD, chunk), F32),
            )
            carry = block(j, carry, True)
            top, total, out = lax.fori_loop(0, j, lambda i, c: block(i, c, False), carry)
            ATTT[l, h, :, rows] = out / total
            LSE[l, h, :, rows] = top + jnp.log(total)

        joined = jnp.concatenate(
            [jnp.zeros((HEAD, chunk), F32)] + [ATTT[l, h, :, rows] for h in range(heads)], axis=0
        )
        ATT[l, rows, :] = joined.T.astype(BF16)
        for n in range(tiles):
            PART[0, rows, n * TILE : (n + 1) * TILE] = nt(
                ATT[l, rows, :], W[l, n * TILE : (n + 1) * TILE, 512:768]
            ).astype(BF16)
        sum_start(RS_ATTN[l], 0, j)

    def attn_sum(l, j):
        total = sum_wait(RS_ATTN[l], 0, j)
        source = X0 if l == 0 else Y0
        own = piece_of(j, rank)
        middle = source[own, :].astype(F32) + total
        MID[l, own_of(j), :] = middle
        unit, _ = unit_rows(middle)
        N2[l, own, :] = (unit * gains[2 * l + 1 : 2 * l + 2, :]).astype(BF16)
        gather_start(AG_NORM2[l], N2.at[l], j)

    def mlp_forward(l, j):
        rows = rows_of(j)
        gather_wait(AG_NORM2[l], N2.at[l], j)
        for n in range(tiles):
            here = slice(n * TILE, (n + 1) * TILE)
            pre = nn(N2[l, rows, :], W[l, :, width + n * TILE : width + (n + 1) * TILE])
            PRE[l, rows, here] = pre.astype(BF16)
            HID[rows, here] = gelu_parts(pre)[0].astype(BF16)
        for n in range(tiles):
            here = slice(n * TILE, (n + 1) * TILE)
            PART[1, rows, here] = nt(HID[rows, :], W[l, here, 2 * width : 3 * width]).astype(BF16)
        sum_start(RS_MLP[l], 1, j)

    def last_out(which, j, section, out):
        LAST_rows = LAST.at[which, own_of(j)]
        target = out.at[y, pl.ds(pl.multiple_of(rank * piece, piece), piece)]

        @pl.when((s == section) & (t == j))
        def _():
            pltpu.make_async_copy(LAST_rows, target, out_recv.at[which, y, rank]).start()

        @pl.when((s != section) | (t != j))
        def _():
            remote(
                LAST_rows,
                target,
                out_send.at[which, j],
                out_recv.at[which, y, rank],
                (section, j, z),
            ).start()

    def last_out_done(which, section, out):
        for j in range(CHUNKS):

            @pl.when((s != section) | (t != j))
            def _():
                arrived(LAST.at[which, own_of(j)], out_send.at[which, j])

        @pl.when(s == section)
        def _():
            for m in range(2):
                for r in range(4):
                    arrived(
                        out.at[m, r * piece : (r + 1) * piece], out_recv.at[which, m, r]
                    )

    def full_out(which, section, ref, out):
        @pl.when(s == section)
        def _():
            pltpu.make_async_copy(
                ref.at[rows_of(t)], out.at[y], full_recv.at[which, y]
            ).start()
            remote(
                ref.at[rows_of(t_y)],
                out.at[y],
                full_send.at[which],
                full_recv.at[which, y],
                (s, t_y, z),
            ).start()

    def full_out_done(which, section, ref, out):
        @pl.when(s == section)
        def _():
            arrived(out.at[0], full_recv.at[which, 0])
            arrived(out.at[1], full_recv.at[which, 1])
            arrived(ref.at[rows_of(t_y)], full_send.at[which])

    def mlp_sum(l, j):
        result = MID[l, own_of(j), :] + sum_wait(RS_MLP[l], 1, j)
        if l == 0:
            Y0[piece_of(j, rank), :] = result.astype(BF16)
            gather_start(AG_MIDDLE, Y0, j)
        else:
            LAST[0, own_of(j), :] = result.astype(BF16)
            last_out(0, j, 1, acts)

    def mlp_backward(l, j):
        rows = rows_of(j)
        source = CT if l == 1 else DR
        if l == 1:
            arrived(CT.at[rows], in_recv.at[1, j])
        else:
            gather_wait(AG_DR, DR, j)
        for n in range(tiles):
            here = slice(n * TILE, (n + 1) * TILE)
            back = nn(source[rows, :], W[l, :, 2 * width + n * TILE : 2 * width + (n + 1) * TILE])
            hidden, slope = gelu_parts(PRE[l, rows, here].astype(F32))
            HID[rows, here] = hidden.astype(BF16)
            DPRE[rows, here] = (slope * back).astype(BF16)
        for n in range(tiles):
            here = slice(n * TILE, (n + 1) * TILE)
            PART[0, rows, here] = nt(DPRE[rows, :], W[l, here, width : 2 * width]).astype(BF16)
        sum_start(RS_DMLP[l], 0, j)

    def mlp_back_sum(l, j):
        total = sum_wait(RS_DMLP[l], 0, j)
        source = CT if l == 1 else DR
        own = piece_of(j, rank)
        unit, scale = unit_rows(MID[l, own_of(j), :])
        row = 2 * l + 1
        gain_out[row : row + 1, :] += jnp.sum(total * unit, axis=0, keepdims=True)
        grad = source[own, :].astype(F32) + norm_back(
            unit, scale, gains[row : row + 1, :], total
        )
        DMID[own_of(j), :] = grad
        DA[l, own, :] = grad.astype(BF16)
        gather_start(AG_DA[l], DA.at[l], j)

    def attn_backward(l, j):
        rows = rows_of(j)
        gather_wait(AG_DA[l], DA.at[l], j)

        @pl.when(j == CHUNKS - 1)
        def _():
            DKV[...] = jnp.zeros_like(DKV)

        back = nn(DA[l, rows, :], W[l, :, 512:768]).astype(BF16)
        turned = back.astype(F32).T.astype(BF16)
        for h in range(heads):
            DATH[h] = back[:, (h + 1) * HEAD : (h + 2) * HEAD]
            DATT[h] = turned[(h + 1) * HEAD : (h + 2) * HEAD]

        @pl.loop(0, heads)
        def _(h):
            query = QKV[l, h, rows, :]
            grad = DATH[h]
            grad_t = DATT[h]
            inner = jnp.sum(grad_t.astype(F32) * ATTT[l, h, :, rows], axis=0, keepdims=True)
            log_total = LSE[l, h, :, rows]

            def block(i, query_grad, diagonal):
                keys = rows_of(i)
                st = nt(QKV[l, heads + h, keys, :], query)
                dp = nn(QKV[l, 2 * heads + h, keys, :], grad_t)
                inverse, magnitude, sign = scores(l, st, i, j, diagonal)
                weights = jnp.exp(magnitude - log_total)
                if l == 0:
                    signed = sign * weights
                    ds = weights * (
                        sign * (sign * dp - inner) + dp * (inverse * inverse * inverse)
                    )
                else:
                    signed = weights
                    ds = weights * (dp - inner)
                ds = ds.astype(BF16)
                DKV[h, keys, :] += nn(ds, query)
                DKV[heads + h, keys, :] += nn(signed.astype(BF16), grad)
                return query_grad + nn(KT[l, h, :, keys], ds)

            query_grad = block(j, jnp.zeros((HEAD, chunk), F32), True)
            query_grad = lax.fori_loop(0, j, lambda i, c: block(i, c, False), query_grad)
            DQT[h] = query_grad * HEAD**-0.5

        turned = jnp.concatenate([DQT[h] for h in range(heads)], axis=0).T
        DQKV[rows, :] = jnp.concatenate(
            [turned] + [DKV[h, rows, :] for h in range(2 * heads)], axis=1
        ).astype(BF16)
        for n in range(tiles):
            here = slice(n * TILE, (n + 1) * TILE)
            PART[1, rows, here] = nt(
                DQKV[rows, :], W[l, here, 0 : 3 * heads * HEAD]
            ).astype(BF16)
        sum_start(RS_DATTN[l], 1, j)

    def attn_back_sum(l, j):
        total = sum_wait(RS_DATTN[l], 1, j)
        source = X0 if l == 0 else Y0
        own = piece_of(j, rank)
        unit, scale = unit_rows(source[own, :].astype(F32))
        row = 2 * l
        gain_out[row : row + 1, :] += jnp.sum(total * unit, axis=0, keepdims=True)
        result = DMID[own_of(j), :] + norm_back(unit, scale, gains[row : row + 1, :], total)
        if l == 1:
            DR[own, :] = result.astype(BF16)
            gather_start(AG_DR, DR, j)
        else:
            LAST[1, own_of(j), :] = result.astype(BF16)
            last_out(1, j, 0, igr)

    def weight_grad(l, group):
        @pl.loop(0, tiles)
        def _(n):
            slot = lax.rem(n, 2)
            target = grads.at[l, columns(n), group * width : (group + 1) * width]

            @pl.when(n >= 2)
            def _():
                arrived(STG.at[slot], stg_sem.at[slot])

            if group == 0:
                STG[slot, :, 0 : 3 * heads * HEAD] = tn(N1[l, :, columns(n)], DQKV[...]).astype(
                    BF16
                )
                out_part = tn(DA[l, :, columns(n)], ATT[l])
                STG[slot, :, 3 * heads * HEAD :] = out_part[:, HEAD:].astype(BF16)
            elif group == 1:
                STG[slot] = tn(N2[l, :, columns(n)], DPRE[...]).astype(BF16)
            else:
                source = CT if l == 1 else DR
                STG[slot] = tn(source[:, columns(n)], HID[...]).astype(BF16)
            pltpu.make_async_copy(STG.at[slot], target, stg_sem.at[slot]).start()

        arrived(STG.at[0], stg_sem.at[0])
        arrived(STG.at[1], stg_sem.at[1])

    def at(j, task, *args):
        @pl.when((j >= 0) & (j < CHUNKS))
        def _():
            task(*args, j)

    def back_at(j, task, *args):
        @pl.when((j >= 0) & (j < CHUNKS))
        def _():
            task(*args, CHUNKS - 1 - j)

    gain_out[...] = jnp.zeros_like(gain_out)
    weight_copies[0].wait()

    @pl.loop(0, 11)
    def _(k):
        for l in range(2):
            at(k - 4 * l - 1, lambda l, j: sum_pass(RS_ATTN[l], 0, j), l)
            at(k - 4 * l - 3, lambda l, j: sum_pass(RS_MLP[l], 1, j), l)
        at(k, attn_forward, 0)
        for l in range(2):
            at(k - 4 * l - 2, lambda l, j: gather_relay(AG_NORM2[l], N2.at[l], j), l)
        at(k - 4, lambda j: gather_relay(AG_MIDDLE, Y0, j))
        for l in range(2):
            at(k - 4 * l - 1, attn_sum, l)
        at(k - 2, mlp_forward, 0)
        for l in range(2):
            at(k - 4 * l - 3, mlp_sum, l)

        @pl.when(k == 4)
        def _():
            weight_copies[1].wait()

        at(k - 4, attn_forward, 1)
        at(k - 6, mlp_forward, 1)

        @pl.when(k == 8)
        def _():
            full_out(0, 0, Y0, acts)

    @pl.loop(0, 11)
    def _(k):
        for l in (1, 0):
            lag = 4 * (1 - l)
            back_at(k - lag - 1, lambda l, j: sum_pass(RS_DMLP[l], 0, j), l)
            back_at(k - lag - 3, lambda l, j: sum_pass(RS_DATTN[l], 1, j), l)
        back_at(k, mlp_backward, 1)
        for l in (1, 0):
            lag = 4 * (1 - l)
            back_at(k - lag - 2, lambda l, j: gather_relay(AG_DA[l], DA.at[l], j), l)
        back_at(k - 4, lambda j: gather_relay(AG_DR, DR, j))
        for l in (1, 0):
            back_at(k - 4 * (1 - l) - 1, mlp_back_sum, l)
        back_at(k - 2, attn_backward, 1)
        for l in (1, 0):
            back_at(k - 4 * (1 - l) - 3, attn_back_sum, l)

        @pl.when(k == 4)
        def _():
            weight_grad(1, 2)
            weight_grad(1, 1)

        back_at(k - 4, mlp_backward, 0)

        @pl.when(k == 6)
        def _():
            weight_grad(1, 0)

        back_at(k - 6, attn_backward, 0)

        @pl.when(k == 8)
        def _():
            full_out(1, 1, DR, igr)
            weight_grad(0, 2)
            weight_grad(0, 1)

    weight_grad(0, 0)

    spread_done(inp, 0)
    spread_done(cot, 1)

    @pl.loop(0, CHUNKS)
    def _(j):
        for stage in range(6):
            for kind in range(3):
                arrived(RX.at[0, 0], ag_send.at[stage, kind, j])

    full_out_done(0, 0, Y0, acts)
    full_out_done(1, 1, DR, igr)
    last_out_done(0, 1, acts)
    last_out_done(1, 0, igr)


def run_blocks(inputs, cotangent, weights, gains, bias):
    buckets, chunk, width = inputs.shape
    rows = CHUNKS * chunk
    piece = chunk // 4
    all_columns = weights.shape[2]
    heads = (all_columns - 2 * width) // (4 * HEAD)
    vmem, dma = pltpu.VMEM, pltpu.SemaphoreType.DMA
    scratch = [
        vmem(weights.shape, BF16),
        vmem((rows, width), BF16),
        vmem((rows, width), BF16),
        vmem((rows, width), BF16),
        vmem((rows, width), BF16),
        vmem((2, rows, width), BF16),
        vmem((2, rows, width), BF16),
        vmem((2, 3 * heads, rows, HEAD), BF16),
        vmem((2, heads, HEAD, rows), BF16),
        vmem((heads, HEAD, rows), BF16),
        vmem((2, rows, (heads + 1) * HEAD), BF16),
        vmem((2, heads, HEAD, rows), F32),
        vmem((2, heads, 1, rows), F32),
        vmem((2, rows, width), BF16),
        vmem((rows, width), BF16),
        vmem((rows, width), BF16),
        vmem((rows, 3 * heads * HEAD), BF16),
        vmem((2, rows, width), BF16),
        vmem((2 * heads, rows, HEAD), F32),
        vmem((heads, chunk, HEAD), BF16),
        vmem((heads, HEAD, chunk), BF16),
        vmem((heads, HEAD, chunk), F32),
        vmem((2, chunk, width), F32),
        vmem((chunk, width), F32),
        vmem((2, rows, width), BF16),
        vmem((2, CHUNKS, 2 * piece, width), BF16),
        vmem((2, CHUNKS, piece, width), BF16),
        vmem((2, CHUNKS, piece, width), BF16),
        vmem((2, chunk, width), BF16),
        vmem((2, TILE, width), BF16),
        dma((2,)),
        dma((2, CHUNKS)),
        dma((2, CHUNKS)),
        dma((6, 3, CHUNKS)),
        dma((6, 3, CHUNKS)),
        dma((8, 2, CHUNKS)),
        dma((8, 2, CHUNKS)),
        dma((2, CHUNKS)),
        dma((2, 2, 4)),
        dma((2,)),
        dma((2, 2)),
        dma((2,)),
    ]
    hbm = pl.BlockSpec(memory_space=pl.ANY)
    in_vmem = pl.BlockSpec(memory_space=pltpu.VMEM)
    return pl.pallas_call(
        block_kernel,
        out_shape=(
            jax.ShapeDtypeStruct(inputs.shape, BF16),
            jax.ShapeDtypeStruct(inputs.shape, BF16),
            jax.ShapeDtypeStruct(weights.shape, BF16),
            jax.ShapeDtypeStruct(gains.shape, F32),
        ),
        in_specs=[hbm, hbm, hbm, in_vmem, in_vmem],
        out_specs=(hbm, hbm, hbm, in_vmem),
        scratch_shapes=scratch,
        compiler_params=pltpu.CompilerParams(
            collective_id=0, has_side_effects=True, vmem_limit_bytes=60 << 20
        ),
        cost_estimate=pl.CostEstimate(
            flops=27_000_000_000, bytes_accessed=40_000_000, transcendentals=20_000_000
        ),
        name="blocks",
    )(inputs, cotangent, weights, gains, bias)


def shards(inputs, lengths, gains, w_qkv, w_out, w_up, w_down, cotangent):
    local_rows, width = inputs.shape[1:]
    y = lax.div(lax.axis_index("tensor"), 2)
    section = lax.axis_index("section")
    own = jnp.concatenate(
        [w_qkv[0].reshape(w_qkv.shape[1], -1), w_out[0].T, w_up[0], w_down[0].T], axis=1
    )
    whole = lax.all_gather(own, "dp", axis=0, tiled=True)
    axes = ("section", "tensor")
    weights = []
    for l in range(2):
        parts = []
        for to_y in range(2):
            pairs = [(4 * l + 2 * c + x, 4 * c + 2 * to_y + x) for c in range(2) for x in range(2)]
            parts.append(lax.ppermute(whole, axes, pairs))
        weights.append(jnp.where(y == 0, parts[0], parts[1]))
    weights = jnp.stack(weights)
    gain_rows = lax.all_gather(gains, "dp", axis=2, tiled=True)
    gain_rows = lax.all_gather(gain_rows, "section", axis=0, tiled=True)
    gain_rows = gain_rows.reshape(4, width).astype(F32)
    gain_rows = jnp.concatenate([gain_rows, jnp.zeros_like(gain_rows)], axis=0)
    first_len = lengths[y]
    bias = jnp.where(first_len == CHUNKS * local_rows, 0.0, MASKED).astype(F32)
    bias = jnp.broadcast_to(bias, (8, local_rows))

    acts, input_grads, partial, gain_part = run_blocks(
        inputs, cotangent, weights, gain_rows, bias
    )

    total = jnp.zeros(partial.shape[1:], F32)
    for l in range(2):
        for from_y in range(2):
            pairs = [
                (4 * c + 2 * from_y + x, 4 * l + 2 * c + x) for c in range(2) for x in range(2)
            ]
            total = total + lax.ppermute(partial[l], axes, pairs).astype(F32)
    total = lax.psum_scatter(total.astype(BF16), "dp", scatter_dimension=0, tiled=True)
    total = total.astype(F32)
    columns = 3 * w_qkv.shape[3]
    out_columns = w_out.shape[1]
    qkv_grads = total[:, :columns].reshape(w_qkv.shape)
    out_grads = total[:, columns : columns + out_columns].T[None]
    columns += out_columns
    up_grads = total[:, columns : columns + w_up.shape[2]][None]
    down_grads = total[:, columns + w_up.shape[2] :].T[None]
    gain_part = lax.psum(gain_part[:4].reshape(2, 2, width), "section")
    gain_part = lax.dynamic_slice_in_dim(gain_part, section, 1, 0)
    gain_grads = lax.psum_scatter(
        gain_part, ("tensor", "dp"), scatter_dimension=2, tiled=True
    )
    return (
        acts[None],
        input_grads[None],
        gain_grads,
        qkv_grads,
        out_grads,
        up_grads,
        down_grads,
    )


def solution(mesh):
    in_specs = (
        P("dp", "tensor", None),
        P("dp"),
        P("section", None, "dp"),
        P("section", "dp", None, "tensor"),
        P("section", "tensor", "dp"),
        P("section", "dp", "tensor"),
        P("section", "tensor", "dp"),
        P("dp", "tensor", None),
    )
    out_specs = (
        P("section", "dp", "tensor", None),
        P("section", "dp", "tensor", None),
        P("section", None, ("tensor", "dp")),
        P("section", "dp", None, "tensor"),
        P("section", "tensor", "dp"),
        P("section", "dp", "tensor"),
        P("section", "tensor", "dp"),
    )
    return jax.shard_map(shards, mesh=mesh, in_specs=in_specs, out_specs=out_specs, check_vma=False)
```

time: 1330 us -> 702 us (0.53)
  waiting for transfers between devices: 765 us -> 270 us
  matrix products: 313 us -> 0 us
  Pallas kernels: 0 us -> 280 us
  other arithmetic: 98.1 us -> 19 us
  starting transfers between devices: 9.86 us -> 70.4 us
  blocking collectives: 62 us -> 20.9 us
  local copies, waits for them, and re-layouts: 50 us -> 23.6 us
    pallas_call x0 -> x1, Pallas kernels: none -> 280 us  [run_blocks(): pl.pallas_call(block_kernel, out_shape=(jax.ShapeDtypeStruct(inputs.shape...]
    reduce_scatter x13 -> x1, waiting for transfers between devices: 342 us -> 66.5 us  [shards(): lax.psum_scatter(total.astype(BF16), 'dp', scatter_dimension=0, tiled=True)]
    dot_general x72 -> x0, matrix products: 250 us -> none  [the longest x6 48.3 us: attend_back(): jnp.einsum('qhd,khd->hqk', query_block, key_rows[:row_end], preferred_ele...]
    all_gather x14 -> x1, waiting for transfers between devices: 263 us -> 72.8 us  [shards(): whole = lax.all_gather(own, 'dp', axis=0, tiled=True)]
    ppermute x4 -> x8, starting transfers between devices: 6.11 us -> 70.1 us  [the longest x4 35.4 us: shards(): parts.append(lax.ppermute(whole, axes, pairs))]
    sub x6 -> x0, matrix products: 63.3 us -> none  [attend_back(): direction * prob_grad - row_inner]
    reduce_sum x32 -> x0, other arithmetic: 50.4 us -> none  [the longest x6 20.7 us: attend(): weight_sum = jnp.sum(weights, axis=-1, keepdims=True)]
    all_gather x3 -> x2, blocking collectives: 62 us -> 17 us  [the longest x1 15.2 us: shards(): gain_rows = lax.all_gather(gains, 'dp', axis=2, tiled=True)]
  transfers between devices with their start and end apart: 35 -> 11, of which waited for: 29 -> 5; matrix products, arithmetic and copies ran while one was open for 16% -> 3% of each run, Pallas kernels for 0% -> 0%
where the time goes in v1:
time: 702 us; the launch traced here: 698 us
  Pallas kernels  280 us (40%)
  waiting for transfers between devices  270 us (38%)
  starting transfers between devices  70.4 us (10%)
  local copies, waits for them, and re-layouts  23.6 us (3%)
  blocking collectives  20.9 us (3%)
  other arithmetic  19 us (3%)
  between operations  14.5 us (2%)
    pallas_call x1, Pallas kernels, run_blocks(): pl.pallas_call(block_kernel, out_shape=(jax.ShapeDtypeStruct(inputs.shape...  280 us
    unnamed x4, waiting for transfers between devices  108 us
    all_gather x1, waiting for transfers between devices, shards(): whole = lax.all_gather(own, 'dp', axis=0, tiled=True)  72.8 us
    reduce_scatter x1, waiting for transfers between devices, shards(): lax.psum_scatter(total.astype(BF16), 'dp', scatter_dimension=0, tiled=True)  66.5 us
    ppermute x4, starting transfers between devices, shards(): parts.append(lax.ppermute(whole, axes, pairs))  35.4 us
    ppermute x4, starting transfers between devices, shards(): total = total + lax.ppermute(partial[l], axes, pairs).astype(F32)  34.7 us
    ppermute x4, waiting for transfers between devices, shards(): parts.append(lax.ppermute(whole, axes, pairs))  20.8 us
    all_gather x1, blocking collectives, shards(): gain_rows = lax.all_gather(gains, 'dp', axis=2, tiled=True)  15.2 us
  transfers between devices with their start and end apart: 11, of which 5 were waited for; matrix products, arithmetic and copies ran while one was open for 3% of the time, Pallas kernels for 0%

profile of v1, /device:TPU:0, one launch (start us, length us, event | category | flops | bytes accessed | tf_op | source)
XLA Modules:
  0.0 697.6 jit_solution(11159473233953923054)
XLA Ops:
  7.2 0.0 all-gather.2.cloned.1.call-start
  7.2 1.0 copy.26
  8.2 1.1 copy.25
  9.4 0.2 copy.27
  9.5 2.0 concatenate.8
  11.5 0.0 all-gather.2.cloned.1.call-update
  11.6 0.0 reduce-scatter.7.cloned.1.call-start
  11.6 72.8 %all-gather.2.cloned.1.call-done = bf16[768,2304]{1,0:T(8,128)(2,1)} async-done(((bf16[192,2304]{1,0:T(8,128)(2,1)}), bf16[768,2304]{1,0:T(8,128)(2,1)}) %all-gather.2.cloned.1.call-update) | async-done | bytes 3538960 | tf_op jit(solution)/shard_map/all_gather | solution.py:722
  84.4 2.5 collective-permute-start.3
  86.9 1.3 collective-permute-start.2
  88.2 3.6 collective-permute-start.1
  91.8 28.0 %collective-permute-start = (bf16[768,2304]{1,0:T(8,128)(2,1)}, bf16[768,2304]{1,0:T(8,128)(2,1)}, u32[]{:S(2)}, u32[]{:S(2)}) collective-permute-start(bf16[768,2304]{1,0:T(8,128)(2,1)} %all-gather.2.cloned.1.call-done), channel_id=1, source_target_pairs={{0,0},{4,4},{8,16},{12,20},{1,1},{5,5},{9,17},{13,21},{2,2},{6,6},... | collective-permute-start | bytes 10616840 | tf_op jit(solution)/shard_map/ppermute | solution.py:729
  119.8 0.8 copy.28
  120.6 15.2 %all_gather.10 = bf16[1,2,768]{1,0,2:T(2,128)(2,1)} all-gather(bf16[1,2,192]{1,0,2:T(2,128)(2,1)} %copy.28), channel_id=1, replica_groups=mesh['section'=2,'tensor'=4,'dp'=4] {'dp'}, dimensions={2}, use_global_device_ids=true | all-gather | bytes 3840 | tf_op jit(solution)/shard_map/all_gather | solution.py:732
  135.8 1.2 copy.29
  136.9 1.8 all_gather.11
  138.8 1.2 dynamic_slice.6
  140.7 0.6 pad_convert_fusion.gains
  141.3 2.4 select_bitcast_fusion
  143.6 20.8 %collective-permute-done.1 = bf16[768,2304]{1,0:T(8,128)(2,1)S(1)} collective-permute-done((bf16[768,2304]{1,0:T(8,128)(2,1)}, bf16[768,2304]{1,0:T(8,128)(2,1)S(1)}, u32[]{:S(2)}, u32[]{:S(2)}) %collective-permute-start.1) | collective-permute-done | bytes 3538976 | tf_op jit(solution)/shard_map/ppermute | solution.py:729
  164.4 2.4 select_bitcast_fusion.1
  166.8 3.5 pad_maximum_fusion.w_in
  170.3 0.6 broadcast_in_dim.19.bias
  170.9 279.6 %blocks.1 = (bf16[2,256,768]{2,1,0:T(8,128)(2,1)}, bf16[2,256,768]{2,1,0:T(8,128)(2,1)}, bf16[2,768,2304]{2,1,0:T(8,128)(2,1)}, f32[8,768]{1,0:T(8,128)}) custom-call(bf16[2,256,768]{2,1,0:T(8,128)(2,1)} %inp.1, bf16[2,256,768]{2,1,0:T(8,128)(2,1)} %cot.1, bf16[2,768,2304]{2,1,0:T(8,128)(2,1)} %pad_maximum_fusion.w_in, f32[8,768]{1,0:T(8,128)} %pad_convert_fusion.gains, ...), custom_call_target="tpu_custom_call" | custom-call | flops 27000000512 | bytes 40000000 | tf_op jit(solution)/shard_map/blocks/pallas_call | solution.py:694
  450.5 5.4 slice_bitcast_fusion.1
  455.9 1.3 collective-permute-start.5
  457.2 28.0 %collective-permute-start.4 = (bf16[768,2304]{1,0:T(8,128)(2,1)}, bf16[768,2304]{1,0:T(8,128)(2,1)}, u32[]{:S(2)}, u32[]{:S(2)}) collective-permute-start(bf16[768,2304]{1,0:T(8,128)(2,1)} %get-tuple-element.36), channel_id=1, source_target_pairs={{0,0},{4,4},{16,8},{20,12},{1,1},{5,5},{17,9},{21,13},{2,2},{6,6},... | collective-permute-start | bytes 10616840 | tf_op jit(solution)/shard_map/ppermute | solution.py:750
  485.2 2.4 collective-permute-start.7
  487.6 3.1 collective-permute-start.6
  490.7 0.7 slice.23
  491.4 0.6 reshape.28
  492.0 4.0 psum.7
  496.0 0.6 constant_dynamic-slice_fusion
  496.6 1.7 copy.33
  498.3 0.3 reduce-scatter.5.cloned.1.call-start
  498.5 1.1 collective-permute-done.5
  499.6 8.7 %add_convert_fusion = bf16[768,2304]{1,0:T(8,128)(2,1)} fusion(bf16[768,2304]{1,0:T(8,128)(2,1)} %collective-permute-done.7, bf16[768,2304]{1,0:T(8,128)(2,1)} %collective-permute-done.6, bf16[768,2304]{1,0:T(8,128)(2,1)} %collective-permute-done.5, bf16[768,2304]{1,0:T(8,128)(2,1)} %collective-permute-done.4), kind=kLoop, calls=%fused_computation.1 | loop fusion | flops 14155776 | bytes 17694720 | tf_op jit(solution)/shard_map/convert_element_type | solution.py:751
  508.4 108.3 %reduce-scatter.7.cloned.1.call-done = f32[48,2]{1,0:T(8,128)} async-done(((f32[768,2]{1,0:T(8,128)}), f32[48,2]{1,0:T(8,128)}) %reduce-scatter.7.cloned.1.call-update) | async-done | bytes 400
  616.7 1.4 copy.34
  618.0 66.5 %reduce-scatter.5.cloned.1.call-done = bf16[192,2304]{1,0:T(8,128)(2,1)} async-done(((bf16[768,2304]{1,0:T(8,128)(2,1)}), bf16[192,2304]{1,0:T(8,128)(2,1)}) %reduce-scatter.5.cloned.1.call-update) | async-done | bytes 884752 | tf_op jit(solution)/shard_map/reduce_scatter | solution.py:751
  684.6 1.4 convert_element_type.28
  685.9 0.1 slice_bitcast_fusion.4
  686.1 1.1 slice_bitcast_fusion.2
  687.2 0.2 copy.30
  687.4 1.1 copy.31
  688.5 0.8 copy.32
  689.3 0.9 copy.37
  690.2 0.9 copy.38
  (18 shorter events, 0.1 us)
Async XLA Ops:
  7.2 112.6 %copy-start.3 = (bf16[1,2,192]{2,1,0:T(2,128)(2,1)S(1)}, bf16[1,2,192]{2,1,0:T(2,128)(2,1)}, u32[]{:S(2)}) copy-start(bf16[1,2,192]{2,1,0:T(2,128)(2,1)} %param.10) | copy-start | bytes 2308
  7.2 77.2 %all-gather.2.cloned.1.call-start = ((), (), s32[]{:S(2)}) async-start(), calls=%async_computation.2 | async-start | bytes 4423680 | tf_op jit(solution)/shard_map/all_gather | solution.py:722
  11.6 605.1 %reduce-scatter.7.cloned.1.call-start = ((), (), s32[]{:S(2)}) async-start(), calls=%async_computation.4 | async-start | bytes 417792
  84.4 56.9 %collective-permute-start.3 = (bf16[768,2304]{1,0:T(8,128)(2,1)}, bf16[768,2304]{1,0:T(8,128)(2,1)}, u32[]{:S(2)}, u32[]{:S(2)}) collective-permute-start(bf16[768,2304]{1,0:T(8,128)(2,1)} %all-gather.2.cloned.1.call-done), channel_id=1, source_target_pairs={{16,8},{20,12},{24,24},{28,28},{17,9},{21,13},{25,25},{29,29},{18,... | collective-permute-start | bytes 10616840 | tf_op jit(solution)/shard_map/ppermute | solution.py:729
  86.9 54.3 %collective-permute-start.2 = (bf16[768,2304]{1,0:T(8,128)(2,1)}, bf16[768,2304]{1,0:T(8,128)(2,1)}, u32[]{:S(2)}, u32[]{:S(2)}) collective-permute-start(bf16[768,2304]{1,0:T(8,128)(2,1)} %all-gather.2.cloned.1.call-done), channel_id=1, source_target_pairs={{16,0},{20,4},{24,16},{28,20},{17,1},{21,5},{25,17},{29,21},{18,2}... | collective-permute-start | bytes 10616840 | tf_op jit(solution)/shard_map/ppermute | solution.py:729
  88.2 76.2 %collective-permute-start.1 = (bf16[768,2304]{1,0:T(8,128)(2,1)}, bf16[768,2304]{1,0:T(8,128)(2,1)S(1)}, u32[]{:S(2)}, u32[]{:S(2)}) collective-permute-start(bf16[768,2304]{1,0:T(8,128)(2,1)} %all-gather.2.cloned.1.call-done), channel_id=1, source_target_pairs={{0,8},{4,12},{8,24},{12,28},{1,9},{5,13},{9,25},{13,29},{2,10},{6,... | collective-permute-start | bytes 10616840 | tf_op jit(solution)/shard_map/ppermute | solution.py:729
  91.8 72.6 %collective-permute-start = (bf16[768,2304]{1,0:T(8,128)(2,1)}, bf16[768,2304]{1,0:T(8,128)(2,1)}, u32[]{:S(2)}, u32[]{:S(2)}) collective-permute-start(bf16[768,2304]{1,0:T(8,128)(2,1)} %all-gather.2.cloned.1.call-done), channel_id=1, source_target_pairs={{0,0},{4,4},{8,16},{12,20},{1,1},{5,5},{9,17},{13,21},{2,2},{6,6},... | collective-permute-start | bytes 10616840 | tf_op jit(solution)/shard_map/ppermute | solution.py:729
  455.9 43.7 %collective-permute-start.5 = (bf16[768,2304]{1,0:T(8,128)(2,1)}, bf16[768,2304]{1,0:T(8,128)(2,1)}, u32[]{:S(2)}, u32[]{:S(2)}) collective-permute-start(bf16[768,2304]{1,0:T(8,128)(2,1)} %get-tuple-element.36), channel_id=1, source_target_pairs={{8,0},{12,4},{24,8},{28,12},{9,1},{13,5},{25,9},{29,13},{10,2},{14... | collective-permute-start | bytes 10616840 | tf_op jit(solution)/shard_map/ppermute | solution.py:750
  457.2 42.4 %collective-permute-start.4 = (bf16[768,2304]{1,0:T(8,128)(2,1)}, bf16[768,2304]{1,0:T(8,128)(2,1)}, u32[]{:S(2)}, u32[]{:S(2)}) collective-permute-start(bf16[768,2304]{1,0:T(8,128)(2,1)} %get-tuple-element.36), channel_id=1, source_target_pairs={{0,0},{4,4},{16,8},{20,12},{1,1},{5,5},{17,9},{21,13},{2,2},{6,6},... | collective-permute-start | bytes 10616840 | tf_op jit(solution)/shard_map/ppermute | solution.py:750
  485.2 14.4 %collective-permute-start.7 = (bf16[768,2304]{1,0:T(8,128)(2,1)S(1)}, bf16[768,2304]{1,0:T(8,128)(2,1)}, u32[]{:S(2)}, u32[]{:S(2)}) collective-permute-start(bf16[768,2304]{1,0:T(8,128)(2,1)S(1)} %get-tuple-element.37), channel_id=1, source_target_pairs={{8,16},{12,20},{24,24},{28,28},{9,17},{13,21},{25,25},{29,29},{10,... | collective-permute-start | bytes 10616840 | tf_op jit(solution)/shard_map/ppermute | solution.py:750
  487.6 12.0 %collective-permute-start.6 = (bf16[768,2304]{1,0:T(8,128)(2,1)S(1)}, bf16[768,2304]{1,0:T(8,128)(2,1)}, u32[]{:S(2)}, u32[]{:S(2)}) collective-permute-start(bf16[768,2304]{1,0:T(8,128)(2,1)S(1)} %get-tuple-element.37), channel_id=1, source_target_pairs={{0,16},{4,20},{16,24},{20,28},{1,17},{5,21},{17,25},{21,29},{2,18}... | collective-permute-start | bytes 10616840 | tf_op jit(solution)/shard_map/ppermute | solution.py:750
  498.3 186.3 %reduce-scatter.5.cloned.1.call-start = ((), (), s32[]{:S(2)}) async-start(), calls=%async_computation.3 | async-start | bytes 4423680 | tf_op jit(solution)/shard_map/reduce_scatter | solution.py:751
  684.6 2.6 copy-start
  685.9 3.3 copy-start.2
  686.0 4.1 copy-start.1
Sparse Core Ops, SparseCore 0:
  11.7 72.6 all-gather.1
  498.4 118.2 reduce-scatter.6
  619.1 65.4 reduce-scatter.4

commit v2 on v0

v2 whole, which is shorter than its diff:
```python
import functools

import jax
import jax.numpy as jnp
from jax import lax
from jax.experimental import pallas as pl
from jax.experimental.pallas import tpu as pltpu
from jax.sharding import PartitionSpec as P

HEAD = 64
EPSILON = 1e-05
MASKED = -1e30
CHUNKS = 4
PARTS = 3
VMEM_LIMIT = 63 << 20
TILE = 256
BF16 = jnp.bfloat16
F32 = jnp.float32
MESH = pl.DeviceIdType.MESH

SUM_ATTN = (0, 2)
SUM_MLP = (1, 3)
SUM_DMLP = (6, 4)
SUM_DATTN = (7, 5)
PAIR_N2 = (0, 1)
PAIR_MIDDLE = 2
PAIR_DA = (4, 3)
PAIR_DR = 5


def nn(left, right):
    return lax.dot_general(left, right, (((1,), (0,)), ((), ())), preferred_element_type=F32)


def nt(left, right):
    return lax.dot_general(left, right, (((1,), (1,)), ((), ())), preferred_element_type=F32)


def tn(left, right):
    return lax.dot_general(left, right, (((0,), (0,)), ((), ())), preferred_element_type=F32)


def unit_rows(rows):
    centre = rows - jnp.mean(rows, axis=-1, keepdims=True)
    spread = jnp.mean(centre * centre, axis=-1, keepdims=True)
    scale = lax.rsqrt(spread + EPSILON)
    return centre * scale, scale


def norm_back(unit, scale, gain, grad):
    wide = grad * gain
    inner = jnp.mean(wide * unit, axis=-1, keepdims=True)
    return scale * (wide - jnp.mean(wide, axis=-1, keepdims=True) - unit * inner)


def gelu_parts(x):
    root = 0.7978845608028654
    square = x * x
    bend = jnp.tanh(root * x * (1.0 + 0.044715 * square))
    half = 0.5 + 0.5 * bend
    slope = half + 0.5 * x * (1.0 - bend * bend) * (root * (1.0 + 0.134145 * square))
    return x * half, slope


class Names:
    pass


def block_kernel(inside, steps, names, *refs):
    n = Names()
    for name, ref in zip(names, refs, strict=True):
        setattr(n, name, ref)
    s = lax.axis_index("section")
    t = lax.axis_index("tensor")
    z = lax.axis_index("dp")
    x = lax.rem(t, 2)
    y = lax.div(t, 2)
    t_y = 2 * (1 - y) + x
    mate = (1 - s, t, z)
    peer_x = (s, 2 * y + 1 - x, z)
    peer_y = (s, t_y, z)
    hub = s == y
    rows_all, width = n.X0.shape
    chunk = rows_all // CHUNKS
    part = chunk // 2
    half = CHUNKS // 2
    heads = n.KT.shape[1]
    tiles = width // TILE
    depth = lax.axis_size("dp")
    slab = width // depth
    q_columns = 2 * heads * HEAD
    o_columns = 3 * heads * HEAD

    def remote(src, dst, send_sem, recv_sem, device):
        return pltpu.make_async_remote_copy(
            src_ref=src,
            dst_ref=dst,
            send_sem=send_sem,
            recv_sem=recv_sem,
            device_id=device,
            device_id_type=MESH,
        )

    def done(ref, sem):
        pltpu.make_async_copy(ref, ref, sem).wait()

    def rows_of(j):
        return pl.ds(pl.multiple_of(j * chunk, chunk), chunk)

    def half_of(j, c):
        return pl.ds(pl.multiple_of(j * chunk + c * part, part), part)

    def own_of(j):
        return pl.ds(pl.multiple_of(j * part, part), part)

    def slab_of(i):
        return pl.ds(pl.multiple_of(i * slab, slab), slab)

    def bytes_of(count):
        return n.PART.at[0, 0:count]

    barrier = pltpu.get_barrier_semaphore()
    greeted = 0
    for other_s in range(2):
        for other in range(CHUNKS):
            greeted += 1

            @pl.when((s != other_s) | (t != other))
            def _():
                pl.semaphore_signal(
                    barrier, inc=1, device_id=(other_s, other, z), device_id_type=MESH
                )

        if inside:
            for other in range(depth):
                greeted += 1

                @pl.when(z != other)
                def _():
                    pl.semaphore_signal(
                        barrier, inc=1, device_id=(other_s, t, other), device_id_type=MESH
                    )

    pl.semaphore_wait(barrier, greeted - 1 - (2 if inside else 0))

    def weights_send(l, p):
        if not inside:
            pltpu.make_async_copy(n.w_whole.at[l, p], n.W.at[l, p], n.w_recv.at[l, p, 0]).start()
            return
        own = (n.own_a, n.own_b, n.own_c)[p]

        @pl.when(s == l)
        def _():
            for far in range(depth):
                @pl.when(hub & (z == far))
                def _():
                    pltpu.make_async_copy(
                        own, n.W.at[l, p, slab_of(z)], n.w_recv.at[l, p, z]
                    ).start()

                @pl.when(jnp.logical_not(hub & (z == far)))
                def _():
                    remote(
                        own,
                        n.W.at[l, p, slab_of(z)],
                        n.w_send.at[p, far],
                        n.w_recv.at[l, p, z],
                        (y, t, far),
                    ).start()

    def weights_sent(p):
        own = (n.own_a, n.own_b, n.own_c)[p]
        for far in range(depth):

            @pl.when(jnp.logical_not(hub & (z == far)))
            def _():
                done(own, n.w_send.at[p, far])

    def weights_relay(l, p):
        if not inside:
            return

        @pl.when(hub)
        def _():
            for step in range(depth):
                far = lax.rem(z + step, depth)
                here = n.W.at[l, p, slab_of(far)]
                done(here, n.w_recv.at[l, p, far])
                remote(
                    here, here, n.relay_send.at[l, p, far], n.w_recv.at[l, p, far], peer_y
                ).start()

    def weights_wait(l, p):
        if not inside:
            done(n.W.at[l, p], n.w_recv.at[l, p, 0])
            return

        @pl.when(jnp.logical_not(hub))
        def _():
            for far in range(depth):
                done(n.W.at[l, p, slab_of(far)], n.w_recv.at[l, p, far])

    def spread(which, source, target):
        pltpu.make_async_copy(
            source.at[y], target.at[rows_of(t)], n.in_recv.at[which, t]
        ).start()
        for other in range(CHUNKS):

            @pl.when(t != other)
            def _():
                remote(
                    source.at[other // 2, half_of(0, s)],
                    target.at[half_of(t, s)],
                    n.in_send.at[which, other],
                    n.in_recv.at[which, t],
                    (s, other, z),
                ).start()

    def spread_pass(which, target, j):
        @pl.when(j == t)
        def _():
            done(target.at[rows_of(j)], n.in_recv.at[which, j])

        @pl.when(j != t)
        def _():
            here = target.at[half_of(j, s)]
            done(here, n.in_recv.at[which, j])
            remote(
                here, here, n.mate_send.at[which, j], n.mate_recv.at[which, j], mate
            ).start()

    def spread_wait(which, target, j):
        @pl.when(j != t)
        def _():
            done(target.at[half_of(j, s)], n.mate_recv.at[which, j])

    def spread_done(which):
        for other in range(CHUNKS):

            @pl.when(t != other)
            def _():
                done(bytes_of(part), n.in_send.at[which, other])
                done(bytes_of(part), n.mate_send.at[which, other])

    def pair_start(stage, ref, j):
        here = ref.at[half_of(j, s)]
        remote(here, here, n.pair_send.at[stage, j], n.pair_recv.at[stage, j], mate).start()

    def pair_wait(stage, j):
        done(bytes_of(part), n.pair_recv.at[stage, j])

    def sum_start(stage, j):
        b = stage % 2
        remote(
            n.PART.at[b, half_of(j, 1 - s)],
            n.RC.at[b, j],
            n.rs_send.at[stage, 0, j],
            n.rs_recv.at[stage, 0, j],
            mate,
        ).start()

    def sum_pass(stage, j):
        b = lax.rem(stage, 2)
        here = half_of(j, s)
        done(n.RC.at[b, j], n.rs_recv.at[stage, 0, j])
        n.PART[b, here, :] = (
            n.PART[b, here, :].astype(F32) + n.RC[b, j].astype(F32)
        ).astype(BF16)
        remote(
            n.PART.at[b, here],
            n.RX.at[b, j],
            n.rs_send.at[stage, 1, j],
            n.rs_recv.at[stage, 1, j],
            peer_x,
        ).start()
        done(n.RC.at[b, j], n.rs_send.at[stage, 0, j])

    def sum_wait(stage, j):
        b = stage % 2
        done(n.RX.at[b, j], n.rs_recv.at[stage, 1, j])
        total = n.PART[b, half_of(j, s), :].astype(F32) + n.RX[b, j].astype(F32)
        done(n.RX.at[b, j], n.rs_send.at[stage, 1, j])
        return total

    key_index = lax.broadcasted_iota(jnp.int32, (chunk, chunk), 0)
    query_index = lax.broadcasted_iota(jnp.int32, (chunk, chunk), 1)
    causal = key_index <= query_index

    def scores(l, st, i, j, diagonal):
        if l == 0:
            grown = st * st + 1.0
            inverse = lax.rsqrt(grown)
            magnitude = grown * inverse
            sign = st * inverse
        else:
            inverse, magnitude, sign = None, st, None
        if diagonal:
            magnitude = jnp.where(causal, magnitude, MASKED)
        else:
            apart = (j >= half) & (i < half)
            magnitude = magnitude + jnp.where(apart, n.bias[0:1, 0:chunk], 0.0)
        return inverse, magnitude, sign

    def norm_qkv(l, j):
        rows = rows_of(j)
        if l == 0:
            spread_wait(0, n.X0, j)
        else:
            pair_wait(PAIR_MIDDLE, j)
        source = n.X0 if l == 0 else n.Y0

        @pl.loop(0, 4)
        def _(i):
            some = pl.ds(pl.multiple_of(j * chunk + i * (chunk // 4), chunk // 4), chunk // 4)
            unit, _ = unit_rows(source[some, :].astype(F32))
            n.N1[l, some, :] = (unit * n.GAINS[2 * l : 2 * l + 1, :]).astype(BF16)

        kv = nn(n.N1[l, rows, :], n.W[l, 0, :, 0:q_columns])
        kv_low = kv.astype(BF16)
        turned = kv.T.astype(BF16)
        for h in range(heads):
            n.KV[l, h, rows, :] = kv_low[:, 2 * h * HEAD : 2 * (h + 1) * HEAD]
            n.KT[l, h, :, rows] = turned[2 * h * HEAD : (2 * h + 1) * HEAD]
            n.VT[h, :, rows] = turned[(2 * h + 1) * HEAD : (2 * h + 2) * HEAD]
        q = nn(n.N1[l, rows, :], n.W[l, 0, :, q_columns:o_columns]).astype(BF16)
        blank = jnp.zeros((chunk, HEAD), BF16)
        for h in range(heads):
            q_h = q[:, h * HEAD : (h + 1) * HEAD] * jnp.asarray(HEAD**-0.5, BF16)
            n.Q[l, h, rows, :] = jnp.concatenate([q_h, blank], axis=1)

    def attend(l, j, h):
        rows = rows_of(j)
        query = n.Q[l, h, rows, :]

        def block(i, carry, diagonal):
            top, total, out = carry
            keys = rows_of(i)
            st = nt(n.KV[l, h, keys, :], query)
            _, magnitude, sign = scores(l, st, i, j, diagonal)
            new_top = jnp.maximum(top, jnp.max(magnitude, axis=0, keepdims=True))
            weights = jnp.exp(magnitude - new_top)
            shrink = jnp.exp(top - new_top)
            total = total * shrink + jnp.sum(weights, axis=0, keepdims=True)
            signed = weights if l == 1 else sign * weights
            out = out * shrink + nn(n.VT[h, :, keys], signed.astype(BF16))
            return new_top, total, out

        carry = (
            jnp.full((1, chunk), MASKED, F32),
            jnp.zeros((1, chunk), F32),
            jnp.zeros((HEAD, chunk), F32),
        )
        carry = block(j, carry, True)
        top, total, out = lax.fori_loop(0, j, lambda i, c: block(i, c, False), carry)
        n.ATTT[l, h, :, rows] = out / total
        n.LSE[l, h, :, rows] = top + jnp.log(total)

    def out_product(l, j):
        rows = rows_of(j)
        joined = jnp.concatenate(
            [jnp.zeros((HEAD, chunk), F32)] + [n.ATTT[l, h, :, rows] for h in range(heads)],
            axis=0,
        )
        n.ATT[l, rows, :] = joined.T.astype(BF16)
        for i in range(tiles):
            here = slice(i * TILE, (i + 1) * TILE)
            n.PART[0, rows, here] = nt(
                n.ATT[l, rows, :], n.W[l, 0, here, o_columns - HEAD : width]
            ).astype(BF16)
        sum_start(SUM_ATTN[l], j)

    def attn_sum(l, j):
        source = n.X0 if l == 0 else n.Y0
        own = half_of(j, s)
        middle = source[own, :].astype(F32) + sum_wait(SUM_ATTN[l], j)
        n.MID[l, own_of(j), :] = middle
        unit, _ = unit_rows(middle)
        n.N2[l, own, :] = (unit * n.GAINS[2 * l + 1 : 2 * l + 2, :]).astype(BF16)
        pair_start(PAIR_N2[l], n.N2.at[l], j)

    def up_product(l, j):
        rows = rows_of(j)
        pair_wait(PAIR_N2[l], j)
        for i in range(tiles):
            here = slice(i * TILE, (i + 1) * TILE)
            pre = nn(n.N2[l, rows, :], n.W[l, 1, :, here])
            n.PRE[l, rows, here] = pre.astype(BF16)
            n.HID[rows, here] = gelu_parts(pre)[0].astype(BF16)

    def down_product(l, j):
        rows = rows_of(j)
        for i in range(tiles):
            here = slice(i * TILE, (i + 1) * TILE)
            n.PART[1, rows, here] = nt(n.HID[rows, :], n.W[l, 2, here, :]).astype(BF16)
        sum_start(SUM_MLP[l], j)

    def mlp_sum(l, j):
        result = n.MID[l, own_of(j), :] + sum_wait(SUM_MLP[l], j)
        if l == 0:
            n.Y0[half_of(j, s), :] = result.astype(BF16)
            pair_start(PAIR_MIDDLE, n.Y0, j)
        else:
            n.PART[1, half_of(j, s), :] = result.astype(BF16)
            last_out(0, 1, n.acts, j)

    def last_out(which, section, out, j):
        here = n.PART.at[1, half_of(j, s)]
        target = out.at[y, half_of(0, s)]

        @pl.when((s == section) & (t == j))
        def _():
            copy = pltpu.make_async_copy(here, target, n.out_send.at[which, j])
            copy.start()
            copy.wait()

        @pl.when((lax.rem(j, 2) == x) & ((s != section) | (t != j)))
        def _():
            remote(
                here,
                target,
                n.out_send.at[which, j],
                n.out_recv.at[which, y, s],
                (section, j, z),
            ).start()

    def last_out_sent(which, section, j):
        @pl.when((lax.rem(j, 2) == x) & ((s != section) | (t != j)))
        def _():
            done(bytes_of(part), n.out_send.at[which, j])

    def last_out_done(which, section, out):
        @pl.when(s == section)
        def _():
            for m in range(2):
                for c in range(2):

                    @pl.when((y != m) | (s != c))
                    def _():
                        done(bytes_of(part), n.out_recv.at[which, m, c])

    def full_out(which, section, ref, out):
        @pl.when(s == section)
        def _():
            pltpu.make_async_copy(
                ref.at[rows_of(t)], out.at[y], n.full_recv.at[which, y]
            ).start()
            remote(
                ref.at[rows_of(t_y)],
                out.at[y],
                n.full_send.at[which],
                n.full_recv.at[which, y],
                peer_y,
            ).start()

    def full_out_done(which, section):
        @pl.when(s == section)
        def _():
            done(bytes_of(chunk), n.full_recv.at[which, 0])
            done(bytes_of(chunk), n.full_recv.at[which, 1])
            done(bytes_of(chunk), n.full_send.at[which])

    def hidden_back(l, j):
        rows = rows_of(j)
        if l == 1:
            spread_wait(1, n.CT, j)
        else:
            pair_wait(PAIR_DR, j)
        source = n.CT if l == 1 else n.DR
        for i in range(tiles):
            here = slice(i * TILE, (i + 1) * TILE)
            back = nn(source[rows, :], n.W[l, 2, :, here])
            hidden, slope = gelu_parts(n.PRE[l, rows, here].astype(F32))
            n.HID[rows, here] = hidden.astype(BF16)
            n.DPRE[rows, here] = (slope * back).astype(BF16)

    def up_back(l, j):
        rows = rows_of(j)
        for i in range(tiles):
            here = slice(i * TILE, (i + 1) * TILE)
            n.PART[0, rows, here] = nt(n.DPRE[rows, :], n.W[l, 1, here, :]).astype(BF16)
        sum_start(SUM_DMLP[l], j)

    def mlp_back_sum(l, j):
        total = sum_wait(SUM_DMLP[l], j)
        source = n.CT if l == 1 else n.DR
        own = half_of(j, s)
        unit, scale = unit_rows(n.MID[l, own_of(j), :])
        n.GACC[l, 1:2, :] += jnp.sum(total * unit, axis=0, keepdims=True)
        gain = n.GAINS[2 * l + 1 : 2 * l + 2, :]
        grad = source[own, :].astype(F32) + norm_back(unit, scale, gain, total)
        n.DMID[own_of(j), :] = grad
        n.DA[l, own, :] = grad.astype(BF16)
        pair_start(PAIR_DA[l], n.DA.at[l], j)

    def attn_grad(l, j):
        rows = rows_of(j)
        pair_wait(PAIR_DA[l], j)

        @pl.when(j == CHUNKS - 1)
        def _():
            n.DKV[...] = jnp.zeros_like(n.DKV)

        back = nn(n.DA[l, rows, :], n.W[l, 0, :, o_columns - HEAD : width])
        low = back.astype(BF16)
        turned = low.astype(F32).T
        blank = jnp.zeros((chunk, HEAD), BF16)
        for h in range(heads):
            here = slice((h + 1) * HEAD, (h + 2) * HEAD)
            n.GRAD[h] = jnp.concatenate([blank, low[:, here]], axis=1)
            inner = jnp.sum(turned[here] * n.ATTT[l, h, :, rows], axis=0, keepdims=True)
            n.GRADT[h] = inner

    def attend_back(l, j, h):
        rows = rows_of(j)
        query = n.Q[l, h, rows, :]
        grad = n.GRAD[h]
        inner = n.GRADT[h]
        log_total = n.LSE[l, h, :, rows]

        def block(i, query_grad, diagonal):
            keys = rows_of(i)
            kv = n.KV[l, h, keys, :]
            st = nt(kv, query)
            dp = nt(kv, grad)
            inverse, magnitude, sign = scores(l, st, i, j, diagonal)
            weights = jnp.exp(magnitude - log_total)
            if l == 0:
                signed = sign * weights
                ds = weights * (sign * (sign * dp - inner) + dp * (inverse * inverse * inverse))
            else:
                signed = weights
                ds = weights * (dp - inner)
            ds = ds.astype(BF16)
            n.DKV[h, keys, :] += nn(ds, query) + nn(signed.astype(BF16), grad)
            return query_grad + nn(n.KT[l, h, :, keys], ds)

        query_grad = block(j, jnp.zeros((HEAD, chunk), F32), True)
        query_grad = lax.fori_loop(0, j, lambda i, c: block(i, c, False), query_grad)
        n.DQT[h] = query_grad * HEAD**-0.5

    def qkv_back(l, j):
        rows = rows_of(j)
        turned = jnp.concatenate([n.DQT[h] for h in range(heads)], axis=0).T
        for h in range(heads):
            n.DQKV[rows, 2 * h * HEAD : 2 * (h + 1) * HEAD] = n.DKV[h, rows, :].astype(BF16)
        n.DQKV[rows, q_columns:] = turned.astype(BF16)
        if l == 1:
            last_out_sent(0, 1, j)
        for i in range(tiles):
            here = slice(i * TILE, (i + 1) * TILE)
            n.PART[1, rows, here] = nt(n.DQKV[rows, :], n.W[l, 0, here, 0:o_columns]).astype(
                BF16
            )
        sum_start(SUM_DATTN[l], j)

    def attn_back_sum(l, j):
        total = sum_wait(SUM_DATTN[l], j)
        source = n.X0 if l == 0 else n.Y0
        own = half_of(j, s)
        unit, scale = unit_rows(source[own, :].astype(F32))
        n.GACC[l, 0:1, :] += jnp.sum(total * unit, axis=0, keepdims=True)
        gain = n.GAINS[2 * l : 2 * l + 1, :]
        result = n.DMID[own_of(j), :] + norm_back(unit, scale, gain, total)
        if l == 1:
            n.DR[own, :] = result.astype(BF16)
            pair_start(PAIR_DR, n.DR, j)
        else:
            n.PART[1, own, :] = result.astype(BF16)
            last_out(1, 0, n.igr, j)

    long = width // 2
    grad_order = ((1, 2), (1, 1), (1, 0), (0, 2), (0, 1), (0, 0))
    grad_to = 2 * s + x

    def kept_here(l):
        return hub & (s == l)

    def grad_sent(l, p, i):
        if not inside:
            done(n.STG.at[i], n.stg_send.at[l, p, i])
            return

        @pl.when(jnp.logical_not(kept_here(l)))
        def _():
            done(n.STG.at[i], n.stg_send.at[l, p, i])

    def weight_grad(l, p, i):
        at = grad_order.index((l, p))
        if at > 0:
            grad_sent(*grad_order[at - 1], i)
        rows = pl.ds(pl.multiple_of(i * long, long), long)
        if p == 0:
            left = n.N1[l, :, rows]
            n.STG[i, :, 0:256] = tn(left, n.DQKV[:, 0:256]).astype(BF16)
            n.STG[i, :, 256:512] = tn(left, n.DQKV[:, 256:512]).astype(BF16)
            last = tn(left, n.DQKV[:, 512:o_columns])
            out_part = tn(n.DA[l, :, rows], n.ATT[l])
            n.STG[i, :, 512:width] = jnp.concatenate([last, out_part[:, HEAD:]], axis=1).astype(
                BF16
            )
        else:
            if p == 1:
                left, right = n.N2[l, :, rows], n.DPRE
            else:
                left, right = (n.CT if l == 1 else n.DR)[:, rows], n.HID
            for k in range(tiles):
                here = slice(k * TILE, (k + 1) * TILE)
                n.STG[i, :, here] = tn(left, right[:, here]).astype(BF16)
        if not inside:
            pltpu.make_async_copy(
                n.STG.at[i], n.grads.at[l, p, rows], n.stg_send.at[l, p, i]
            ).start()
            return

        @pl.when(kept_here(l))
        def _():
            n.GR[0, p, rows, :] = n.STG[i]

        @pl.when(jnp.logical_not(kept_here(l)))
        def _():
            way = jnp.where(hub, 0, 1)
            remote(
                n.STG.at[i],
                n.GR.at[way, p, rows],
                n.stg_send.at[l, p, i],
                n.gr_recv.at[way, p, i],
                (l, grad_to, z),
            ).start()

    def slot_of(source, target):
        return jnp.where(source > target, source - 1, source)

    def grad_pass(l, p, i):
        if not inside:
            return

        @pl.when(s == l)
        def _():
            rows = pl.ds(pl.multiple_of(i * long, long), long)

            @pl.when(jnp.logical_not(hub))
            def _():
                done(n.GR.at[0, p, rows], n.gr_recv.at[0, p, i])

            done(n.GR.at[1, p, rows], n.gr_recv.at[1, p, i])
            for k in range(depth // 2):
                far = i * (depth // 2) + k

                @pl.when(z != far)
                def _():
                    here = slab_of(far)
                    n.GR[0, p, here, :] = (
                        n.GR[0, p, here, :].astype(F32) + n.GR[1, p, here, :].astype(F32)
                    ).astype(BF16)
                    slot = slot_of(z, far)
                    remote(
                        n.GR.at[0, p, here],
                        n.ZR.at[slot, p],
                        n.z_send.at[p, far],
                        n.z_recv.at[p, slot],
                        (s, t, far),
                    ).start()

    def grad_final(l, p):
        if not inside:
            return

        @pl.when(s == l)
        def _():
            here = slab_of(z)
            total = n.GR[0, p, here, :].astype(F32) + n.GR[1, p, here, :].astype(F32)
            for slot in range(depth - 1):
                done(n.ZR.at[slot, p], n.z_recv.at[p, slot])
                total = total + n.ZR[slot, p].astype(F32)
            n.FIN[p] = total
            pltpu.make_async_copy(n.FIN.at[p], n.gsum.at[p], n.fin_send.at[p]).start()

    def grads_done():
        if not inside:
            grad_sent(*grad_order[-1], 0)
            grad_sent(*grad_order[-1], 1)
            return
        grad_sent(*grad_order[-1], 0)
        grad_sent(*grad_order[-1], 1)
        for p in range(PARTS):
            for far in range(depth):

                @pl.when(z != far)
                def _():
                    done(n.ZR.at[0, p], n.z_send.at[p, far])

            done(n.FIN.at[p], n.fin_send.at[p])

    def gains_send():
        if not inside:
            n.GAINS[...] = n.gain_rows[...]
            return
        n.GIN[s, z] = n.gain_rows[...]
        for c in range(2):
            for far in range(depth):

                @pl.when((s != c) | (z != far))
                def _():
                    remote(
                        n.gain_rows,
                        n.GIN.at[s, z],
                        n.gin_send.at[c, far],
                        n.gin_recv.at[s, z],
                        (c, t, far),
                    ).start()

    def gains_wait():
        if not inside:
            return
        for c in range(2):
            for far in range(depth):

                @pl.when((s != c) | (z != far))
                def _():
                    done(n.gain_rows, n.gin_recv.at[c, far])
                    done(n.gain_rows, n.gin_send.at[c, far])

                for k in range(2):
                    n.GAINS[2 * c + k : 2 * c + k + 1, far * slab : (far + 1) * slab] = n.GIN[
                        c, far, k : k + 1, 0:slab
                    ]

    def gain_grads():
        if not inside:
            n.gain_out[...] = jnp.concatenate([n.GACC[0, 0:2], n.GACC[1, 0:2], n.GACC[0, 4:8]])
            return
        remote(n.GACC.at[1 - s], n.GC, n.gg_send.at[0], n.gg_recv.at[0], mate).start()
        done(n.GC, n.gg_recv.at[0])
        n.GACC[s] += n.GC[...]
        remote(n.GACC.at[s], n.GY, n.gg_send.at[1], n.gg_recv.at[1], peer_y).start()
        done(n.GY, n.gg_recv.at[1])
        n.GC[...] = n.GACC[s] + n.GY[...]
        for far in range(depth):

            @pl.when(z != far)
            def _():
                slot = slot_of(z, far)
                remote(
                    n.GC, n.GZ.at[slot], n.gg_send.at[2 + far], n.gg_recv.at[2 + slot], (s, t, far)
                ).start()

    def gain_grads_done():
        if not inside:
            return
        total = n.GC[...]
        for slot in range(depth - 1):
            done(n.GZ.at[slot], n.gg_recv.at[2 + slot])
            total = total + n.GZ[slot]
        n.gain_out[...] = total
        done(n.GC, n.gg_send.at[0])
        done(n.GC, n.gg_send.at[1])
        for far in range(depth):

            @pl.when(z != far)
            def _():
                done(n.GC, n.gg_send.at[2 + far])

    tasks = {"none": lambda h, j: None}
    for l in range(2):
        tasks[f"nq{l}"] = lambda h, j, l=l: norm_qkv(l, j)
        tasks[f"at{l}"] = lambda h, j, l=l: attend(l, j, h)
        tasks[f"op{l}"] = lambda h, j, l=l: out_product(l, j)
        tasks[f"sa{l}"] = lambda h, j, l=l: attn_sum(l, j)
        tasks[f"up{l}"] = lambda h, j, l=l: up_product(l, j)
        tasks[f"dn{l}"] = lambda h, j, l=l: down_product(l, j)
        tasks[f"sm{l}"] = lambda h, j, l=l: mlp_sum(l, j)
        tasks[f"hb{l}"] = lambda h, j, l=l: hidden_back(l, j)
        tasks[f"ub{l}"] = lambda h, j, l=l: up_back(l, j)
        tasks[f"sd{l}"] = lambda h, j, l=l: mlp_back_sum(l, j)
        tasks[f"ag{l}"] = lambda h, j, l=l: attn_grad(l, j)
        tasks[f"ab{l}"] = lambda h, j, l=l: attend_back(l, j, h)
        tasks[f"qb{l}"] = lambda h, j, l=l: qkv_back(l, j)
        tasks[f"sb{l}"] = lambda h, j, l=l: attn_back_sum(l, j)
        for p in range(PARTS):
            tasks[f"wg{l}{p}"] = lambda h, j, l=l, p=p: weight_grad(l, p, j)
    for p in range(PARTS):
        tasks[f"ws{p}"] = lambda h, j, p=p: weights_send(1, p)
    tasks["r"] = lambda h, j: sum_pass(h, j)
    tasks["x0"] = lambda h, j: spread_pass(0, n.X0, j)
    tasks["x1"] = lambda h, j: spread_pass(1, n.CT, j)
    tasks["wr"] = lambda h, j: weights_relay(h, j)
    tasks["ww"] = lambda h, j: weights_wait(h, j)
    tasks["gp"] = lambda h, j: grad_pass(lax.div(j, 2), h, lax.rem(j, 2))
    tasks["gf"] = lambda h, j: grad_final(j, h)
    tasks["fy"] = lambda h, j: full_out(0, 0, n.Y0, n.acts)
    tasks["fd"] = lambda h, j: full_out(1, 1, n.DR, n.igr)
    tasks["gw"] = lambda h, j: gains_wait()
    tasks["cs"] = lambda h, j: spread(1, n.cot, n.CT)
    order = list(tasks)
    run = [tasks[name] for name in order]

    weights_send(0, 0)
    gains_send()
    spread(0, n.inp, n.X0)
    weights_send(0, 1)
    weights_send(0, 2)
    n.GACC[...] = jnp.zeros_like(n.GACC)

    group = 12
    codes = [order.index(name) * 32 + h * 4 + j for name, h, j in steps]
    codes += [0] * (-len(codes) % group)
    pairs = [codes[i] + 4096 * codes[i + 1] for i in range(0, len(codes), 2)]
    per_group = group // 2
    groups = len(pairs) // per_group

    def pick(index, values):
        value = values[0]
        for at in range(1, len(values)):
            value = jnp.where(index == at, values[at], value)
        return value

    def dispatch(low, high, op, h, j):
        if high - low == 1:
            run[low](h, j)
            return
        middle = (low + high) // 2
        lax.cond(
            op < middle,
            lambda: dispatch(low, middle, op, h, j),
            lambda: dispatch(middle, high, op, h, j),
        )

    @pl.loop(0, groups)
    def _(g):
        words = [
            pick(g, [pairs[q * per_group + w] for q in range(groups)]) for w in range(per_group)
        ]

        @pl.loop(0, group)
        def _(i):
            word = pick(lax.div(i, 2), words)
            code = jnp.where(lax.rem(i, 2) == 0, lax.rem(word, 4096), lax.div(word, 4096))
            dispatch(
                0, len(run), lax.div(code, 32), lax.rem(lax.div(code, 4), 8), lax.rem(code, 4)
            )

    gain_grads()

    if inside:
        for p in range(PARTS):
            weights_sent(p)
            for l in range(2):

                @pl.when(hub)
                def _():
                    for far in range(depth):
                        done(n.W.at[l, p, slab_of(far)], n.relay_send.at[l, p, far])

    spread_done(0)
    spread_done(1)

    @pl.loop(0, CHUNKS)
    def _(j):
        for stage in range(6):
            done(bytes_of(part), n.pair_send.at[stage, j])
        last_out_sent(1, 0, j)

    full_out_done(0, 0)
    full_out_done(1, 1)
    last_out_done(0, 1, n.acts)
    last_out_done(1, 0, n.igr)
    grads_done()
    gain_grads_done()


def schedule():
    steps = []

    def add(name, j=0, h=0):
        steps.append((name, h, j))

    def when(name, j, h=0):
        if 0 <= j < CHUNKS:
            add(name, j, h)

    def back(name, j, h=0):
        if 0 <= j < CHUNKS:
            add(name, CHUNKS - 1 - j, h)

    add("gw")
    add("wr", 0, 0)
    for k in range(11):
        for l in range(2):
            when("r", k - 4 * l - 1, SUM_ATTN[l])
            when("r", k - 4 * l - 3, SUM_MLP[l])
        if k < CHUNKS:
            add("x0", k)
            if k == 0:
                add("ww", 0, 0)
        for l in range(2):
            if l == 1 and k == 4:
                add("wr", 0, 1)
                add("ww", 0, 1)
            for name in ("nq", "at", "op"):
                for h in range(3 if name == "at" else 1):
                    when(f"{name}{l}", k - 4 * l, h)
            if l == 0:
                for m in range(2):
                    when(f"sa{m}", k - 4 * m - 1)
                if k == 0:
                    add("wr", 1, 0)
                if k == 1:
                    add("wr", 2, 0)
                    for p in range(PARTS):
                        add(f"ws{p}")
                    add("cs")
                if k == 2:
                    add("ww", 1, 0)
                    add("ww", 2, 0)
                when("up0", k - 2)
                when("dn0", k - 2)
                for m in range(2):
                    when(f"sm{m}", k - 4 * m - 3)
        if k == 5:
            add("wr", 1, 1)
            add("wr", 2, 1)
        if k == 6:
            add("ww", 1, 1)
            add("ww", 2, 1)
            for j in range(CHUNKS):
                add("x1", j)
        when("up1", k - 6)
        when("dn1", k - 6)
        if k == 8:
            add("fy")
    for k in range(11):
        for l in (1, 0):
            lag = 4 * (1 - l)
            back("r", k - lag - 1, SUM_DMLP[l])
            back("r", k - lag - 3, SUM_DATTN[l])
        back("hb1", k)
        back("ub1", k)
        for l in (1, 0):
            back(f"sd{l}", k - 4 * (1 - l) - 1)
        back("ag1", k - 2)
        for h in range(3):
            back("ab1", k - 2, h)
        back("qb1", k - 2)
        for l in (1, 0):
            back(f"sb{l}", k - 4 * (1 - l) - 3)
        if k == 4:
            for p in (2, 1):
                add(f"wg1{p}", 0)
                add(f"wg1{p}", 1)
        back("hb0", k - 4)
        back("ub0", k - 4)
        if k == 6:
            add("wg10", 0)
            add("wg10", 1)
            for p in (2, 1):
                add("gp", 2, p)
                add("gp", 3, p)
        back("ag0", k - 6)
        for h in range(3):
            back("ab0", k - 6, h)
        back("qb0", k - 6)
        if k == 8:
            add("fd")
            for p in (2, 1):
                add(f"wg0{p}", 0)
                add(f"wg0{p}", 1)
            add("gp", 2, 0)
            add("gp", 3, 0)
            add("gf", 1, 2)
            add("gf", 1, 1)
    add("wg00", 0)
    add("wg00", 1)
    for p in (2, 1):
        add("gp", 0, p)
        add("gp", 1, p)
    add("gp", 0, 0)
    add("gp", 1, 0)
    add("gf", 1, 0)
    for p in (2, 1, 0):
        add("gf", 0, p)
    return steps


def run_blocks(inputs, cotangent, weights, gain_rows, bias, depth, inside):
    buckets, chunk, width = inputs.shape
    rows = CHUNKS * chunk
    part = chunk // 2
    heads = width // 4 // HEAD
    vmem, dma = pltpu.VMEM, pltpu.SemaphoreType.DMA
    scratch = dict(
        W=vmem((2, PARTS, width, width), BF16),
        X0=vmem((rows, width), BF16),
        Y0=vmem((rows, width), BF16),
        CT=vmem((rows, width), BF16),
        DR=vmem((rows, width), BF16),
        N1=vmem((2, rows, width), BF16),
        N2=vmem((2, rows, width), BF16),
        Q=vmem((2, heads, rows, 2 * HEAD), BF16),
        KV=vmem((2, heads, rows, 2 * HEAD), BF16),
        KT=vmem((2, heads, HEAD, rows), BF16),
        VT=vmem((heads, HEAD, rows), BF16),
        ATT=vmem((2, rows, (heads + 1) * HEAD), BF16),
        ATTT=vmem((2, heads, HEAD, rows), F32),
        LSE=vmem((2, heads, 1, rows), F32),
        PRE=vmem((2, rows, width), BF16),
        HID=vmem((rows, width), BF16),
        DPRE=vmem((rows, width), BF16),
        DQKV=vmem((rows, 3 * heads * HEAD), BF16),
        DA=vmem((2, rows, width), BF16),
        DKV=vmem((heads, rows, 2 * HEAD), F32),
        GRAD=vmem((heads, chunk, 2 * HEAD), BF16),
        GRADT=vmem((heads, 1, chunk), F32),
        DQT=vmem((heads, HEAD, chunk), F32),
        MID=vmem((2, CHUNKS * part, width), F32),
        DMID=vmem((CHUNKS * part, width), F32),
        PART=vmem((2, rows, width), BF16),
        RC=vmem((2, CHUNKS, part, width), BF16),
        RX=vmem((2, CHUNKS, part, width), BF16),
        STG=vmem((2, width // 2, width), BF16),
        GAINS=vmem((8, width), F32),
        GACC=vmem((2, 8, width), F32),
        in_send=dma((2, CHUNKS)),
        in_recv=dma((2, CHUNKS)),
        mate_send=dma((2, CHUNKS)),
        mate_recv=dma((2, CHUNKS)),
        pair_send=dma((6, CHUNKS)),
        pair_recv=dma((6, CHUNKS)),
        rs_send=dma((8, 2, CHUNKS)),
        rs_recv=dma((8, 2, CHUNKS)),
        w_recv=dma((2, PARTS, depth if inside else 1)),
        stg_send=dma((2, PARTS, 2)),
        out_send=dma((2, CHUNKS)),
        out_recv=dma((2, 2, 2)),
        full_send=dma((2,)),
        full_recv=dma((2, 2)),
    )
    outs = dict(
        acts=jax.ShapeDtypeStruct(inputs.shape, BF16), igr=jax.ShapeDtypeStruct(inputs.shape, BF16)
    )
    if inside:
        slab = width // depth
        scratch.update(
            GR=vmem((2, PARTS, width, width), BF16),
            ZR=vmem((depth - 1, PARTS, slab, width), BF16),
            FIN=vmem((PARTS, slab, width), F32),
            GIN=vmem((2, depth) + gain_rows.shape, F32),
            GC=vmem((8, width), F32),
            GY=vmem((8, width), F32),
            GZ=vmem((depth - 1, 8, width), F32),
            w_send=dma((PARTS, depth)),
            relay_send=dma((2, PARTS, depth)),
            gr_recv=dma((2, PARTS, 2)),
            z_send=dma((PARTS, depth)),
            z_recv=dma((PARTS, depth - 1)),
            fin_send=dma((PARTS,)),
            gin_send=dma((2, depth)),
            gin_recv=dma((2, depth)),
            gg_send=dma((2 + depth,)),
            gg_recv=dma((1 + depth,)),
        )
        own = dict(own_a=weights[0], own_b=weights[1], own_c=weights[2])
        outs["gsum"] = jax.ShapeDtypeStruct((PARTS, slab, width), F32)
    else:
        own = dict(w_whole=weights)
        outs["grads"] = jax.ShapeDtypeStruct(weights.shape, BF16)
    outs["gain_out"] = jax.ShapeDtypeStruct((8, width), F32)
    given = dict(inp=inputs, cot=cotangent, **own, gain_rows=gain_rows, bias=bias)
    hbm = pl.BlockSpec(memory_space=pl.ANY)
    in_vmem = pl.BlockSpec(memory_space=pltpu.VMEM)
    small = ("gain_rows", "bias", "gain_out")
    return pl.pallas_call(
        functools.partial(
            block_kernel, inside, schedule(), list(given) + list(outs) + list(scratch)
        ),
        out_shape=tuple(outs.values()),
        in_specs=[in_vmem if name in small else hbm for name in given],
        out_specs=tuple(in_vmem if name in small else hbm for name in outs),
        scratch_shapes=list(scratch.values()),
        compiler_params=pltpu.CompilerParams(
            collective_id=0, has_side_effects=True, vmem_limit_bytes=VMEM_LIMIT
        ),
        cost_estimate=pl.CostEstimate(
            flops=27_000_000_000, bytes_accessed=40_000_000, transcendentals=20_000_000
        ),
        name="blocks",
    )(*given.values())


def shards(inputs, lengths, gains, w_qkv, w_out, w_up, w_down, cotangent):
    local_rows, width = inputs.shape[1:]
    slab = w_up.shape[1]
    heads = w_qkv.shape[3] // HEAD
    depth = lax.axis_size("dp")
    y = lax.div(lax.axis_index("tensor"), 2)
    section = lax.axis_index("section")
    inside = slab % 16 == 0 and depth % 2 == 0
    split = (slab, heads, HEAD)
    kv = jnp.stack([w_qkv[0, :, 1].reshape(split), w_qkv[0, :, 2].reshape(split)], axis=2)
    own = (
        jnp.concatenate([kv.reshape(slab, -1), w_qkv[0, :, 0], w_out[0].T], axis=1),
        w_up[0],
        w_down[0].T,
    )
    bias = jnp.where(lengths[y] == CHUNKS * local_rows, 0.0, MASKED).astype(F32)
    bias = jnp.broadcast_to(bias, (8, local_rows))
    axes = ("section", "tensor")
    if inside:
        gain_rows = jnp.pad(gains[0].astype(F32), ((0, 6), (0, -slab % 128)))
        acts, input_grads, total, gain_part = run_blocks(
            inputs, cotangent, own, gain_rows, bias, depth, inside
        )
        gain_part = gain_part[None, :2]
        at = lax.axis_index("tensor") * depth + lax.axis_index("dp")
        share = width // (depth * lax.axis_size("tensor"))
        gain_grads = lax.dynamic_slice_in_dim(gain_part, at * share, share, 2)
    else:
        whole = lax.all_gather(jnp.stack(own), "dp", axis=1, tiled=True)
        weights = []
        for l in range(2):
            parts = []
            for to_y in range(2):
                pairs = [
                    (4 * l + 2 * c + x, 4 * c + 2 * to_y + x) for c in range(2) for x in range(2)
                ]
                parts.append(lax.ppermute(whole, axes, pairs))
            weights.append(jnp.where(y == 0, parts[0], parts[1]))
        weights = jnp.stack(weights)
        gain_rows = lax.all_gather(gains, "dp", axis=2, tiled=True)
        gain_rows = lax.all_gather(gain_rows, "section", axis=0, tiled=True)
        gain_rows = jnp.pad(gain_rows.reshape(4, width).astype(F32), ((0, 4), (0, 0)))
        acts, input_grads, partial, gain_part = run_blocks(
            inputs, cotangent, weights, gain_rows, bias, depth, inside
        )
        total = jnp.zeros(partial.shape[1:], F32)
        for l in range(2):
            for from_y in range(2):
                pairs = [
                    (4 * c + 2 * from_y + x, 4 * l + 2 * c + x) for c in range(2) for x in range(2)
                ]
                total = total + lax.ppermute(partial[l], axes, pairs).astype(F32)
        total = lax.psum_scatter(total.astype(BF16), "dp", scatter_dimension=1, tiled=True)
        total = total.astype(F32)
        gain_part = lax.psum(gain_part[:4].reshape(2, 2, width), "section")
        gain_part = lax.dynamic_slice_in_dim(gain_part, section, 1, 0)
        gain_grads = 0.5 * lax.psum_scatter(
            gain_part, ("tensor", "dp"), scatter_dimension=2, tiled=True
        )
    columns = heads * HEAD
    kv = total[0, :, : 2 * columns].reshape(slab, heads, 2, HEAD)
    q = total[0, :, 2 * columns : 3 * columns]
    qkv_grads = jnp.stack([q, kv[:, :, 0].reshape(q.shape), kv[:, :, 1].reshape(q.shape)], axis=1)
    return (
        acts[None],
        input_grads[None],
        gain_grads,
        qkv_grads[None],
        total[0, :, 3 * columns :].T[None],
        total[1][None],
        total[2].T[None],
    )


def solution(mesh):
    in_specs = (
        P("dp", "tensor", None),
        P("dp"),
        P("section", None, "dp"),
        P("section", "dp", None, "tensor"),
        P("section", "tensor", "dp"),
        P("section", "dp", "tensor"),
        P("section", "tensor", "dp"),
        P("dp", "tensor", None),
    )
    out_specs = (
        P("section", "dp", "tensor", None),
        P("section", "dp", "tensor", None),
        P("section", None, ("tensor", "dp")),
        P("section", "dp", None, "tensor"),
        P("section", "tensor", "dp"),
        P("section", "dp", "tensor"),
        P("section", "tensor", "dp"),
    )
    return jax.shard_map(shards, mesh=mesh, in_specs=in_specs, out_specs=out_specs, check_vma=False)
```

time: 1330 us -> 440 us (0.33)
  waiting for transfers between devices: 765 us -> 0 us
  Pallas kernels: 0 us -> 426 us
  matrix products: 313 us -> 0 us
  other arithmetic: 98.1 us -> 2.31 us
  blocking collectives: 62 us -> 0 us
  local copies, waits for them, and re-layouts: 50 us -> 10.2 us
  between operations: 22.6 us -> 1.43 us
    pallas_call x0 -> x1, Pallas kernels: none -> 426 us  [run_blocks(): pl.pallas_call(functools.partial(block_kernel, inside, schedule(), list(g...]
    reduce_scatter x13 -> x0, waiting for transfers between devices: 342 us -> none  [the longest x6 191 us: summed_branch(): lax.psum_scatter(term_fn(jnp.int32(0), lax.axis_size('tensor') * local_ro...]
    all_gather x14 -> x0, waiting for transfers between devices: 263 us -> none  [the longest x6 136 us: gathered_rows(): return lax.all_gather(local_piece, 'tensor', axis=0, tiled=True)]
    dot_general x72 -> x0, matrix products: 250 us -> none  [the longest x6 48.3 us: attend_back(): jnp.einsum('qhd,khd->hqk', query_block, key_rows[:row_end], preferred_ele...]
    unnamed x35 -> x0, waiting for transfers between devices: 153 us -> none
    sub x6 -> x0, matrix products: 63.3 us -> none  [attend_back(): direction * prob_grad - row_inner]
    all_gather x3 -> x0, blocking collectives: 62 us -> none  [the longest x1 28.6 us: shards(): lax.all_gather(w_qkv, 'dp', axis=1, tiled=True)]
    reduce_sum x32 -> x0, other arithmetic: 50.4 us -> none  [the longest x6 20.7 us: attend(): weight_sum = jnp.sum(weights, axis=-1, keepdims=True)]
  transfers between devices with their start and end apart: 35 -> 0, of which waited for: 29 -> 0; matrix products, arithmetic and copies ran while one was open for 16% -> 0% of each run, Pallas kernels for 0% -> 0%
where the time goes in v2:
time: 440 us
  Pallas kernels  426 us (97%)
  local copies, waits for them, and re-layouts  10.2 us (2%)
    pallas_call x1, Pallas kernels, run_blocks(): pl.pallas_call(functools.partial(block_kernel, inside, schedule(), list(g...  426 us

profile of v2, /device:TPU:0, one launch (start us, length us, event | category | flops | bytes accessed | tf_op | source)
XLA Modules:
  0.0 439.6 jit_solution(17522824463501667161)
XLA Ops:
  0.6 0.0 copy-start.3
  0.6 0.0 copy-start.4
  0.7 1.0 copy.22
  1.7 1.0 fusion.1
  2.7 0.1 copy.29
  2.8 0.1 copy.28
  3.0 0.1 copy.23
  3.1 0.8 pad_maximum_fusion.refs_2_
  3.9 0.0 copy-done.3
  3.9 0.6 pad_convert_fusion.refs_5_
  4.5 0.0 copy-done.4
  4.5 0.6 dynamic_slice.6
  5.8 0.6 broadcast_in_dim.19.refs_6_
  6.4 425.6 %blocks.1 = (bf16[2,256,768]{2,1,0:T(8,128)(2,1)}, bf16[2,256,768]{2,1,0:T(8,128)(2,1)}, f32[3,192,768]{2,1,0:T(8,128)}, f32[8,768]{1,0:T(8,128)}) custom-call(bf16[2,256,768]{2,1,0:T(8,128)(2,1)} %refs_0_.1, bf16[2,256,768]{2,1,0:T(8,128)(2,1)} %refs_1_.1, bf16[192,768]{1,0:T(8,128)(2,1)} %pad_maximum_fusion.refs_2_, bf16[192,768]{1,0:T(8,128)(2,1)} %bitcast.47, ...), custom_call_target="tpu_custom_call" | custom-call | flops 27000000512 | bytes 40000000 | tf_op jit(solution)/shard_map/blocks/pallas_call | solution.py:1071
  432.0 0.0 copy-start
  432.0 0.9 slice.36
  432.9 0.6 dynamic-slice_bitcast_fusion
  433.5 1.0 slice.38
  434.5 0.2 copy.24
  434.7 0.1 copy.26
  434.8 0.1 copy.25
  434.9 0.0 copy-done
  434.9 0.1 slice_bitcast_fusion.1
  435.1 0.0 copy-start.2
  435.1 0.9 maximum_bitcast_fusion
  435.9 0.8 copy.27
  436.7 0.0 copy-start.1
  436.7 1.1 slice_bitcast_fusion
  437.8 0.0 copy-done.2
  437.8 0.9 copy.32
  438.7 0.0 copy-done.1
  438.7 0.9 copy.33
  (3 shorter events, 0.1 us)
Async XLA Ops:
  0.6 3.3 copy-start.3
  0.6 3.9 copy-start.4
  432.0 2.9 copy-start
  435.1 2.7 copy-start.2
  436.7 2.0 copy-start.1

commit v3 on v2

--- a/solution.py
+++ b/solution.py
@@ -868,117 +868,47 @@
     gain_grads_done()
 
 
-def schedule():
-    steps = []
-
-    def add(name, j=0, h=0):
-        steps.append((name, h, j))
-
-    def when(name, j, h=0):
-        if 0 <= j < CHUNKS:
-            add(name, j, h)
-
-    def back(name, j, h=0):
-        if 0 <= j < CHUNKS:
-            add(name, CHUNKS - 1 - j, h)
-
-    add("gw")
-    add("wr", 0, 0)
-    for k in range(11):
-        for l in range(2):
-            when("r", k - 4 * l - 1, SUM_ATTN[l])
-            when("r", k - 4 * l - 3, SUM_MLP[l])
-        if k < CHUNKS:
-            add("x0", k)
-            if k == 0:
-                add("ww", 0, 0)
-        for l in range(2):
-            if l == 1 and k == 4:
-                add("wr", 0, 1)
-                add("ww", 0, 1)
-            for name in ("nq", "at", "op"):
-                for h in range(3 if name == "at" else 1):
-                    when(f"{name}{l}", k - 4 * l, h)
-            if l == 0:
-                for m in range(2):
-                    when(f"sa{m}", k - 4 * m - 1)
-                if k == 0:
-                    add("wr", 1, 0)
-                if k == 1:
-                    add("wr", 2, 0)
-                    for p in range(PARTS):
-                        add(f"ws{p}")
-                    add("cs")
-                if k == 2:
-                    add("ww", 1, 0)
-                    add("ww", 2, 0)
-                when("up0", k - 2)
-                when("dn0", k - 2)
-                for m in range(2):
-                    when(f"sm{m}", k - 4 * m - 3)
-        if k == 5:
-            add("wr", 1, 1)
-            add("wr", 2, 1)
-        if k == 6:
-            add("ww", 1, 1)
-            add("ww", 2, 1)
-            for j in range(CHUNKS):
-                add("x1", j)
-        when("up1", k - 6)
-        when("dn1", k - 6)
-        if k == 8:
-            add("fy")
-    for k in range(11):
-        for l in (1, 0):
-            lag = 4 * (1 - l)
-            back("r", k - lag - 1, SUM_DMLP[l])
-            back("r", k - lag - 3, SUM_DATTN[l])
-        back("hb1", k)
-        back("ub1", k)
-        for l in (1, 0):
-            back(f"sd{l}", k - 4 * (1 - l) - 1)
-        back("ag1", k - 2)
-        for h in range(3):
-            back("ab1", k - 2, h)
-        back("qb1", k - 2)
-        for l in (1, 0):
-            back(f"sb{l}", k - 4 * (1 - l) - 3)
-        if k == 4:
-            for p in (2, 1):
-                add(f"wg1{p}", 0)
-                add(f"wg1{p}", 1)
-        back("hb0", k - 4)
-        back("ub0", k - 4)
-        if k == 6:
-            add("wg10", 0)
-            add("wg10", 1)
-            for p in (2, 1):
-                add("gp", 2, p)
-                add("gp", 3, p)
-        back("ag0", k - 6)
-        for h in range(3):
-            back("ab0", k - 6, h)
-        back("qb0", k - 6)
-        if k == 8:
-            add("fd")
-            for p in (2, 1):
-                add(f"wg0{p}", 0)
-                add(f"wg0{p}", 1)
-            add("gp", 2, 0)
-            add("gp", 3, 0)
-            add("gf", 1, 2)
-            add("gf", 1, 1)
-    add("wg00", 0)
-    add("wg00", 1)
-    for p in (2, 1):
-        add("gp", 0, p)
-        add("gp", 1, p)
-    add("gp", 0, 0)
-    add("gp", 1, 0)
-    add("gf", 1, 0)
-    for p in (2, 1, 0):
-        add("gf", 0, p)
-    return steps
+STEPS = (
+    ("x0", 0, 3), ("gw", 0, 0), ("cs", 0, 0), ("x0", 0, 0), ("x0", 0, 1), ("x0", 0, 2),
+    ("wr", 0, 0), ("ww", 0, 0), ("ws0", 0, 0), ("nq0", 0, 0), ("at0", 0, 0), ("at0", 2, 0),
+    ("at0", 1, 0), ("nq0", 0, 3), ("nq0", 0, 1), ("wr", 0, 1), ("op0", 0, 0), ("at0", 2, 1),
+    ("at0", 1, 1), ("nq0", 0, 2), ("x1", 0, 3), ("at0", 0, 1), ("at0", 0, 2), ("r", 0, 0),
+    ("wr", 0, 2), ("op0", 0, 1), ("at0", 2, 2), ("ws1", 0, 0), ("at0", 1, 2), ("r", 0, 1),
+    ("at0", 1, 3), ("at0", 0, 3), ("ww", 0, 1), ("op0", 0, 2), ("sa0", 0, 0), ("x1", 0, 0),
+    ("sa0", 0, 1), ("r", 0, 2), ("up0", 0, 0), ("wr", 1, 0), ("up0", 0, 1), ("ww", 0, 2),
+    ("dn0", 0, 0), ("r", 1, 0), ("dn0", 0, 1), ("ws2", 0, 0), ("r", 1, 1), ("at0", 2, 3),
+    ("sa0", 0, 2), ("op0", 0, 3), ("up0", 0, 2), ("r", 0, 3), ("dn0", 0, 2), ("sm0", 0, 0),
+    ("wr", 1, 1), ("x1", 0, 1), ("ww", 1, 0), ("sm0", 0, 1), ("nq1", 0, 0), ("r", 1, 2),
+    ("sa0", 0, 3), ("at1", 0, 0), ("at1", 1, 0), ("up0", 0, 3), ("at1", 2, 0), ("dn0", 0, 3),
+    ("nq1", 0, 1), ("at1", 0, 1), ("r", 1, 3), ("sm0", 0, 2), ("op1", 0, 0), ("at1", 1, 1),
+    ("at1", 2, 1), ("nq1", 0, 2), ("op1", 0, 1), ("r", 2, 0), ("at1", 0, 2), ("at1", 2, 2),
+    ("sm0", 0, 3), ("wr", 1, 2), ("x1", 0, 2), ("at1", 1, 2), ("r", 2, 1), ("op1", 0, 2),
+    ("ww", 1, 1), ("nq1", 0, 3), ("at1", 2, 3), ("sa1", 0, 0), ("r", 2, 2), ("at1", 1, 3),
+    ("at1", 0, 3), ("op1", 0, 3), ("sa1", 0, 1), ("up1", 0, 0), ("r", 2, 3), ("sa1", 0, 2),
+    ("ww", 1, 2), ("dn1", 0, 0), ("r", 3, 0), ("up1", 0, 1), ("sa1", 0, 3), ("dn1", 0, 1),
+    ("fy", 0, 0), ("r", 3, 1), ("up1", 0, 2), ("dn1", 0, 2), ("up1", 0, 3), ("hb1", 0, 2),
+    ("hb1", 0, 0), ("dn1", 0, 3), ("sm1", 0, 0), ("r", 3, 3), ("hb1", 0, 3), ("ub1", 0, 3),
+    ("hb1", 0, 1), ("wg12", 0, 1), ("r", 3, 2), ("ub1", 0, 1), ("sm1", 0, 3), ("r", 4, 3),
+    ("ub1", 0, 2), ("sm1", 0, 2), ("sm1", 0, 1), ("ub1", 0, 0), ("r", 4, 2), ("wg11", 0, 1),
+    ("sd1", 0, 3), ("r", 4, 0), ("wg12", 0, 0), ("ag1", 0, 3), ("ab1", 1, 3), ("ab1", 2, 3),
+    ("sd1", 0, 2), ("r", 4, 1), ("ab1", 0, 3), ("qb1", 0, 3), ("ag1", 0, 2), ("sd1", 0, 0),
+    ("ab1", 0, 2), ("ab1", 1, 2), ("r", 5, 3), ("sd1", 0, 1), ("ab1", 2, 2), ("qb1", 0, 2),
+    ("ag1", 0, 1), ("ab1", 2, 1), ("r", 5, 2), ("wg11", 0, 0), ("gp", 1, 3), ("ab1", 0, 1),
+    ("gp", 2, 2), ("ab1", 1, 1), ("qb1", 0, 1), ("ag1", 0, 0), ("ab1", 1, 0), ("ab1", 0, 0),
+    ("r", 5, 1), ("ab1", 2, 0), ("sb1", 0, 3), ("qb1", 0, 0), ("wg10", 0, 0), ("sb1", 0, 2),
+    ("hb0", 0, 3), ("r", 5, 0), ("gp", 1, 2), ("ub0", 0, 3), ("sb1", 0, 1), ("r", 6, 3),
+    ("hb0", 0, 2), ("ub0", 0, 2), ("wg10", 0, 1), ("hb0", 0, 1), ("ub0", 0, 1), ("r", 6, 2),
+    ("gp", 2, 3), ("sb1", 0, 0), ("sd0", 0, 3), ("r", 6, 1), ("hb0", 0, 0), ("wg02", 0, 0),
+    ("ag0", 0, 3), ("gp", 0, 3), ("sd0", 0, 2), ("wg02", 0, 1), ("gp", 0, 2), ("ab0", 1, 3),
+    ("ab0", 0, 3), ("gf", 2, 1), ("ab0", 2, 3), ("qb0", 0, 3), ("ag0", 0, 2), ("sd0", 0, 1),
+    ("ub0", 0, 0), ("ab0", 0, 2), ("wg01", 0, 0), ("gp", 2, 0), ("r", 6, 0), ("ab0", 2, 2),
+    ("ab0", 1, 2), ("qb0", 0, 2), ("ag0", 0, 1), ("gp", 2, 1), ("wg01", 0, 1), ("ab0", 1, 1),
+    ("ab0", 2, 1), ("ab0", 0, 1), ("qb0", 0, 1), ("gp", 1, 0), ("sd0", 0, 0), ("ag0", 0, 0),
+    ("r", 7, 1), ("gf", 0, 1), ("ab0", 0, 0), ("ab0", 2, 0), ("ab0", 1, 0), ("qb0", 0, 0),
+    ("r", 7, 2), ("wg00", 0, 0), ("r", 7, 3), ("r", 7, 0), ("gp", 1, 1), ("sb0", 0, 1),
+    ("gf", 1, 1), ("wg00", 0, 1), ("gp", 0, 0), ("sb0", 0, 3), ("gp", 0, 1), ("sb0", 0, 2),
+    ("gf", 1, 0), ("fd", 0, 0), ("gf", 2, 0), ("sb0", 0, 0), ("gf", 0, 0),
+)
 
 
 def run_blocks(inputs, cotangent, weights, gain_rows, bias, depth, inside):
@@ -1070,7 +1000,7 @@
     small = ("gain_rows", "bias", "gain_out")
     return pl.pallas_call(
         functools.partial(
-            block_kernel, inside, schedule(), list(given) + list(outs) + list(scratch)
+            block_kernel, inside, STEPS, list(given) + list(outs) + list(scratch)
         ),
         out_shape=tuple(outs.values()),
         in_specs=[in_vmem if name in small else hbm for name in given],

time: 440 us -> 290 us (0.66); the launches traced: 440 us -> 285 us
  Pallas kernels: 426 us -> 271 us
    pallas_call x1, Pallas kernels: 426 us -> 271 us  [run_blocks(): pl.pallas_call(functools.partial(block_kernel, inside, STEPS, list(given)...]
where the time goes in v3:
time: 290 us; the launch traced here: 285 us
  Pallas kernels  271 us (93%)
  local copies, waits for them, and re-layouts  10.2 us (4%)
    pallas_call x1, Pallas kernels, run_blocks(): pl.pallas_call(functools.partial(block_kernel, inside, STEPS, list(given)...  271 us

profile of v3, /device:TPU:0, one launch (start us, length us, event | category | flops | bytes accessed | tf_op | source)
XLA Modules:
  0.0 284.6 jit_solution(5927190753652400704)
XLA Ops:
  0.6 0.0 copy-start.3
  0.6 0.0 copy-start.4
  0.7 1.0 copy.22
  1.7 1.0 fusion.1
  2.7 0.1 copy.29
  2.8 0.1 copy.28
  3.0 0.1 copy.23
  3.1 0.8 pad_maximum_fusion.refs_2_
  3.9 0.0 copy-done.3
  3.9 0.6 pad_convert_fusion.refs_5_
  4.5 0.0 copy-done.4
  4.5 0.6 dynamic_slice.6
  5.8 0.6 broadcast_in_dim.19.refs_6_
  6.4 270.7 %blocks.1 = (bf16[2,256,768]{2,1,0:T(8,128)(2,1)}, bf16[2,256,768]{2,1,0:T(8,128)(2,1)}, f32[3,192,768]{2,1,0:T(8,128)}, f32[8,768]{1,0:T(8,128)}) custom-call(bf16[2,256,768]{2,1,0:T(8,128)(2,1)} %refs_0_.1, bf16[2,256,768]{2,1,0:T(8,128)(2,1)} %refs_1_.1, bf16[192,768]{1,0:T(8,128)(2,1)} %pad_maximum_fusion.refs_2_, bf16[192,768]{1,0:T(8,128)(2,1)} %bitcast.47, ...), custom_call_target="tpu_custom_call" | custom-call | flops 27000000512 | bytes 40000000 | tf_op jit(solution)/shard_map/blocks/pallas_call | solution.py:1001
  277.1 0.0 copy-start
  277.1 0.9 slice.36
  277.9 0.6 dynamic-slice_bitcast_fusion
  278.6 1.0 slice.38
  279.5 0.2 copy.24
  279.8 0.1 copy.26
  279.9 0.1 copy.25
  280.0 0.0 copy-done
  280.0 0.1 slice_bitcast_fusion.1
  280.1 0.0 copy-start.2
  280.1 0.9 maximum_bitcast_fusion
  281.0 0.8 copy.27
  281.8 0.0 copy-start.1
  281.8 1.1 slice_bitcast_fusion
  282.9 0.0 copy-done.2
  282.9 0.9 copy.32
  283.7 0.0 copy-done.1
  283.8 0.9 copy.33
  (3 shorter events, 0.1 us)
Async XLA Ops:
  0.6 3.3 %copy-start.3 = (bf16[1,2,192]{2,1,0:T(2,128)(2,1)S(1)}, bf16[1,2,192]{2,1,0:T(2,128)(2,1)}, u32[]{:S(2)}) copy-start(bf16[1,2,192]{2,1,0:T(2,128)(2,1)} %param.10) | copy-start | bytes 2308
  0.6 3.9 %copy-start.4 = (s32[2]{0:T(128)S(1)}, s32[2]{0:T(128)}, u32[]{:S(2)}) copy-start(s32[2]{0:T(128)} %param.9) | copy-start | bytes 28
  277.1 2.9 %copy-start = (f32[3,192,768]{2,1,0:T(8,128)S(1)}, f32[3,192,768]{2,1,0:T(8,128)}, u32[]{:S(2)}) copy-start(f32[3,192,768]{2,1,0:T(8,128)} %get-tuple-element.14) | copy-start | bytes 5308420
  280.1 2.7 copy-start.2
  281.8 2.0 copy-start.1

commit v4 on v3

--- a/solution.py
+++ b/solution.py
@@ -23,7 +23,7 @@
 SUM_DMLP = (6, 4)
 SUM_DATTN = (7, 5)
 PAIR_N2 = (0, 1)
-PAIR_MIDDLE = 2
+PAIR_N1 = (6, 2)
 PAIR_DA = (4, 3)
 PAIR_DR = 5
 
@@ -80,7 +80,7 @@
     peer_x = (s, 2 * y + 1 - x, z)
     peer_y = (s, t_y, z)
     hub = s == y
-    rows_all, width = n.X0.shape
+    rows_all, width = n.CT.shape
     chunk = rows_all // CHUNKS
     part = chunk // 2
     half = CHUNKS // 2
@@ -143,6 +143,12 @@
 
     pl.semaphore_wait(barrier, greeted - 1 - (2 if inside else 0))
 
+    def pick(index, values):
+        value = values[0]
+        for at in range(1, len(values)):
+            value = jnp.where(index == at, values[at], value)
+        return value
+
     def weights_send(l, p):
         if not inside:
             pltpu.make_async_copy(n.w_whole.at[l, p], n.W.at[l, p], n.w_recv.at[l, p, 0]).start()
@@ -176,19 +182,19 @@
             def _():
                 done(own, n.w_send.at[p, far])
 
-    def weights_relay(l, p):
+    def weights_relay(l, p, step):
         if not inside:
             return
 
         @pl.when(hub)
         def _():
-            for step in range(depth):
-                far = lax.rem(z + step, depth)
-                here = n.W.at[l, p, slab_of(far)]
-                done(here, n.w_recv.at[l, p, far])
-                remote(
-                    here, here, n.relay_send.at[l, p, far], n.w_recv.at[l, p, far], peer_y
-                ).start()
+            beside = z + 1 - 2 * lax.rem(z, 2)
+            far = pick(step, [z, beside, lax.rem(z + 2, depth), lax.rem(beside + 2, depth)])
+            here = n.W.at[l, p, slab_of(far)]
+            done(here, n.w_recv.at[l, p, far])
+            remote(
+                here, here, n.relay_send.at[l, p, far], n.w_recv.at[l, p, far], peer_y
+            ).start()
 
     def weights_wait(l, p):
         if not inside:
@@ -201,8 +207,9 @@
                 done(n.W.at[l, p, slab_of(far)], n.w_recv.at[l, p, far])
 
     def spread(which, source, target):
+        own = target.at[own_of(t)] if which == 0 else target.at[half_of(t, s)]
         pltpu.make_async_copy(
-            source.at[y], target.at[rows_of(t)], n.in_recv.at[which, t]
+            source.at[y, half_of(0, s)], own, n.in_recv.at[which, t]
         ).start()
         for other in range(CHUNKS):
 
@@ -210,29 +217,23 @@
             def _():
                 remote(
                     source.at[other // 2, half_of(0, s)],
-                    target.at[half_of(t, s)],
+                    own,
                     n.in_send.at[which, other],
                     n.in_recv.at[which, t],
                     (s, other, z),
                 ).start()
 
-    def spread_pass(which, target, j):
-        @pl.when(j == t)
-        def _():
-            done(target.at[rows_of(j)], n.in_recv.at[which, j])
-
-        @pl.when(j != t)
-        def _():
-            here = target.at[half_of(j, s)]
-            done(here, n.in_recv.at[which, j])
-            remote(
-                here, here, n.mate_send.at[which, j], n.mate_recv.at[which, j], mate
-            ).start()
-
-    def spread_wait(which, target, j):
-        @pl.when(j != t)
-        def _():
-            done(target.at[half_of(j, s)], n.mate_recv.at[which, j])
+    def inputs_pass(j):
+        done(bytes_of(part), n.in_recv.at[0, j])
+        norm_first(0, n.X0[own_of(j), :].astype(F32), j)
+
+    def cotangent_pass(j):
+        here = n.CT.at[half_of(j, s)]
+        done(here, n.in_recv.at[1, j])
+        remote(here, here, n.mate_send.at[j], n.mate_recv.at[j], mate).start()
+
+    def cotangent_wait(j):
+        done(bytes_of(part), n.mate_recv.at[j])
 
     def spread_done(which):
         for other in range(CHUNKS):
@@ -240,7 +241,9 @@
             @pl.when(t != other)
             def _():
                 done(bytes_of(part), n.in_send.at[which, other])
-                done(bytes_of(part), n.mate_send.at[which, other])
+
+            if which == 1:
+                done(bytes_of(part), n.mate_send.at[other])
 
     def pair_start(stage, ref, j):
         here = ref.at[half_of(j, s)]
@@ -266,20 +269,31 @@
         n.PART[b, here, :] = (
             n.PART[b, here, :].astype(F32) + n.RC[b, j].astype(F32)
         ).astype(BF16)
-        remote(
-            n.PART.at[b, here],
-            n.RX.at[b, j],
-            n.rs_send.at[stage, 1, j],
-            n.rs_recv.at[stage, 1, j],
-            peer_x,
-        ).start()
+        arriving = jnp.where(stage == SUM_DMLP[1], 2, b)
+        one_way = (stage == SUM_MLP[1]) | (stage == SUM_DATTN[0])
+
+        @pl.when(jnp.logical_not(one_way) | (lax.rem(j, 2) != x))
+        def _():
+            remote(
+                n.PART.at[b, here],
+                n.RX.at[arriving, j],
+                n.rs_send.at[stage, 1, j],
+                n.rs_recv.at[stage, 1, j],
+                peer_x,
+            ).start()
+
         done(n.RC.at[b, j], n.rs_send.at[stage, 0, j])
+
+    def sum_sent(stage, j):
+        done(n.RX.at[stage % 2, j], n.rs_send.at[stage, 1, j])
 
     def sum_wait(stage, j):
         b = stage % 2
-        done(n.RX.at[b, j], n.rs_recv.at[stage, 1, j])
-        total = n.PART[b, half_of(j, s), :].astype(F32) + n.RX[b, j].astype(F32)
-        done(n.RX.at[b, j], n.rs_send.at[stage, 1, j])
+        arriving = 2 if stage == SUM_DMLP[1] else b
+        done(n.RX.at[arriving, j], n.rs_recv.at[stage, 1, j])
+        total = n.PART[b, half_of(j, s), :].astype(F32) + n.RX[arriving, j].astype(F32)
+        if stage not in (SUM_MLP[1], SUM_DATTN[0]):
+            sum_sent(stage, j)
         return total
 
     key_index = lax.broadcasted_iota(jnp.int32, (chunk, chunk), 0)
@@ -301,20 +315,14 @@
             magnitude = magnitude + jnp.where(apart, n.bias[0:1, 0:chunk], 0.0)
         return inverse, magnitude, sign
 
-    def norm_qkv(l, j):
+    def norm_first(l, own_rows, j):
+        unit, _ = unit_rows(own_rows)
+        n.N1[l, half_of(j, s), :] = (unit * n.GAINS[2 * l : 2 * l + 1, :]).astype(BF16)
+        pair_start(PAIR_N1[l], n.N1.at[l], j)
+
+    def qkv_product(l, j):
         rows = rows_of(j)
-        if l == 0:
-            spread_wait(0, n.X0, j)
-        else:
-            pair_wait(PAIR_MIDDLE, j)
-        source = n.X0 if l == 0 else n.Y0
-
-        @pl.loop(0, 4)
-        def _(i):
-            some = pl.ds(pl.multiple_of(j * chunk + i * (chunk // 4), chunk // 4), chunk // 4)
-            unit, _ = unit_rows(source[some, :].astype(F32))
-            n.N1[l, some, :] = (unit * n.GAINS[2 * l : 2 * l + 1, :]).astype(BF16)
-
+        pair_wait(PAIR_N1[l], j)
         kv = nn(n.N1[l, rows, :], n.W[l, 0, :, 0:q_columns])
         kv_low = kv.astype(BF16)
         turned = kv.T.astype(BF16)
@@ -327,6 +335,11 @@
         for h in range(heads):
             q_h = q[:, h * HEAD : (h + 1) * HEAD] * jnp.asarray(HEAD**-0.5, BF16)
             n.Q[l, h, rows, :] = jnp.concatenate([q_h, blank], axis=1)
+
+    def heads_loop(task, l, j, h):
+        @pl.loop(jnp.where(h == heads, 0, h), jnp.where(h == heads, heads, h + 1))
+        def _(one):
+            task(l, j, one)
 
     def attend(l, j, h):
         rows = rows_of(j)
@@ -372,7 +385,7 @@
     def attn_sum(l, j):
         source = n.X0 if l == 0 else n.Y0
         own = half_of(j, s)
-        middle = source[own, :].astype(F32) + sum_wait(SUM_ATTN[l], j)
+        middle = source[own_of(j), :].astype(F32) + sum_wait(SUM_ATTN[l], j)
         n.MID[l, own_of(j), :] = middle
         unit, _ = unit_rows(middle)
         n.N2[l, own, :] = (unit * n.GAINS[2 * l + 1 : 2 * l + 2, :]).astype(BF16)
@@ -386,25 +399,30 @@
             pre = nn(n.N2[l, rows, :], n.W[l, 1, :, here])
             n.PRE[l, rows, here] = pre.astype(BF16)
             n.HID[rows, here] = gelu_parts(pre)[0].astype(BF16)
-
-    def down_product(l, j):
-        rows = rows_of(j)
         for i in range(tiles):
             here = slice(i * TILE, (i + 1) * TILE)
             n.PART[1, rows, here] = nt(n.HID[rows, :], n.W[l, 2, here, :]).astype(BF16)
         sum_start(SUM_MLP[l], j)
 
     def mlp_sum(l, j):
-        result = n.MID[l, own_of(j), :] + sum_wait(SUM_MLP[l], j)
         if l == 0:
-            n.Y0[half_of(j, s), :] = result.astype(BF16)
-            pair_start(PAIR_MIDDLE, n.Y0, j)
+            result = (n.MID[l, own_of(j), :] + sum_wait(SUM_MLP[l], j)).astype(BF16)
+            n.Y0[own_of(j), :] = result
+            norm_first(1, result.astype(F32), j)
+            give_out(2, 0, n.Y0.at[own_of(j)], n.acts, j)
         else:
-            n.PART[1, half_of(j, s), :] = result.astype(BF16)
-            last_out(0, 1, n.acts, j)
-
-    def last_out(which, section, out, j):
-        here = n.PART.at[1, half_of(j, s)]
+
+            @pl.when(lax.rem(j, 2) == x)
+            def _():
+                result = n.MID[l, own_of(j), :] + sum_wait(SUM_MLP[l], j)
+                n.PART[1, half_of(j, s), :] = result.astype(BF16)
+                give_out(0, 1, n.PART.at[1, half_of(j, s)], n.acts, j)
+
+            @pl.when(lax.rem(j, 2) != x)
+            def _():
+                sum_sent(SUM_MLP[l], j)
+
+    def give_out(which, section, here, out, j):
         target = out.at[y, half_of(0, s)]
 
         @pl.when((s == section) & (t == j))
@@ -423,12 +441,12 @@
                 (section, j, z),
             ).start()
 
-    def last_out_sent(which, section, j):
+    def given_out(which, section, j):
         @pl.when((lax.rem(j, 2) == x) & ((s != section) | (t != j)))
         def _():
             done(bytes_of(part), n.out_send.at[which, j])
 
-    def last_out_done(which, section, out):
+    def got_out(which, section):
         @pl.when(s == section)
         def _():
             for m in range(2):
@@ -438,31 +456,10 @@
                     def _():
                         done(bytes_of(part), n.out_recv.at[which, m, c])
 
-    def full_out(which, section, ref, out):
-        @pl.when(s == section)
-        def _():
-            pltpu.make_async_copy(
-                ref.at[rows_of(t)], out.at[y], n.full_recv.at[which, y]
-            ).start()
-            remote(
-                ref.at[rows_of(t_y)],
-                out.at[y],
-                n.full_send.at[which],
-                n.full_recv.at[which, y],
-                peer_y,
-            ).start()
-
-    def full_out_done(which, section):
-        @pl.when(s == section)
-        def _():
-            done(bytes_of(chunk), n.full_recv.at[which, 0])
-            done(bytes_of(chunk), n.full_recv.at[which, 1])
-            done(bytes_of(chunk), n.full_send.at[which])
-
     def hidden_back(l, j):
         rows = rows_of(j)
         if l == 1:
-            spread_wait(1, n.CT, j)
+            cotangent_wait(j)
         else:
             pair_wait(PAIR_DR, j)
         source = n.CT if l == 1 else n.DR
@@ -472,9 +469,6 @@
             hidden, slope = gelu_parts(n.PRE[l, rows, here].astype(F32))
             n.HID[rows, here] = hidden.astype(BF16)
             n.DPRE[rows, here] = (slope * back).astype(BF16)
-
-    def up_back(l, j):
-        rows = rows_of(j)
         for i in range(tiles):
             here = slice(i * TILE, (i + 1) * TILE)
             n.PART[0, rows, here] = nt(n.DPRE[rows, :], n.W[l, 1, here, :]).astype(BF16)
@@ -545,7 +539,7 @@
             n.DQKV[rows, 2 * h * HEAD : 2 * (h + 1) * HEAD] = n.DKV[h, rows, :].astype(BF16)
         n.DQKV[rows, q_columns:] = turned.astype(BF16)
         if l == 1:
-            last_out_sent(0, 1, j)
+            given_out(0, 1, j)
         for i in range(tiles):
             here = slice(i * TILE, (i + 1) * TILE)
             n.PART[1, rows, here] = nt(n.DQKV[rows, :], n.W[l, 0, here, 0:o_columns]).astype(
@@ -553,20 +547,30 @@
             )
         sum_start(SUM_DATTN[l], j)
 
-    def attn_back_sum(l, j):
+    def attn_back_result(l, j):
         total = sum_wait(SUM_DATTN[l], j)
         source = n.X0 if l == 0 else n.Y0
-        own = half_of(j, s)
-        unit, scale = unit_rows(source[own, :].astype(F32))
+        unit, scale = unit_rows(source[own_of(j), :].astype(F32))
         n.GACC[l, 0:1, :] += jnp.sum(total * unit, axis=0, keepdims=True)
         gain = n.GAINS[2 * l : 2 * l + 1, :]
-        result = n.DMID[own_of(j), :] + norm_back(unit, scale, gain, total)
+        return n.DMID[own_of(j), :] + norm_back(unit, scale, gain, total)
+
+    def attn_back_sum(l, j):
+        own = half_of(j, s)
         if l == 1:
-            n.DR[own, :] = result.astype(BF16)
+            n.DR[own, :] = attn_back_result(l, j).astype(BF16)
             pair_start(PAIR_DR, n.DR, j)
+            give_out(3, 1, n.DR.at[own], n.igr, j)
         else:
-            n.PART[1, own, :] = result.astype(BF16)
-            last_out(1, 0, n.igr, j)
+
+            @pl.when(lax.rem(j, 2) == x)
+            def _():
+                n.PART[1, own, :] = attn_back_result(l, j).astype(BF16)
+                give_out(1, 0, n.PART.at[1, own], n.igr, j)
+
+            @pl.when(lax.rem(j, 2) != x)
+            def _():
+                sum_sent(SUM_DATTN[l], j)
 
     long = width // 2
     grad_order = ((1, 2), (1, 1), (1, 0), (0, 2), (0, 1), (0, 0))
@@ -725,31 +729,44 @@
                         c, far, k : k + 1, 0:slab
                     ]
 
-    def gain_grads():
+    def gain_grads(step):
+        if not inside:
+            return
+        if step == 0:
+            remote(n.GACC.at[1 - s], n.GC, n.gg_send.at[0], n.gg_recv.at[0], mate).start()
+        elif step == 1:
+            done(n.GC, n.gg_recv.at[0])
+            n.GACC[s] += n.GC[...]
+            remote(n.GACC.at[s], n.GX, n.gg_send.at[6], n.gg_recv.at[4], peer_x).start()
+        elif step == 2:
+            done(n.GX, n.gg_recv.at[4])
+            done(n.GX, n.gg_send.at[6])
+            row = lax.broadcasted_iota(jnp.int32, n.GX.shape, 0)
+            n.GACC[s] += jnp.where((row == 0) & (s == 0), n.GX[...], 0.0)
+            remote(n.GACC.at[s], n.GY, n.gg_send.at[1], n.gg_recv.at[1], peer_y).start()
+        else:
+            done(n.GY, n.gg_recv.at[1])
+            n.GC[...] = n.GACC[s] + n.GY[...]
+            for far in range(depth):
+
+                @pl.when(z != far)
+                def _():
+                    slot = slot_of(z, far)
+                    remote(
+                        n.GC,
+                        n.GZ.at[slot],
+                        n.gg_send.at[2 + far],
+                        n.gg_recv.at[5 + slot],
+                        (s, t, far),
+                    ).start()
+
+    def gain_grads_done():
         if not inside:
             n.gain_out[...] = jnp.concatenate([n.GACC[0, 0:2], n.GACC[1, 0:2], n.GACC[0, 4:8]])
             return
-        remote(n.GACC.at[1 - s], n.GC, n.gg_send.at[0], n.gg_recv.at[0], mate).start()
-        done(n.GC, n.gg_recv.at[0])
-        n.GACC[s] += n.GC[...]
-        remote(n.GACC.at[s], n.GY, n.gg_send.at[1], n.gg_recv.at[1], peer_y).start()
-        done(n.GY, n.gg_recv.at[1])
-        n.GC[...] = n.GACC[s] + n.GY[...]
-        for far in range(depth):
-
-            @pl.when(z != far)
-            def _():
-                slot = slot_of(z, far)
-                remote(
-                    n.GC, n.GZ.at[slot], n.gg_send.at[2 + far], n.gg_recv.at[2 + slot], (s, t, far)
-                ).start()
-
-    def gain_grads_done():
-        if not inside:
-            return
         total = n.GC[...]
         for slot in range(depth - 1):
-            done(n.GZ.at[slot], n.gg_recv.at[2 + slot])
+            done(n.GZ.at[slot], n.gg_recv.at[5 + slot])
             total = total + n.GZ[slot]
         n.gain_out[...] = total
         done(n.GC, n.gg_send.at[0])
@@ -762,43 +779,41 @@
 
     tasks = {"none": lambda h, j: None}
     for l in range(2):
-        tasks[f"nq{l}"] = lambda h, j, l=l: norm_qkv(l, j)
-        tasks[f"at{l}"] = lambda h, j, l=l: attend(l, j, h)
+        tasks[f"nq{l}"] = lambda h, j, l=l: qkv_product(l, j)
+        tasks[f"at{l}"] = lambda h, j, l=l: heads_loop(attend, l, j, h)
         tasks[f"op{l}"] = lambda h, j, l=l: out_product(l, j)
         tasks[f"sa{l}"] = lambda h, j, l=l: attn_sum(l, j)
-        tasks[f"up{l}"] = lambda h, j, l=l: up_product(l, j)
-        tasks[f"dn{l}"] = lambda h, j, l=l: down_product(l, j)
+        tasks[f"ud{l}"] = lambda h, j, l=l: up_product(l, j)
         tasks[f"sm{l}"] = lambda h, j, l=l: mlp_sum(l, j)
-        tasks[f"hb{l}"] = lambda h, j, l=l: hidden_back(l, j)
-        tasks[f"ub{l}"] = lambda h, j, l=l: up_back(l, j)
+        tasks[f"hu{l}"] = lambda h, j, l=l: hidden_back(l, j)
         tasks[f"sd{l}"] = lambda h, j, l=l: mlp_back_sum(l, j)
         tasks[f"ag{l}"] = lambda h, j, l=l: attn_grad(l, j)
-        tasks[f"ab{l}"] = lambda h, j, l=l: attend_back(l, j, h)
+        tasks[f"ab{l}"] = lambda h, j, l=l: heads_loop(attend_back, l, j, h)
         tasks[f"qb{l}"] = lambda h, j, l=l: qkv_back(l, j)
         tasks[f"sb{l}"] = lambda h, j, l=l: attn_back_sum(l, j)
         for p in range(PARTS):
             tasks[f"wg{l}{p}"] = lambda h, j, l=l, p=p: weight_grad(l, p, j)
     for p in range(PARTS):
         tasks[f"ws{p}"] = lambda h, j, p=p: weights_send(1, p)
+        tasks[f"wt{p}"] = lambda h, j, p=p: weights_send(0, p)
     tasks["r"] = lambda h, j: sum_pass(h, j)
-    tasks["x0"] = lambda h, j: spread_pass(0, n.X0, j)
-    tasks["x1"] = lambda h, j: spread_pass(1, n.CT, j)
-    tasks["wr"] = lambda h, j: weights_relay(h, j)
+    tasks["x0"] = lambda h, j: inputs_pass(j)
+    tasks["x1"] = lambda h, j: cotangent_pass(j)
+    tasks["wr"] = lambda h, j: weights_relay(lax.div(h, PARTS), lax.rem(h, PARTS), j)
     tasks["ww"] = lambda h, j: weights_wait(h, j)
     tasks["gp"] = lambda h, j: grad_pass(lax.div(j, 2), h, lax.rem(j, 2))
     tasks["gf"] = lambda h, j: grad_final(j, h)
-    tasks["fy"] = lambda h, j: full_out(0, 0, n.Y0, n.acts)
-    tasks["fd"] = lambda h, j: full_out(1, 1, n.DR, n.igr)
+    for step in range(4):
+        tasks[f"gg{step}"] = lambda h, j, step=step: gain_grads(step)
     tasks["gw"] = lambda h, j: gains_wait()
     tasks["cs"] = lambda h, j: spread(1, n.cot, n.CT)
-    order = list(tasks)
+    used = {"none"} | {name for name, _, _ in steps}
+    order = [name for name in tasks if name in used]
     run = [tasks[name] for name in order]
 
     weights_send(0, 0)
     gains_send()
     spread(0, n.inp, n.X0)
-    weights_send(0, 1)
-    weights_send(0, 2)
     n.GACC[...] = jnp.zeros_like(n.GACC)
 
     group = 12
@@ -807,12 +822,6 @@
     pairs = [codes[i] + 4096 * codes[i + 1] for i in range(0, len(codes), 2)]
     per_group = group // 2
     groups = len(pairs) // per_group
-
-    def pick(index, values):
-        value = values[0]
-        for at in range(1, len(values)):
-            value = jnp.where(index == at, values[at], value)
-        return value
 
     def dispatch(low, high, op, h, j):
         if high - low == 1:
@@ -839,8 +848,6 @@
                 0, len(run), lax.div(code, 32), lax.rem(lax.div(code, 4), 8), lax.rem(code, 4)
             )
 
-    gain_grads()
-
     if inside:
         for p in range(PARTS):
             weights_sent(p)
@@ -856,58 +863,56 @@
 
     @pl.loop(0, CHUNKS)
     def _(j):
-        for stage in range(6):
+        for stage in range(7):
             done(bytes_of(part), n.pair_send.at[stage, j])
-        last_out_sent(1, 0, j)
-
-    full_out_done(0, 0)
-    full_out_done(1, 1)
-    last_out_done(0, 1, n.acts)
-    last_out_done(1, 0, n.igr)
+        for which, section in ((1, 0), (2, 0), (3, 1)):
+            given_out(which, section, j)
+
+    for which, section in ((0, 1), (1, 0), (2, 0), (3, 1)):
+        got_out(which, section)
     grads_done()
     gain_grads_done()
 
 
 STEPS = (
-    ("x0", 0, 3), ("gw", 0, 0), ("cs", 0, 0), ("x0", 0, 0), ("x0", 0, 1), ("x0", 0, 2),
-    ("wr", 0, 0), ("ww", 0, 0), ("ws0", 0, 0), ("nq0", 0, 0), ("at0", 0, 0), ("at0", 2, 0),
-    ("at0", 1, 0), ("nq0", 0, 3), ("nq0", 0, 1), ("wr", 0, 1), ("op0", 0, 0), ("at0", 2, 1),
-    ("at0", 1, 1), ("nq0", 0, 2), ("x1", 0, 3), ("at0", 0, 1), ("at0", 0, 2), ("r", 0, 0),
-    ("wr", 0, 2), ("op0", 0, 1), ("at0", 2, 2), ("ws1", 0, 0), ("at0", 1, 2), ("r", 0, 1),
-    ("at0", 1, 3), ("at0", 0, 3), ("ww", 0, 1), ("op0", 0, 2), ("sa0", 0, 0), ("x1", 0, 0),
-    ("sa0", 0, 1), ("r", 0, 2), ("up0", 0, 0), ("wr", 1, 0), ("up0", 0, 1), ("ww", 0, 2),
-    ("dn0", 0, 0), ("r", 1, 0), ("dn0", 0, 1), ("ws2", 0, 0), ("r", 1, 1), ("at0", 2, 3),
-    ("sa0", 0, 2), ("op0", 0, 3), ("up0", 0, 2), ("r", 0, 3), ("dn0", 0, 2), ("sm0", 0, 0),
-    ("wr", 1, 1), ("x1", 0, 1), ("ww", 1, 0), ("sm0", 0, 1), ("nq1", 0, 0), ("r", 1, 2),
-    ("sa0", 0, 3), ("at1", 0, 0), ("at1", 1, 0), ("up0", 0, 3), ("at1", 2, 0), ("dn0", 0, 3),
-    ("nq1", 0, 1), ("at1", 0, 1), ("r", 1, 3), ("sm0", 0, 2), ("op1", 0, 0), ("at1", 1, 1),
-    ("at1", 2, 1), ("nq1", 0, 2), ("op1", 0, 1), ("r", 2, 0), ("at1", 0, 2), ("at1", 2, 2),
-    ("sm0", 0, 3), ("wr", 1, 2), ("x1", 0, 2), ("at1", 1, 2), ("r", 2, 1), ("op1", 0, 2),
-    ("ww", 1, 1), ("nq1", 0, 3), ("at1", 2, 3), ("sa1", 0, 0), ("r", 2, 2), ("at1", 1, 3),
-    ("at1", 0, 3), ("op1", 0, 3), ("sa1", 0, 1), ("up1", 0, 0), ("r", 2, 3), ("sa1", 0, 2),
-    ("ww", 1, 2), ("dn1", 0, 0), ("r", 3, 0), ("up1", 0, 1), ("sa1", 0, 3), ("dn1", 0, 1),
-    ("fy", 0, 0), ("r", 3, 1), ("up1", 0, 2), ("dn1", 0, 2), ("up1", 0, 3), ("hb1", 0, 2),
-    ("hb1", 0, 0), ("dn1", 0, 3), ("sm1", 0, 0), ("r", 3, 3), ("hb1", 0, 3), ("ub1", 0, 3),
-    ("hb1", 0, 1), ("wg12", 0, 1), ("r", 3, 2), ("ub1", 0, 1), ("sm1", 0, 3), ("r", 4, 3),
-    ("ub1", 0, 2), ("sm1", 0, 2), ("sm1", 0, 1), ("ub1", 0, 0), ("r", 4, 2), ("wg11", 0, 1),
-    ("sd1", 0, 3), ("r", 4, 0), ("wg12", 0, 0), ("ag1", 0, 3), ("ab1", 1, 3), ("ab1", 2, 3),
-    ("sd1", 0, 2), ("r", 4, 1), ("ab1", 0, 3), ("qb1", 0, 3), ("ag1", 0, 2), ("sd1", 0, 0),
-    ("ab1", 0, 2), ("ab1", 1, 2), ("r", 5, 3), ("sd1", 0, 1), ("ab1", 2, 2), ("qb1", 0, 2),
-    ("ag1", 0, 1), ("ab1", 2, 1), ("r", 5, 2), ("wg11", 0, 0), ("gp", 1, 3), ("ab1", 0, 1),
-    ("gp", 2, 2), ("ab1", 1, 1), ("qb1", 0, 1), ("ag1", 0, 0), ("ab1", 1, 0), ("ab1", 0, 0),
-    ("r", 5, 1), ("ab1", 2, 0), ("sb1", 0, 3), ("qb1", 0, 0), ("wg10", 0, 0), ("sb1", 0, 2),
-    ("hb0", 0, 3), ("r", 5, 0), ("gp", 1, 2), ("ub0", 0, 3), ("sb1", 0, 1), ("r", 6, 3),
-    ("hb0", 0, 2), ("ub0", 0, 2), ("wg10", 0, 1), ("hb0", 0, 1), ("ub0", 0, 1), ("r", 6, 2),
-    ("gp", 2, 3), ("sb1", 0, 0), ("sd0", 0, 3), ("r", 6, 1), ("hb0", 0, 0), ("wg02", 0, 0),
-    ("ag0", 0, 3), ("gp", 0, 3), ("sd0", 0, 2), ("wg02", 0, 1), ("gp", 0, 2), ("ab0", 1, 3),
-    ("ab0", 0, 3), ("gf", 2, 1), ("ab0", 2, 3), ("qb0", 0, 3), ("ag0", 0, 2), ("sd0", 0, 1),
-    ("ub0", 0, 0), ("ab0", 0, 2), ("wg01", 0, 0), ("gp", 2, 0), ("r", 6, 0), ("ab0", 2, 2),
-    ("ab0", 1, 2), ("qb0", 0, 2), ("ag0", 0, 1), ("gp", 2, 1), ("wg01", 0, 1), ("ab0", 1, 1),
-    ("ab0", 2, 1), ("ab0", 0, 1), ("qb0", 0, 1), ("gp", 1, 0), ("sd0", 0, 0), ("ag0", 0, 0),
-    ("r", 7, 1), ("gf", 0, 1), ("ab0", 0, 0), ("ab0", 2, 0), ("ab0", 1, 0), ("qb0", 0, 0),
-    ("r", 7, 2), ("wg00", 0, 0), ("r", 7, 3), ("r", 7, 0), ("gp", 1, 1), ("sb0", 0, 1),
-    ("gf", 1, 1), ("wg00", 0, 1), ("gp", 0, 0), ("sb0", 0, 3), ("gp", 0, 1), ("sb0", 0, 2),
-    ("gf", 1, 0), ("fd", 0, 0), ("gf", 2, 0), ("sb0", 0, 0), ("gf", 0, 0),
+    ("cs", 0, 0), ("wt1", 0, 0), ("wr", 0, 1), ("wt2", 0, 0), ("wr", 0, 3), ("wr", 0, 0),
+    ("wr", 0, 2), ("gw", 0, 0), ("wr", 1, 0), ("wr", 1, 1), ("x0", 0, 2), ("ww", 0, 0),
+    ("x0", 0, 1), ("x0", 0, 0), ("x0", 0, 3), ("nq0", 0, 2), ("nq0", 0, 0), ("nq0", 0, 1),
+    ("wr", 2, 0), ("nq0", 0, 3), ("at0", 0, 2), ("ws0", 0, 0), ("at0", 3, 1), ("wr", 2, 2),
+    ("op0", 0, 1), ("at0", 1, 2), ("at0", 2, 2), ("wr", 1, 3), ("at0", 0, 3), ("r", 0, 1),
+    ("wr", 2, 1), ("at0", 3, 0), ("at0", 1, 3), ("op0", 0, 2), ("wr", 2, 3), ("wr", 1, 2),
+    ("ws2", 0, 0), ("op0", 0, 0), ("ws1", 0, 0), ("at0", 2, 3), ("r", 0, 0), ("ww", 0, 1),
+    ("r", 0, 2), ("op0", 0, 3), ("sa0", 0, 1), ("wr", 3, 0), ("sa0", 0, 0), ("ww", 0, 2),
+    ("wr", 3, 2), ("r", 0, 3), ("wr", 4, 0), ("x1", 0, 3), ("ud0", 0, 1), ("sa0", 0, 2),
+    ("wr", 3, 3), ("r", 1, 1), ("ud0", 0, 0), ("sa0", 0, 3), ("r", 1, 0), ("wr", 3, 1),
+    ("wr", 5, 2), ("ud0", 0, 3), ("sm0", 0, 1), ("ud0", 0, 2), ("wr", 5, 0), ("r", 1, 2),
+    ("x1", 0, 2), ("ww", 1, 0), ("sm0", 0, 0), ("nq1", 0, 1), ("nq1", 0, 0), ("sm0", 0, 2),
+    ("x1", 0, 1), ("r", 1, 3), ("at1", 3, 0), ("op1", 0, 0), ("wr", 4, 1), ("wr", 5, 1),
+    ("at1", 3, 1), ("nq1", 0, 2), ("r", 2, 0), ("at1", 1, 2), ("at1", 0, 2), ("wr", 5, 3),
+    ("op1", 0, 1), ("sm0", 0, 3), ("at1", 2, 2), ("op1", 0, 2), ("wr", 4, 2), ("r", 2, 1),
+    ("nq1", 0, 3), ("r", 2, 2), ("x1", 0, 0), ("at1", 2, 3), ("wr", 4, 3), ("at1", 0, 3),
+    ("at1", 1, 3), ("sa1", 0, 0), ("sa1", 0, 1), ("op1", 0, 3), ("r", 2, 3), ("ww", 1, 2),
+    ("ww", 1, 1), ("ud1", 0, 1), ("sa1", 0, 2), ("r", 3, 1), ("ud1", 0, 2), ("ud1", 0, 0),
+    ("sa1", 0, 3), ("r", 3, 2), ("hu1", 0, 0), ("ud1", 0, 3), ("hu1", 0, 2), ("r", 3, 3),
+    ("sm1", 0, 2), ("hu1", 0, 3), ("sm1", 0, 3), ("r", 4, 3), ("r", 3, 0), ("hu1", 0, 1),
+    ("wg12", 0, 1), ("sm1", 0, 1), ("r", 4, 2), ("r", 4, 1), ("wg12", 0, 0), ("sd1", 0, 3),
+    ("ag1", 0, 3), ("ab1", 2, 3), ("ab1", 1, 3), ("ab1", 0, 3), ("sd1", 0, 2), ("qb1", 0, 3),
+    ("wg11", 0, 1), ("ag1", 0, 2), ("r", 5, 3), ("wg11", 0, 0), ("ab1", 2, 2), ("gp", 2, 2),
+    ("ab1", 1, 2), ("ab1", 0, 2), ("sm1", 0, 0), ("r", 4, 0), ("qb1", 0, 2), ("sb1", 0, 3),
+    ("r", 5, 2), ("gp", 2, 3), ("hu0", 0, 3), ("gp", 1, 3), ("sd1", 0, 1), ("r", 6, 3),
+    ("sd1", 0, 0), ("ag1", 0, 1), ("ab1", 3, 1), ("qb1", 0, 1), ("ag1", 0, 0), ("ab1", 3, 0),
+    ("qb1", 0, 0), ("gp", 1, 2), ("wg10", 0, 0), ("r", 5, 1), ("sd0", 0, 3), ("sb1", 0, 2),
+    ("wg10", 0, 1), ("ag0", 0, 3), ("r", 5, 0), ("ab0", 0, 3), ("hu0", 0, 2), ("sb1", 0, 1),
+    ("ab0", 1, 3), ("r", 6, 2), ("sb1", 0, 0), ("gp", 0, 2), ("ab0", 2, 3), ("hu0", 0, 0),
+    ("sd0", 0, 2), ("hu0", 0, 1), ("wg02", 0, 0), ("qb0", 0, 3), ("gp", 0, 3), ("wg02", 0, 1),
+    ("r", 6, 1), ("wg01", 0, 0), ("ag0", 0, 2), ("r", 7, 3), ("ab0", 0, 2), ("sd0", 0, 1),
+    ("r", 6, 0), ("ab0", 1, 2), ("ab0", 2, 2), ("gp", 2, 0), ("qb0", 0, 2), ("wg01", 0, 1),
+    ("ag0", 0, 1), ("sd0", 0, 0), ("gp", 2, 1), ("ab0", 3, 1), ("qb0", 0, 1), ("r", 7, 1),
+    ("ag0", 0, 0), ("gf", 1, 1), ("ab0", 3, 0), ("sb0", 0, 3), ("qb0", 0, 0), ("r", 7, 0),
+    ("wg00", 0, 0), ("gp", 1, 0), ("wg00", 0, 1), ("gf", 2, 0), ("r", 7, 2), ("sb0", 0, 1),
+    ("gf", 2, 1), ("gp", 1, 1), ("gp", 0, 0), ("sb0", 0, 0), ("sb0", 0, 2), ("gg0", 0, 0),
+    ("gg1", 0, 0), ("gg2", 0, 0), ("gp", 0, 1), ("gf", 1, 0), ("gf", 0, 1), ("gg3", 0, 0),
+    ("gf", 0, 0),
 )
 
 
@@ -919,8 +924,8 @@
     vmem, dma = pltpu.VMEM, pltpu.SemaphoreType.DMA
     scratch = dict(
         W=vmem((2, PARTS, width, width), BF16),
-        X0=vmem((rows, width), BF16),
-        Y0=vmem((rows, width), BF16),
+        X0=vmem((CHUNKS * part, width), BF16),
+        Y0=vmem((CHUNKS * part, width), BF16),
         CT=vmem((rows, width), BF16),
         DR=vmem((rows, width), BF16),
         N1=vmem((2, rows, width), BF16),
@@ -945,24 +950,22 @@
         DMID=vmem((CHUNKS * part, width), F32),
         PART=vmem((2, rows, width), BF16),
         RC=vmem((2, CHUNKS, part, width), BF16),
-        RX=vmem((2, CHUNKS, part, width), BF16),
+        RX=vmem((3, CHUNKS, part, width), BF16),
         STG=vmem((2, width // 2, width), BF16),
         GAINS=vmem((8, width), F32),
         GACC=vmem((2, 8, width), F32),
         in_send=dma((2, CHUNKS)),
         in_recv=dma((2, CHUNKS)),
-        mate_send=dma((2, CHUNKS)),
-        mate_recv=dma((2, CHUNKS)),
-        pair_send=dma((6, CHUNKS)),
-        pair_recv=dma((6, CHUNKS)),
+        mate_send=dma((CHUNKS,)),
+        mate_recv=dma((CHUNKS,)),
+        pair_send=dma((7, CHUNKS)),
+        pair_recv=dma((7, CHUNKS)),
         rs_send=dma((8, 2, CHUNKS)),
         rs_recv=dma((8, 2, CHUNKS)),
         w_recv=dma((2, PARTS, depth if inside else 1)),
         stg_send=dma((2, PARTS, 2)),
-        out_send=dma((2, CHUNKS)),
-        out_recv=dma((2, 2, 2)),
-        full_send=dma((2,)),
-        full_recv=dma((2, 2)),
+        out_send=dma((4, CHUNKS)),
+        out_recv=dma((4, 2, 2)),
     )
     outs = dict(
         acts=jax.ShapeDtypeStruct(inputs.shape, BF16), igr=jax.ShapeDtypeStruct(inputs.shape, BF16)
@@ -975,6 +978,7 @@
             FIN=vmem((PARTS, slab, width), F32),
             GIN=vmem((2, depth) + gain_rows.shape, F32),
             GC=vmem((8, width), F32),
+            GX=vmem((8, width), F32),
             GY=vmem((8, width), F32),
             GZ=vmem((depth - 1, 8, width), F32),
             w_send=dma((PARTS, depth)),
@@ -985,8 +989,8 @@
             fin_send=dma((PARTS,)),
             gin_send=dma((2, depth)),
             gin_recv=dma((2, depth)),
-            gg_send=dma((2 + depth,)),
-            gg_recv=dma((1 + depth,)),
+            gg_send=dma((3 + depth,)),
+            gg_recv=dma((4 + depth,)),
         )
         own = dict(own_a=weights[0], own_b=weights[1], own_c=weights[2])
         outs["gsum"] = jax.ShapeDtypeStruct((PARTS, slab, width), F32)
@@ -1023,7 +1027,7 @@
     depth = lax.axis_size("dp")
     y = lax.div(lax.axis_index("tensor"), 2)
     section = lax.axis_index("section")
-    inside = slab % 16 == 0 and depth % 2 == 0
+    inside = slab % 16 == 0 and depth == 4
     split = (slab, heads, HEAD)
     kv = jnp.stack([w_qkv[0, :, 1].reshape(split), w_qkv[0, :, 2].reshape(split)], axis=2)
     own = (
@@ -1072,7 +1076,9 @@
         total = total.astype(F32)
         gain_part = lax.psum(gain_part[:4].reshape(2, 2, width), "section")
         gain_part = lax.dynamic_slice_in_dim(gain_part, section, 1, 0)
-        gain_grads = 0.5 * lax.psum_scatter(
+        first = (section == 0) & (jnp.arange(2) == 0)
+        gain_part = gain_part * jnp.where(first, 1.0, 0.5)[None, :, None]
+        gain_grads = lax.psum_scatter(
             gain_part, ("tensor", "dp"), scatter_dimension=2, tiled=True
         )
     columns = heads * HEAD

time: 290 us -> 256 us (0.88); the launches traced: 285 us -> 254 us
  Pallas kernels: 271 us -> 240 us
    pallas_call x1, Pallas kernels: 271 us -> 240 us  [run_blocks(): pl.pallas_call(functools.partial(block_kernel, inside, STEPS, list(given)...]
where the time goes in v4:
time: 256 us; the launch traced here: 254 us
  Pallas kernels  240 us (94%)
  local copies, waits for them, and re-layouts  10.2 us (4%)
    pallas_call x1, Pallas kernels, run_blocks(): pl.pallas_call(functools.partial(block_kernel, inside, STEPS, list(given)...  240 us

profile of v4, /device:TPU:0, one launch (start us, length us, event | category | flops | bytes accessed | tf_op | source)
XLA Modules:
  0.0 253.7 jit_solution(1229768700401718013)
XLA Ops:
  0.6 0.0 copy-start.3
  0.6 0.0 copy-start.4
  0.7 1.0 copy.22
  1.7 1.0 fusion.1
  2.7 0.1 copy.29
  2.8 0.1 copy.28
  3.0 0.1 copy.23
  3.1 0.8 pad_maximum_fusion.refs_2_
  3.9 0.0 copy-done.3
  3.9 0.6 pad_convert_fusion.refs_5_
  4.5 0.0 copy-done.4
  4.5 0.6 dynamic_slice.6
  5.8 0.6 broadcast_in_dim.19.refs_6_
  6.4 239.8 %blocks.1 = (bf16[2,256,768]{2,1,0:T(8,128)(2,1)}, bf16[2,256,768]{2,1,0:T(8,128)(2,1)}, f32[3,192,768]{2,1,0:T(8,128)}, f32[8,768]{1,0:T(8,128)}) custom-call(bf16[2,256,768]{2,1,0:T(8,128)(2,1)} %refs_0_.1, bf16[2,256,768]{2,1,0:T(8,128)(2,1)} %refs_1_.1, bf16[192,768]{1,0:T(8,128)(2,1)} %pad_maximum_fusion.refs_2_, bf16[192,768]{1,0:T(8,128)(2,1)} %bitcast.47, ...), custom_call_target="tpu_custom_call" | custom-call | flops 27000000512 | bytes 40000000 | tf_op jit(solution)/shard_map/blocks/pallas_call | solution.py:1005
  246.1 0.0 copy-start
  246.2 0.9 slice.36
  247.0 0.6 dynamic-slice_bitcast_fusion
  247.7 1.0 slice.38
  248.6 0.2 copy.24
  248.8 0.1 copy.26
  249.0 0.1 copy.25
  249.1 0.0 copy-done
  249.1 0.1 slice_bitcast_fusion.1
  249.2 0.0 copy-start.2
  249.2 0.9 maximum_bitcast_fusion
  250.1 0.8 copy.27
  250.9 0.0 copy-start.1
  250.9 1.1 slice_bitcast_fusion
  252.0 0.0 copy-done.2
  252.0 0.9 copy.32
  252.8 0.0 copy-done.1
  252.8 0.9 copy.33
  (3 shorter events, 0.1 us)
Async XLA Ops:
  0.6 3.3 %copy-start.3 = (bf16[1,2,192]{2,1,0:T(2,128)(2,1)S(1)}, bf16[1,2,192]{2,1,0:T(2,128)(2,1)}, u32[]{:S(2)}) copy-start(bf16[1,2,192]{2,1,0:T(2,128)(2,1)} %param.10) | copy-start | bytes 2308
  0.6 3.9 %copy-start.4 = (s32[2]{0:T(128)S(1)}, s32[2]{0:T(128)}, u32[]{:S(2)}) copy-start(s32[2]{0:T(128)} %param.9) | copy-start | bytes 28
  246.1 2.9 %copy-start = (f32[3,192,768]{2,1,0:T(8,128)S(1)}, f32[3,192,768]{2,1,0:T(8,128)}, u32[]{:S(2)}) copy-start(f32[3,192,768]{2,1,0:T(8,128)} %get-tuple-element.14) | copy-start | bytes 5308420
  249.2 2.7 %copy-start.2 = (bf16[2,256,768]{2,1,0:T(8,128)(2,1)S(1)}, bf16[2,256,768]{2,1,0:T(8,128)(2,1)}, u32[]{:S(2)}) copy-start(bf16[2,256,768]{2,1,0:T(8,128)(2,1)} %get-tuple-element.11) | copy-start | bytes 2359300
  250.9 2.0 copy-start.1

commit v5 on v4

--- a/solution.py
+++ b/solution.py
@@ -149,6 +149,13 @@
             value = jnp.where(index == at, values[at], value)
         return value
 
+    def not_far(end):
+        if end == 0:
+            return z < depth // 2
+        if end == depth - 1:
+            return z >= depth // 2
+        return z >= 0
+
     def weights_send(l, p):
         if not inside:
             pltpu.make_async_copy(n.w_whole.at[l, p], n.W.at[l, p], n.w_recv.at[l, p, 0]).start()
@@ -164,7 +171,7 @@
                         own, n.W.at[l, p, slab_of(z)], n.w_recv.at[l, p, z]
                     ).start()
 
-                @pl.when(jnp.logical_not(hub & (z == far)))
+                @pl.when(jnp.logical_not(hub & (z == far)) & not_far(far))
                 def _():
                     remote(
                         own,
@@ -178,7 +185,7 @@
         own = (n.own_a, n.own_b, n.own_c)[p]
         for far in range(depth):
 
-            @pl.when(jnp.logical_not(hub & (z == far)))
+            @pl.when(jnp.logical_not(hub & (z == far)) & not_far(far))
             def _():
                 done(own, n.w_send.at[p, far])
 
@@ -189,12 +196,24 @@
         @pl.when(hub)
         def _():
             beside = z + 1 - 2 * lax.rem(z, 2)
-            far = pick(step, [z, beside, lax.rem(z + 2, depth), lax.rem(beside + 2, depth)])
+            low = z < 2
+            far = pick(step, [z, beside, jnp.where(low, 2, 1), jnp.where(low, 3, 0)])
             here = n.W.at[l, p, slab_of(far)]
             done(here, n.w_recv.at[l, p, far])
             remote(
                 here, here, n.relay_send.at[l, p, far], n.w_recv.at[l, p, far], peer_y
             ).start()
+            for place, end in ((1, 0), (2, 3)):
+
+                @pl.when((z == place) & (far >= 2 if place == 1 else far < 2))
+                def _():
+                    remote(
+                        here,
+                        here,
+                        n.onward_send.at[l, p, far],
+                        n.w_recv.at[l, p, far],
+                        (s, t, end),
+                    ).start()
 
     def weights_wait(l, p):
         if not inside:
@@ -206,44 +225,53 @@
             for far in range(depth):
                 done(n.W.at[l, p, slab_of(far)], n.w_recv.at[l, p, far])
 
+    t_x = 2 * y + 1 - x
+    t_far = 2 * (1 - y) + 1 - x
+
+    def landing(which, target, source_t):
+        return target.at[own_of(source_t)] if which == 0 else target.at[half_of(source_t, s)]
+
     def spread(which, source, target):
-        own = target.at[own_of(t)] if which == 0 else target.at[half_of(t, s)]
-        pltpu.make_async_copy(
-            source.at[y, half_of(0, s)], own, n.in_recv.at[which, t]
+        here = source.at[y, half_of(0, s)]
+        own = landing(which, target, t)
+        remote(
+            source.at[1 - y, half_of(0, s)],
+            own,
+            n.in_send.at[which, 0],
+            n.in_recv.at[which, t],
+            peer_y,
         ).start()
-        for other in range(CHUNKS):
-
-            @pl.when(t != other)
-            def _():
-                remote(
-                    source.at[other // 2, half_of(0, s)],
-                    own,
-                    n.in_send.at[which, other],
-                    n.in_recv.at[which, t],
-                    (s, other, z),
-                ).start()
+        remote(here, own, n.in_send.at[which, 1], n.in_recv.at[which, t], peer_x).start()
+        pltpu.make_async_copy(here, own, n.in_recv.at[which, t]).start()
+
+    def spread_pass(which, target):
+        near = landing(which, target, t_y)
+        done(near, n.in_recv.at[which, t_y])
+        remote(near, near, n.in_send.at[which, 2], n.in_recv.at[which, t_y], peer_x).start()
+
+    def spread_wait(which, j):
+        @pl.when(j != t_y)
+        def _():
+            done(bytes_of(part), n.in_recv.at[which, j])
 
     def inputs_pass(j):
-        done(bytes_of(part), n.in_recv.at[0, j])
+        spread_wait(0, j)
         norm_first(0, n.X0[own_of(j), :].astype(F32), j)
 
     def cotangent_pass(j):
         here = n.CT.at[half_of(j, s)]
-        done(here, n.in_recv.at[1, j])
+        spread_wait(1, j)
         remote(here, here, n.mate_send.at[j], n.mate_recv.at[j], mate).start()
 
     def cotangent_wait(j):
         done(bytes_of(part), n.mate_recv.at[j])
 
     def spread_done(which):
-        for other in range(CHUNKS):
-
-            @pl.when(t != other)
-            def _():
-                done(bytes_of(part), n.in_send.at[which, other])
-
-            if which == 1:
-                done(bytes_of(part), n.mate_send.at[other])
+        for way in range(3):
+            done(bytes_of(part), n.in_send.at[which, way])
+        if which == 1:
+            for j in range(CHUNKS):
+                done(bytes_of(part), n.mate_send.at[j])
 
     def pair_start(stage, ref, j):
         here = ref.at[half_of(j, s)]
@@ -296,11 +324,10 @@
             sum_sent(stage, j)
         return total
 
-    key_index = lax.broadcasted_iota(jnp.int32, (chunk, chunk), 0)
-    query_index = lax.broadcasted_iota(jnp.int32, (chunk, chunk), 1)
-    causal = key_index <= query_index
-
-    def scores(l, st, i, j, diagonal):
+    first_index = lax.broadcasted_iota(jnp.int32, (chunk, chunk), 0)
+    second_index = lax.broadcasted_iota(jnp.int32, (chunk, chunk), 1)
+
+    def scores(l, st, i, j, diagonal, keys_first):
         if l == 0:
             grown = st * st + 1.0
             inverse = lax.rsqrt(grown)
@@ -309,10 +336,11 @@
         else:
             inverse, magnitude, sign = None, st, None
         if diagonal:
-            magnitude = jnp.where(causal, magnitude, MASKED)
+            seen = first_index <= second_index if keys_first else second_index <= first_index
+            magnitude = jnp.where(seen, magnitude, MASKED)
         else:
             apart = (j >= half) & (i < half)
-            magnitude = magnitude + jnp.where(apart, n.bias[0:1, 0:chunk], 0.0)
+            magnitude = magnitude + jnp.where(apart, n.BIAS[0:1, :], 0.0)
         return inverse, magnitude, sign
 
     def norm_first(l, own_rows, j):
@@ -329,52 +357,51 @@
         for h in range(heads):
             n.KV[l, h, rows, :] = kv_low[:, 2 * h * HEAD : 2 * (h + 1) * HEAD]
             n.KT[l, h, :, rows] = turned[2 * h * HEAD : (2 * h + 1) * HEAD]
-            n.VT[h, :, rows] = turned[(2 * h + 1) * HEAD : (2 * h + 2) * HEAD]
         q = nn(n.N1[l, rows, :], n.W[l, 0, :, q_columns:o_columns]).astype(BF16)
         blank = jnp.zeros((chunk, HEAD), BF16)
         for h in range(heads):
             q_h = q[:, h * HEAD : (h + 1) * HEAD] * jnp.asarray(HEAD**-0.5, BF16)
             n.Q[l, h, rows, :] = jnp.concatenate([q_h, blank], axis=1)
 
-    def heads_loop(task, l, j, h):
-        @pl.loop(jnp.where(h == heads, 0, h), jnp.where(h == heads, heads, h + 1))
-        def _(one):
-            task(l, j, one)
-
-    def attend(l, j, h):
+    def attend(l, j):
         rows = rows_of(j)
-        query = n.Q[l, h, rows, :]
 
         def block(i, carry, diagonal):
-            top, total, out = carry
             keys = rows_of(i)
-            st = nt(n.KV[l, h, keys, :], query)
-            _, magnitude, sign = scores(l, st, i, j, diagonal)
-            new_top = jnp.maximum(top, jnp.max(magnitude, axis=0, keepdims=True))
-            weights = jnp.exp(magnitude - new_top)
-            shrink = jnp.exp(top - new_top)
-            total = total * shrink + jnp.sum(weights, axis=0, keepdims=True)
-            signed = weights if l == 1 else sign * weights
-            out = out * shrink + nn(n.VT[h, :, keys], signed.astype(BF16))
-            return new_top, total, out
+            new = []
+            for h in range(heads):
+                top, total, out = carry[h]
+                kv = n.KV[l, h, keys, :]
+                st = nt(n.Q[l, h, rows, :], kv)
+                _, magnitude, sign = scores(l, st, i, j, diagonal, False)
+                new_top = jnp.maximum(top, jnp.max(magnitude, axis=1, keepdims=True))
+                weights = jnp.exp(magnitude - new_top)
+                shrink = jnp.exp(top - new_top)
+                total = total * shrink + jnp.sum(weights, axis=1, keepdims=True)
+                signed = weights if l == 1 else sign * weights
+                out = out * shrink + nn(signed.astype(BF16), kv)
+                new.append((new_top, total, out))
+            return tuple(new)
 
         carry = (
-            jnp.full((1, chunk), MASKED, F32),
-            jnp.zeros((1, chunk), F32),
-            jnp.zeros((HEAD, chunk), F32),
+            jnp.full((chunk, 1), MASKED, F32),
+            jnp.zeros((chunk, 1), F32),
+            jnp.zeros((chunk, 2 * HEAD), F32),
         )
-        carry = block(j, carry, True)
-        top, total, out = lax.fori_loop(0, j, lambda i, c: block(i, c, False), carry)
-        n.ATTT[l, h, :, rows] = out / total
-        n.LSE[l, h, :, rows] = top + jnp.log(total)
+        carry = block(j, (carry,) * heads, True)
+        carry = lax.fori_loop(0, j, lambda i, c: block(i, c, False), carry)
+        lane = lax.broadcasted_iota(jnp.int32, (chunk, 128), 1)
+        logs = jnp.zeros((chunk, 128), F32)
+        outs = [jnp.zeros((chunk, HEAD), BF16)]
+        for h in range(heads):
+            top, total, out = carry[h]
+            outs.append((out / total)[:, HEAD:].astype(BF16))
+            logs = jnp.where(lane == h, top + jnp.log(total), logs)
+        n.ATT[l, rows, :] = jnp.concatenate(outs, axis=1)
+        n.LSE[l, :, rows] = logs.T[0:8]
 
     def out_product(l, j):
         rows = rows_of(j)
-        joined = jnp.concatenate(
-            [jnp.zeros((HEAD, chunk), F32)] + [n.ATTT[l, h, :, rows] for h in range(heads)],
-            axis=0,
-        )
-        n.ATT[l, rows, :] = joined.T.astype(BF16)
         for i in range(tiles):
             here = slice(i * TILE, (i + 1) * TILE)
             n.PART[0, rows, here] = nt(
@@ -494,43 +521,52 @@
         def _():
             n.DKV[...] = jnp.zeros_like(n.DKV)
 
-        back = nn(n.DA[l, rows, :], n.W[l, 0, :, o_columns - HEAD : width])
-        low = back.astype(BF16)
-        turned = low.astype(F32).T
+        low = nn(n.DA[l, rows, :], n.W[l, 0, :, o_columns - HEAD : width]).astype(BF16)
+        product = low.astype(F32) * n.ATT[l, rows, :].astype(F32)
         blank = jnp.zeros((chunk, HEAD), BF16)
+        lane = lax.broadcasted_iota(jnp.int32, (chunk, 128), 1)
+        inner = jnp.zeros((chunk, 128), F32)
         for h in range(heads):
             here = slice((h + 1) * HEAD, (h + 2) * HEAD)
             n.GRAD[h] = jnp.concatenate([blank, low[:, here]], axis=1)
-            inner = jnp.sum(turned[here] * n.ATTT[l, h, :, rows], axis=0, keepdims=True)
-            n.GRADT[h] = inner
-
-    def attend_back(l, j, h):
+            inner = jnp.where(
+                lane == h, jnp.sum(product[:, here], axis=1, keepdims=True), inner
+            )
+        n.GRADT[...] = inner.T[0:8]
+
+    def attend_back(l, j):
         rows = rows_of(j)
-        query = n.Q[l, h, rows, :]
-        grad = n.GRAD[h]
-        inner = n.GRADT[h]
-        log_total = n.LSE[l, h, :, rows]
-
-        def block(i, query_grad, diagonal):
+
+        def block(i, carry, diagonal):
             keys = rows_of(i)
-            kv = n.KV[l, h, keys, :]
-            st = nt(kv, query)
-            dp = nt(kv, grad)
-            inverse, magnitude, sign = scores(l, st, i, j, diagonal)
-            weights = jnp.exp(magnitude - log_total)
-            if l == 0:
-                signed = sign * weights
-                ds = weights * (sign * (sign * dp - inner) + dp * (inverse * inverse * inverse))
-            else:
-                signed = weights
-                ds = weights * (dp - inner)
-            ds = ds.astype(BF16)
-            n.DKV[h, keys, :] += nn(ds, query) + nn(signed.astype(BF16), grad)
-            return query_grad + nn(n.KT[l, h, :, keys], ds)
-
-        query_grad = block(j, jnp.zeros((HEAD, chunk), F32), True)
+            new = []
+            for h in range(heads):
+                kv = n.KV[l, h, keys, :]
+                st = nt(kv, n.Q[l, h, rows, :])
+                dp = nt(kv, n.GRAD[h])
+                inverse, magnitude, sign = scores(l, st, i, j, diagonal, True)
+                weights = jnp.exp(magnitude - n.LSE[l, h : h + 1, rows])
+                inner = n.GRADT[h : h + 1, :]
+                if l == 0:
+                    signed = sign * weights
+                    ds = weights * (
+                        sign * (sign * dp - inner) + dp * (inverse * inverse * inverse)
+                    )
+                else:
+                    signed = weights
+                    ds = weights * (dp - inner)
+                ds = ds.astype(BF16)
+                n.DKV[h, keys, :] += nn(ds, n.Q[l, h, rows, :]) + nn(
+                    signed.astype(BF16), n.GRAD[h]
+                )
+                new.append(carry[h] + nn(n.KT[l, h, :, keys], ds))
+            return tuple(new)
+
+        blank = jnp.zeros((HEAD, chunk), F32)
+        query_grad = block(j, (blank,) * heads, True)
         query_grad = lax.fori_loop(0, j, lambda i, c: block(i, c, False), query_grad)
-        n.DQT[h] = query_grad * HEAD**-0.5
+        for h in range(heads):
+            n.DQT[h] = query_grad[h] * HEAD**-0.5
 
     def qkv_back(l, j):
         rows = rows_of(j)
@@ -581,25 +617,27 @@
 
     def grad_sent(l, p, i):
         if not inside:
-            done(n.STG.at[i], n.stg_send.at[l, p, i])
+            done(n.STG.at[0], n.stg_send.at[l, p, i])
             return
 
         @pl.when(jnp.logical_not(kept_here(l)))
         def _():
-            done(n.STG.at[i], n.stg_send.at[l, p, i])
+            for k in range(2):
+                done(n.STG.at[0, 0:slab], n.stg_send.at[l, p, 2 * i + k])
 
     def weight_grad(l, p, i):
         at = grad_order.index((l, p))
-        if at > 0:
-            grad_sent(*grad_order[at - 1], i)
+        slot = 2 * (at % 2) + i
+        if at > 1:
+            grad_sent(*grad_order[at - 2], i)
         rows = pl.ds(pl.multiple_of(i * long, long), long)
         if p == 0:
             left = n.N1[l, :, rows]
-            n.STG[i, :, 0:256] = tn(left, n.DQKV[:, 0:256]).astype(BF16)
-            n.STG[i, :, 256:512] = tn(left, n.DQKV[:, 256:512]).astype(BF16)
+            n.STG[slot, :, 0:256] = tn(left, n.DQKV[:, 0:256]).astype(BF16)
+            n.STG[slot, :, 256:512] = tn(left, n.DQKV[:, 256:512]).astype(BF16)
             last = tn(left, n.DQKV[:, 512:o_columns])
             out_part = tn(n.DA[l, :, rows], n.ATT[l])
-            n.STG[i, :, 512:width] = jnp.concatenate([last, out_part[:, HEAD:]], axis=1).astype(
+            n.STG[slot, :, 512:width] = jnp.concatenate([last, out_part[:, HEAD:]], axis=1).astype(
                 BF16
             )
         else:
@@ -609,61 +647,61 @@
                 left, right = (n.CT if l == 1 else n.DR)[:, rows], n.HID
             for k in range(tiles):
                 here = slice(k * TILE, (k + 1) * TILE)
-                n.STG[i, :, here] = tn(left, right[:, here]).astype(BF16)
+                n.STG[slot, :, here] = tn(left, right[:, here]).astype(BF16)
         if not inside:
             pltpu.make_async_copy(
-                n.STG.at[i], n.grads.at[l, p, rows], n.stg_send.at[l, p, i]
+                n.STG.at[slot], n.grads.at[l, p, rows], n.stg_send.at[l, p, i]
             ).start()
             return
 
         @pl.when(kept_here(l))
         def _():
-            n.GR[0, p, rows, :] = n.STG[i]
+            n.GR[0, p, rows, :] = n.STG[slot]
 
         @pl.when(jnp.logical_not(kept_here(l)))
         def _():
             way = jnp.where(hub, 0, 1)
-            remote(
-                n.STG.at[i],
-                n.GR.at[way, p, rows],
-                n.stg_send.at[l, p, i],
-                n.gr_recv.at[way, p, i],
-                (l, grad_to, z),
-            ).start()
+            for k in range(2):
+                k_at = jnp.where(i == 0, k, 1 - k)
+                at_slab = 2 * i + k_at
+                remote(
+                    n.STG.at[slot, slab_of(k_at)],
+                    n.GR.at[way, p, slab_of(at_slab)],
+                    n.stg_send.at[l, p, at_slab],
+                    n.gr_recv.at[way, p, at_slab],
+                    (l, grad_to, z),
+                ).start()
 
     def slot_of(source, target):
         return jnp.where(source > target, source - 1, source)
 
-    def grad_pass(l, p, i):
+    def grad_pass(l, p, far):
         if not inside:
             return
 
         @pl.when(s == l)
         def _():
-            rows = pl.ds(pl.multiple_of(i * long, long), long)
+            here = slab_of(far)
 
             @pl.when(jnp.logical_not(hub))
             def _():
-                done(n.GR.at[0, p, rows], n.gr_recv.at[0, p, i])
-
-            done(n.GR.at[1, p, rows], n.gr_recv.at[1, p, i])
-            for k in range(depth // 2):
-                far = i * (depth // 2) + k
-
-                @pl.when(z != far)
-                def _():
-                    here = slab_of(far)
-                    n.GR[0, p, here, :] = (
-                        n.GR[0, p, here, :].astype(F32) + n.GR[1, p, here, :].astype(F32)
-                    ).astype(BF16)
-                    slot = slot_of(z, far)
-                    remote(
-                        n.GR.at[0, p, here],
-                        n.ZR.at[slot, p],
-                        n.z_send.at[p, far],
-                        n.z_recv.at[p, slot],
-                        (s, t, far),
-                    ).start()
+                done(n.GR.at[0, p, here], n.gr_recv.at[0, p, far])
+
+            done(n.GR.at[1, p, here], n.gr_recv.at[1, p, far])
+
+            @pl.when(z != far)
+            def _():
+                n.GR[0, p, here, :] = (
+                    n.GR[0, p, here, :].astype(F32) + n.GR[1, p, here, :].astype(F32)
+                ).astype(BF16)
+                slot = slot_of(z, far)
+                remote(
+                    n.GR.at[0, p, here],
+                    n.ZR.at[slot, p],
+                    n.z_send.at[p, far],
+                    n.z_recv.at[p, slot],
+                    (s, t, far),
+                ).start()
 
     def grad_final(l, p):
         if not inside:
@@ -676,16 +714,24 @@
             for slot in range(depth - 1):
                 done(n.ZR.at[slot, p], n.z_recv.at[p, slot])
                 total = total + n.ZR[slot, p].astype(F32)
-            n.FIN[p] = total
-            pltpu.make_async_copy(n.FIN.at[p], n.gsum.at[p], n.fin_send.at[p]).start()
+            slot = lax.rem(p, 2)
+
+            @pl.when(p == 0)
+            def _():
+                done(n.FIN.at[0], n.fin_send.at[2])
+
+            n.FIN[slot] = total
+            pltpu.make_async_copy(n.FIN.at[slot], n.gsum.at[p], n.fin_send.at[p]).start()
 
     def grads_done():
         if not inside:
-            grad_sent(*grad_order[-1], 0)
-            grad_sent(*grad_order[-1], 1)
-            return
-        grad_sent(*grad_order[-1], 0)
-        grad_sent(*grad_order[-1], 1)
+            for late in grad_order[-2:]:
+                grad_sent(*late, 0)
+                grad_sent(*late, 1)
+            return
+        for late in grad_order[-2:]:
+            grad_sent(*late, 0)
+            grad_sent(*late, 1)
         for p in range(PARTS):
             for far in range(depth):
 
@@ -693,7 +739,8 @@
                 def _():
                     done(n.ZR.at[0, p], n.z_send.at[p, far])
 
-            done(n.FIN.at[p], n.fin_send.at[p])
+        done(n.FIN.at[0], n.fin_send.at[0])
+        done(n.FIN.at[1], n.fin_send.at[1])
 
     def gains_send():
         if not inside:
@@ -780,7 +827,7 @@
     tasks = {"none": lambda h, j: None}
     for l in range(2):
         tasks[f"nq{l}"] = lambda h, j, l=l: qkv_product(l, j)
-        tasks[f"at{l}"] = lambda h, j, l=l: heads_loop(attend, l, j, h)
+        tasks[f"at{l}"] = lambda h, j, l=l: attend(l, j)
         tasks[f"op{l}"] = lambda h, j, l=l: out_product(l, j)
         tasks[f"sa{l}"] = lambda h, j, l=l: attn_sum(l, j)
         tasks[f"ud{l}"] = lambda h, j, l=l: up_product(l, j)
@@ -788,7 +835,7 @@
         tasks[f"hu{l}"] = lambda h, j, l=l: hidden_back(l, j)
         tasks[f"sd{l}"] = lambda h, j, l=l: mlp_back_sum(l, j)
         tasks[f"ag{l}"] = lambda h, j, l=l: attn_grad(l, j)
-        tasks[f"ab{l}"] = lambda h, j, l=l: heads_loop(attend_back, l, j, h)
+        tasks[f"ab{l}"] = lambda h, j, l=l: attend_back(l, j)
         tasks[f"qb{l}"] = lambda h, j, l=l: qkv_back(l, j)
         tasks[f"sb{l}"] = lambda h, j, l=l: attn_back_sum(l, j)
         for p in range(PARTS):
@@ -801,11 +848,14 @@
     tasks["x1"] = lambda h, j: cotangent_pass(j)
     tasks["wr"] = lambda h, j: weights_relay(lax.div(h, PARTS), lax.rem(h, PARTS), j)
     tasks["ww"] = lambda h, j: weights_wait(h, j)
-    tasks["gp"] = lambda h, j: grad_pass(lax.div(j, 2), h, lax.rem(j, 2))
+    for l in range(2):
+        tasks[f"gp{l}"] = lambda h, j, l=l: grad_pass(l, h, j)
     tasks["gf"] = lambda h, j: grad_final(j, h)
     for step in range(4):
         tasks[f"gg{step}"] = lambda h, j, step=step: gain_grads(step)
     tasks["gw"] = lambda h, j: gains_wait()
+    tasks["xp"] = lambda h, j: spread_pass(0, n.X0)
+    tasks["cp"] = lambda h, j: spread_pass(1, n.CT)
     tasks["cs"] = lambda h, j: spread(1, n.cot, n.CT)
     used = {"none"} | {name for name, _, _ in steps}
     order = [name for name in tasks if name in used]
@@ -815,6 +865,7 @@
     gains_send()
     spread(0, n.inp, n.X0)
     n.GACC[...] = jnp.zeros_like(n.GACC)
+    n.BIAS[...] = jnp.where(n.lengths[y] == rows_all, 0.0, MASKED) + jnp.zeros_like(n.BIAS)
 
     group = 12
     codes = [order.index(name) * 32 + h * 4 + j for name, h, j in steps]
@@ -842,10 +893,14 @@
 
         @pl.loop(0, group)
         def _(i):
-            word = pick(lax.div(i, 2), words)
-            code = jnp.where(lax.rem(i, 2) == 0, lax.rem(word, 4096), lax.div(word, 4096))
+            word = pick(lax.shift_right_logical(i, 1), words)
+            code = jnp.where((i & 1) == 0, word & 4095, lax.shift_right_logical(word, 12))
             dispatch(
-                0, len(run), lax.div(code, 32), lax.rem(lax.div(code, 4), 8), lax.rem(code, 4)
+                0,
+                len(run),
+                lax.shift_right_logical(code, 5),
+                lax.shift_right_logical(code, 2) & 7,
+                code & 3,
             )
 
     if inside:
@@ -857,6 +912,10 @@
                 def _():
                     for far in range(depth):
                         done(n.W.at[l, p, slab_of(far)], n.relay_send.at[l, p, far])
+
+                        @pl.when((z == 1) if far >= 2 else (z == 2))
+                        def _():
+                            done(n.W.at[l, p, slab_of(far)], n.onward_send.at[l, p, far])
 
     spread_done(0)
     spread_done(1)
@@ -875,48 +934,47 @@
 
 
 STEPS = (
-    ("cs", 0, 0), ("wt1", 0, 0), ("wr", 0, 1), ("wt2", 0, 0), ("wr", 0, 3), ("wr", 0, 0),
-    ("wr", 0, 2), ("gw", 0, 0), ("wr", 1, 0), ("wr", 1, 1), ("x0", 0, 2), ("ww", 0, 0),
-    ("x0", 0, 1), ("x0", 0, 0), ("x0", 0, 3), ("nq0", 0, 2), ("nq0", 0, 0), ("nq0", 0, 1),
-    ("wr", 2, 0), ("nq0", 0, 3), ("at0", 0, 2), ("ws0", 0, 0), ("at0", 3, 1), ("wr", 2, 2),
-    ("op0", 0, 1), ("at0", 1, 2), ("at0", 2, 2), ("wr", 1, 3), ("at0", 0, 3), ("r", 0, 1),
-    ("wr", 2, 1), ("at0", 3, 0), ("at0", 1, 3), ("op0", 0, 2), ("wr", 2, 3), ("wr", 1, 2),
-    ("ws2", 0, 0), ("op0", 0, 0), ("ws1", 0, 0), ("at0", 2, 3), ("r", 0, 0), ("ww", 0, 1),
-    ("r", 0, 2), ("op0", 0, 3), ("sa0", 0, 1), ("wr", 3, 0), ("sa0", 0, 0), ("ww", 0, 2),
-    ("wr", 3, 2), ("r", 0, 3), ("wr", 4, 0), ("x1", 0, 3), ("ud0", 0, 1), ("sa0", 0, 2),
-    ("wr", 3, 3), ("r", 1, 1), ("ud0", 0, 0), ("sa0", 0, 3), ("r", 1, 0), ("wr", 3, 1),
-    ("wr", 5, 2), ("ud0", 0, 3), ("sm0", 0, 1), ("ud0", 0, 2), ("wr", 5, 0), ("r", 1, 2),
-    ("x1", 0, 2), ("ww", 1, 0), ("sm0", 0, 0), ("nq1", 0, 1), ("nq1", 0, 0), ("sm0", 0, 2),
-    ("x1", 0, 1), ("r", 1, 3), ("at1", 3, 0), ("op1", 0, 0), ("wr", 4, 1), ("wr", 5, 1),
-    ("at1", 3, 1), ("nq1", 0, 2), ("r", 2, 0), ("at1", 1, 2), ("at1", 0, 2), ("wr", 5, 3),
-    ("op1", 0, 1), ("sm0", 0, 3), ("at1", 2, 2), ("op1", 0, 2), ("wr", 4, 2), ("r", 2, 1),
-    ("nq1", 0, 3), ("r", 2, 2), ("x1", 0, 0), ("at1", 2, 3), ("wr", 4, 3), ("at1", 0, 3),
-    ("at1", 1, 3), ("sa1", 0, 0), ("sa1", 0, 1), ("op1", 0, 3), ("r", 2, 3), ("ww", 1, 2),
-    ("ww", 1, 1), ("ud1", 0, 1), ("sa1", 0, 2), ("r", 3, 1), ("ud1", 0, 2), ("ud1", 0, 0),
-    ("sa1", 0, 3), ("r", 3, 2), ("hu1", 0, 0), ("ud1", 0, 3), ("hu1", 0, 2), ("r", 3, 3),
-    ("sm1", 0, 2), ("hu1", 0, 3), ("sm1", 0, 3), ("r", 4, 3), ("r", 3, 0), ("hu1", 0, 1),
-    ("wg12", 0, 1), ("sm1", 0, 1), ("r", 4, 2), ("r", 4, 1), ("wg12", 0, 0), ("sd1", 0, 3),
-    ("ag1", 0, 3), ("ab1", 2, 3), ("ab1", 1, 3), ("ab1", 0, 3), ("sd1", 0, 2), ("qb1", 0, 3),
-    ("wg11", 0, 1), ("ag1", 0, 2), ("r", 5, 3), ("wg11", 0, 0), ("ab1", 2, 2), ("gp", 2, 2),
-    ("ab1", 1, 2), ("ab1", 0, 2), ("sm1", 0, 0), ("r", 4, 0), ("qb1", 0, 2), ("sb1", 0, 3),
-    ("r", 5, 2), ("gp", 2, 3), ("hu0", 0, 3), ("gp", 1, 3), ("sd1", 0, 1), ("r", 6, 3),
-    ("sd1", 0, 0), ("ag1", 0, 1), ("ab1", 3, 1), ("qb1", 0, 1), ("ag1", 0, 0), ("ab1", 3, 0),
-    ("qb1", 0, 0), ("gp", 1, 2), ("wg10", 0, 0), ("r", 5, 1), ("sd0", 0, 3), ("sb1", 0, 2),
-    ("wg10", 0, 1), ("ag0", 0, 3), ("r", 5, 0), ("ab0", 0, 3), ("hu0", 0, 2), ("sb1", 0, 1),
-    ("ab0", 1, 3), ("r", 6, 2), ("sb1", 0, 0), ("gp", 0, 2), ("ab0", 2, 3), ("hu0", 0, 0),
-    ("sd0", 0, 2), ("hu0", 0, 1), ("wg02", 0, 0), ("qb0", 0, 3), ("gp", 0, 3), ("wg02", 0, 1),
-    ("r", 6, 1), ("wg01", 0, 0), ("ag0", 0, 2), ("r", 7, 3), ("ab0", 0, 2), ("sd0", 0, 1),
-    ("r", 6, 0), ("ab0", 1, 2), ("ab0", 2, 2), ("gp", 2, 0), ("qb0", 0, 2), ("wg01", 0, 1),
-    ("ag0", 0, 1), ("sd0", 0, 0), ("gp", 2, 1), ("ab0", 3, 1), ("qb0", 0, 1), ("r", 7, 1),
-    ("ag0", 0, 0), ("gf", 1, 1), ("ab0", 3, 0), ("sb0", 0, 3), ("qb0", 0, 0), ("r", 7, 0),
-    ("wg00", 0, 0), ("gp", 1, 0), ("wg00", 0, 1), ("gf", 2, 0), ("r", 7, 2), ("sb0", 0, 1),
-    ("gf", 2, 1), ("gp", 1, 1), ("gp", 0, 0), ("sb0", 0, 0), ("sb0", 0, 2), ("gg0", 0, 0),
-    ("gg1", 0, 0), ("gg2", 0, 0), ("gp", 0, 1), ("gf", 1, 0), ("gf", 0, 1), ("gg3", 0, 0),
-    ("gf", 0, 0),
+    ("wr", 0, 0), ("wt1", 0, 0), ("xp", 0, 0), ("wr", 1, 0), ("gw", 0, 0), ("wt2", 0, 0),
+    ("wr", 0, 1), ("x0", 0, 0), ("wr", 0, 3), ("wr", 0, 2), ("x0", 0, 1), ("x0", 0, 3),
+    ("ww", 0, 0), ("nq0", 0, 1), ("cs", 0, 0), ("nq0", 0, 0), ("x0", 0, 2), ("wr", 1, 3),
+    ("at0", 3, 1), ("wr", 2, 0), ("op0", 0, 1), ("ws1", 0, 0), ("ws0", 0, 0), ("wr", 1, 2),
+    ("wr", 2, 2), ("wr", 1, 1), ("cp", 0, 0), ("nq0", 0, 2), ("ws2", 0, 0), ("nq0", 0, 3),
+    ("wr", 2, 1), ("r", 0, 1), ("at0", 3, 3), ("op0", 0, 3), ("at0", 3, 0), ("at0", 3, 2),
+    ("r", 0, 3), ("op0", 0, 0), ("wr", 2, 3), ("sa0", 0, 3), ("wr", 5, 0), ("wr", 3, 2),
+    ("r", 0, 0), ("wr", 3, 0), ("ww", 0, 1), ("wr", 3, 1), ("wr", 3, 3), ("op0", 0, 2),
+    ("sa0", 0, 1), ("wr", 4, 1), ("r", 0, 2), ("wr", 4, 2), ("x1", 0, 3), ("wr", 4, 0),
+    ("x1", 0, 0), ("ww", 0, 2), ("x1", 0, 2), ("ud0", 0, 1), ("r", 1, 1), ("sa0", 0, 0),
+    ("ud0", 0, 0), ("r", 1, 0), ("sa0", 0, 2), ("ud0", 0, 2), ("wr", 5, 3), ("sm0", 0, 1),
+    ("r", 1, 2), ("ud0", 0, 3), ("ww", 1, 0), ("r", 1, 3), ("sm0", 0, 0), ("wr", 5, 2),
+    ("nq1", 0, 0), ("at1", 3, 0), ("wr", 5, 1), ("nq1", 0, 1), ("x1", 0, 1), ("at1", 3, 1),
+    ("sm0", 0, 2), ("op1", 0, 0), ("wr", 4, 3), ("nq1", 0, 2), ("sm0", 0, 3), ("r", 2, 0),
+    ("at1", 3, 2), ("op1", 0, 2), ("nq1", 0, 3), ("r", 2, 2), ("at1", 3, 3), ("op1", 0, 3),
+    ("r", 2, 3), ("sa1", 0, 2), ("op1", 0, 1), ("sa1", 0, 0), ("ww", 1, 2), ("r", 2, 1),
+    ("sa1", 0, 3), ("ww", 1, 1), ("ud1", 0, 2), ("ud1", 0, 3), ("ud1", 0, 0), ("sa1", 0, 1),
+    ("r", 3, 3), ("hu1", 0, 2), ("ud1", 0, 1), ("hu1", 0, 3), ("r", 3, 2), ("hu1", 0, 0),
+    ("sm1", 0, 3), ("r", 4, 3), ("hu1", 0, 1), ("wg12", 0, 0), ("r", 3, 0), ("r", 3, 1),
+    ("sm1", 0, 2), ("wg12", 0, 1), ("r", 4, 2), ("sd1", 0, 3), ("ag1", 0, 3), ("ab1", 3, 3),
+    ("sm1", 0, 1), ("wg11", 0, 0), ("r", 4, 1), ("wg11", 0, 1), ("qb1", 0, 3), ("sd1", 0, 2),
+    ("gp1", 2, 1), ("sm1", 0, 0), ("r", 4, 0), ("ag1", 0, 2), ("ab1", 3, 2), ("sd1", 0, 1),
+    ("gp1", 2, 3), ("qb1", 0, 2), ("r", 5, 3), ("ag1", 0, 1), ("ab1", 3, 1), ("gp1", 1, 0),
+    ("sd1", 0, 0), ("gp1", 2, 0), ("qb1", 0, 1), ("ag1", 0, 0), ("r", 5, 1), ("ab1", 3, 0),
+    ("sb1", 0, 3), ("gp1", 2, 2), ("r", 5, 2), ("qb1", 0, 0), ("gp1", 1, 3), ("wg10", 0, 0),
+    ("hu0", 0, 3), ("r", 5, 0), ("gp1", 1, 2), ("sb1", 0, 1), ("wg10", 0, 1), ("r", 6, 3),
+    ("sb1", 0, 2), ("hu0", 0, 2), ("gp1", 0, 1), ("hu0", 0, 1), ("sb1", 0, 0), ("gp1", 0, 0),
+    ("r", 6, 2), ("hu0", 0, 0), ("wg02", 0, 1), ("sd0", 0, 3), ("gf", 2, 1), ("r", 6, 1),
+    ("gp1", 0, 3), ("ag0", 0, 3), ("wg02", 0, 0), ("ab0", 3, 3), ("gp1", 1, 1), ("gp1", 0, 2),
+    ("qb0", 0, 3), ("gp0", 2, 2), ("gp0", 2, 3), ("sd0", 0, 2), ("wg01", 0, 1), ("r", 6, 0),
+    ("r", 7, 3), ("gp0", 2, 0), ("ag0", 0, 2), ("ab0", 3, 2), ("wg01", 0, 0), ("sd0", 0, 0),
+    ("qb0", 0, 2), ("gp0", 2, 1), ("sd0", 0, 1), ("ag0", 0, 1), ("ab0", 3, 1), ("qb0", 0, 1),
+    ("ag0", 0, 0), ("ab0", 3, 0), ("qb0", 0, 0), ("r", 7, 2), ("wg00", 0, 1), ("gp0", 1, 2),
+    ("gp0", 1, 0), ("r", 7, 1), ("gp0", 1, 1), ("r", 7, 0), ("sb0", 0, 3), ("gf", 0, 1),
+    ("gp0", 1, 3), ("wg00", 0, 0), ("sb0", 0, 0), ("gp0", 0, 2), ("sb0", 0, 1), ("sb0", 0, 2),
+    ("gg0", 0, 0), ("gg1", 0, 0), ("gf", 1, 1), ("gp0", 0, 0), ("gf", 1, 0), ("gf", 2, 0),
+    ("gp0", 0, 1), ("gp0", 0, 3), ("gg2", 0, 0), ("gg3", 0, 0), ("gf", 0, 0),
 )
 
 
-def run_blocks(inputs, cotangent, weights, gain_rows, bias, depth, inside):
+def run_blocks(inputs, cotangent, weights, gain_rows, lengths, depth, inside):
     buckets, chunk, width = inputs.shape
     rows = CHUNKS * chunk
     part = chunk // 2
@@ -933,10 +991,8 @@
         Q=vmem((2, heads, rows, 2 * HEAD), BF16),
         KV=vmem((2, heads, rows, 2 * HEAD), BF16),
         KT=vmem((2, heads, HEAD, rows), BF16),
-        VT=vmem((heads, HEAD, rows), BF16),
         ATT=vmem((2, rows, (heads + 1) * HEAD), BF16),
-        ATTT=vmem((2, heads, HEAD, rows), F32),
-        LSE=vmem((2, heads, 1, rows), F32),
+        LSE=vmem((2, 8, rows), F32),
         PRE=vmem((2, rows, width), BF16),
         HID=vmem((rows, width), BF16),
         DPRE=vmem((rows, width), BF16),
@@ -944,17 +1000,18 @@
         DA=vmem((2, rows, width), BF16),
         DKV=vmem((heads, rows, 2 * HEAD), F32),
         GRAD=vmem((heads, chunk, 2 * HEAD), BF16),
-        GRADT=vmem((heads, 1, chunk), F32),
+        GRADT=vmem((8, chunk), F32),
         DQT=vmem((heads, HEAD, chunk), F32),
         MID=vmem((2, CHUNKS * part, width), F32),
         DMID=vmem((CHUNKS * part, width), F32),
         PART=vmem((2, rows, width), BF16),
         RC=vmem((2, CHUNKS, part, width), BF16),
         RX=vmem((3, CHUNKS, part, width), BF16),
-        STG=vmem((2, width // 2, width), BF16),
+        STG=vmem((4, width // 2, width), BF16),
         GAINS=vmem((8, width), F32),
+        BIAS=vmem((8, chunk), F32),
         GACC=vmem((2, 8, width), F32),
-        in_send=dma((2, CHUNKS)),
+        in_send=dma((2, 3)),
         in_recv=dma((2, CHUNKS)),
         mate_send=dma((CHUNKS,)),
         mate_recv=dma((CHUNKS,)),
@@ -963,7 +1020,7 @@
         rs_send=dma((8, 2, CHUNKS)),
         rs_recv=dma((8, 2, CHUNKS)),
         w_recv=dma((2, PARTS, depth if inside else 1)),
-        stg_send=dma((2, PARTS, 2)),
+        stg_send=dma((2, PARTS, 4)),
         out_send=dma((4, CHUNKS)),
         out_recv=dma((4, 2, 2)),
     )
@@ -975,7 +1032,7 @@
         scratch.update(
             GR=vmem((2, PARTS, width, width), BF16),
             ZR=vmem((depth - 1, PARTS, slab, width), BF16),
-            FIN=vmem((PARTS, slab, width), F32),
+            FIN=vmem((2, slab, width), F32),
             GIN=vmem((2, depth) + gain_rows.shape, F32),
             GC=vmem((8, width), F32),
             GX=vmem((8, width), F32),
@@ -983,7 +1040,8 @@
             GZ=vmem((depth - 1, 8, width), F32),
             w_send=dma((PARTS, depth)),
             relay_send=dma((2, PARTS, depth)),
-            gr_recv=dma((2, PARTS, 2)),
+            onward_send=dma((2, PARTS, depth)),
+            gr_recv=dma((2, PARTS, 4)),
             z_send=dma((PARTS, depth)),
             z_recv=dma((PARTS, depth - 1)),
             fin_send=dma((PARTS,)),
@@ -998,16 +1056,19 @@
         own = dict(w_whole=weights)
         outs["grads"] = jax.ShapeDtypeStruct(weights.shape, BF16)
     outs["gain_out"] = jax.ShapeDtypeStruct((8, width), F32)
-    given = dict(inp=inputs, cot=cotangent, **own, gain_rows=gain_rows, bias=bias)
+    given = dict(inp=inputs, cot=cotangent, **own, gain_rows=gain_rows, lengths=lengths)
     hbm = pl.BlockSpec(memory_space=pl.ANY)
     in_vmem = pl.BlockSpec(memory_space=pltpu.VMEM)
-    small = ("gain_rows", "bias", "gain_out")
+    small = ("gain_rows", "gain_out")
+    in_smem = pl.BlockSpec(memory_space=pltpu.SMEM)
     return pl.pallas_call(
         functools.partial(
             block_kernel, inside, STEPS, list(given) + list(outs) + list(scratch)
         ),
         out_shape=tuple(outs.values()),
-        in_specs=[in_vmem if name in small else hbm for name in given],
+        in_specs=[
+            in_vmem if name in small else in_smem if name == "lengths" else hbm for name in given
+        ],
         out_specs=tuple(in_vmem if name in small else hbm for name in outs),
         scratch_shapes=list(scratch.values()),
         compiler_params=pltpu.CompilerParams(
@@ -1035,13 +1096,11 @@
         w_up[0],
         w_down[0].T,
     )
-    bias = jnp.where(lengths[y] == CHUNKS * local_rows, 0.0, MASKED).astype(F32)
-    bias = jnp.broadcast_to(bias, (8, local_rows))
     axes = ("section", "tensor")
     if inside:
         gain_rows = jnp.pad(gains[0].astype(F32), ((0, 6), (0, -slab % 128)))
         acts, input_grads, total, gain_part = run_blocks(
-            inputs, cotangent, own, gain_rows, bias, depth, inside
+            inputs, cotangent, own, gain_rows, lengths, depth, inside
         )
         gain_part = gain_part[None, :2]
         at = lax.axis_index("tensor") * depth + lax.axis_index("dp")
@@ -1063,7 +1122,7 @@
         gain_rows = lax.all_gather(gain_rows, "section", axis=0, tiled=True)
         gain_rows = jnp.pad(gain_rows.reshape(4, width).astype(F32), ((0, 4), (0, 0)))
         acts, input_grads, partial, gain_part = run_blocks(
-            inputs, cotangent, weights, gain_rows, bias, depth, inside
+            inputs, cotangent, weights, gain_rows, lengths, depth, inside
         )
         total = jnp.zeros(partial.shape[1:], F32)
         for l in range(2):

time: 256 us -> 235 us (0.918)
  Pallas kernels: 240 us -> 222 us
    pallas_call x1, Pallas kernels: 240 us -> 222 us  [run_blocks(): pl.pallas_call(functools.partial(block_kernel, inside, STEPS, list(given)...]
where the time goes in v5:
time: 235 us; the launch traced here: 234 us
  Pallas kernels  222 us (94%)
  local copies, waits for them, and re-layouts  9.02 us (4%)
    pallas_call x1, Pallas kernels, run_blocks(): pl.pallas_call(functools.partial(block_kernel, inside, STEPS, list(given)...  222 us

profile of v5, /device:TPU:0, one launch (start us, length us, event | category | flops | bytes accessed | tf_op | source)
XLA Modules:
  0.0 234.3 jit_solution(2827490869121711062)
XLA Ops:
  0.6 0.0 copy-start.3
  0.6 1.0 copy.22
  1.6 1.0 fusion.1
  2.7 0.1 copy.29
  2.8 0.1 copy.28
  2.9 0.1 copy.23
  3.1 0.8 pad_maximum_fusion.refs_2_
  3.9 0.0 copy-done.3
  3.9 0.6 pad_convert_fusion.refs_5_
  4.5 222.2 %blocks.1 = (bf16[2,256,768]{2,1,0:T(8,128)(2,1)}, bf16[2,256,768]{2,1,0:T(8,128)(2,1)}, f32[3,192,768]{2,1,0:T(8,128)}, f32[8,768]{1,0:T(8,128)}) custom-call(bf16[2,256,768]{2,1,0:T(8,128)(2,1)} %refs_0_.1, bf16[2,256,768]{2,1,0:T(8,128)(2,1)} %refs_1_.1, bf16[192,768]{1,0:T(8,128)(2,1)} %pad_maximum_fusion.refs_2_, bf16[192,768]{1,0:T(8,128)(2,1)} %bitcast.46, ...), custom_call_target="tpu_custom_call" | custom-call | flops 27000000512 | bytes 40000000 | tf_op jit(solution)/shard_map/blocks/pallas_call | solution.py:1064
  226.7 0.0 copy-start
  226.7 0.9 slice.36
  227.6 0.6 dynamic-slice_bitcast_fusion
  228.2 1.0 slice.38
  229.2 0.2 copy.24
  229.4 0.1 copy.26
  229.5 0.1 copy.25
  229.6 0.0 copy-done
  229.6 0.1 slice_bitcast_fusion.1
  229.8 0.0 copy-start.2
  229.8 0.9 maximum_bitcast_fusion
  230.6 0.8 copy.27
  231.4 0.0 copy-start.1
  231.4 1.1 slice_bitcast_fusion
  232.5 0.0 copy-done.2
  232.5 0.9 copy.32
  233.4 0.0 copy-done.1
  233.4 0.9 copy.33
  (3 shorter events, 0.1 us)
Async XLA Ops:
  0.6 3.3 %copy-start.3 = (bf16[1,2,192]{2,1,0:T(2,128)(2,1)S(1)}, bf16[1,2,192]{2,1,0:T(2,128)(2,1)}, u32[]{:S(2)}) copy-start(bf16[1,2,192]{2,1,0:T(2,128)(2,1)} %param.10) | copy-start | bytes 2308
  226.7 2.9 %copy-start = (f32[3,192,768]{2,1,0:T(8,128)S(1)}, f32[3,192,768]{2,1,0:T(8,128)}, u32[]{:S(2)}) copy-start(f32[3,192,768]{2,1,0:T(8,128)} %get-tuple-element.14) | copy-start | bytes 5308420
  229.8 2.7 %copy-start.2 = (bf16[2,256,768]{2,1,0:T(8,128)(2,1)S(1)}, bf16[2,256,768]{2,1,0:T(8,128)(2,1)}, u32[]{:S(2)}) copy-start(bf16[2,256,768]{2,1,0:T(8,128)(2,1)} %get-tuple-element.11) | copy-start | bytes 2359300
  231.4 2.0 copy-start.1

commit v6 on v5

--- a/solution.py
+++ b/solution.py
@@ -934,43 +934,43 @@
 
 
 STEPS = (
-    ("wr", 0, 0), ("wt1", 0, 0), ("xp", 0, 0), ("wr", 1, 0), ("gw", 0, 0), ("wt2", 0, 0),
-    ("wr", 0, 1), ("x0", 0, 0), ("wr", 0, 3), ("wr", 0, 2), ("x0", 0, 1), ("x0", 0, 3),
-    ("ww", 0, 0), ("nq0", 0, 1), ("cs", 0, 0), ("nq0", 0, 0), ("x0", 0, 2), ("wr", 1, 3),
-    ("at0", 3, 1), ("wr", 2, 0), ("op0", 0, 1), ("ws1", 0, 0), ("ws0", 0, 0), ("wr", 1, 2),
-    ("wr", 2, 2), ("wr", 1, 1), ("cp", 0, 0), ("nq0", 0, 2), ("ws2", 0, 0), ("nq0", 0, 3),
-    ("wr", 2, 1), ("r", 0, 1), ("at0", 3, 3), ("op0", 0, 3), ("at0", 3, 0), ("at0", 3, 2),
-    ("r", 0, 3), ("op0", 0, 0), ("wr", 2, 3), ("sa0", 0, 3), ("wr", 5, 0), ("wr", 3, 2),
-    ("r", 0, 0), ("wr", 3, 0), ("ww", 0, 1), ("wr", 3, 1), ("wr", 3, 3), ("op0", 0, 2),
-    ("sa0", 0, 1), ("wr", 4, 1), ("r", 0, 2), ("wr", 4, 2), ("x1", 0, 3), ("wr", 4, 0),
-    ("x1", 0, 0), ("ww", 0, 2), ("x1", 0, 2), ("ud0", 0, 1), ("r", 1, 1), ("sa0", 0, 0),
-    ("ud0", 0, 0), ("r", 1, 0), ("sa0", 0, 2), ("ud0", 0, 2), ("wr", 5, 3), ("sm0", 0, 1),
-    ("r", 1, 2), ("ud0", 0, 3), ("ww", 1, 0), ("r", 1, 3), ("sm0", 0, 0), ("wr", 5, 2),
-    ("nq1", 0, 0), ("at1", 3, 0), ("wr", 5, 1), ("nq1", 0, 1), ("x1", 0, 1), ("at1", 3, 1),
-    ("sm0", 0, 2), ("op1", 0, 0), ("wr", 4, 3), ("nq1", 0, 2), ("sm0", 0, 3), ("r", 2, 0),
-    ("at1", 3, 2), ("op1", 0, 2), ("nq1", 0, 3), ("r", 2, 2), ("at1", 3, 3), ("op1", 0, 3),
-    ("r", 2, 3), ("sa1", 0, 2), ("op1", 0, 1), ("sa1", 0, 0), ("ww", 1, 2), ("r", 2, 1),
-    ("sa1", 0, 3), ("ww", 1, 1), ("ud1", 0, 2), ("ud1", 0, 3), ("ud1", 0, 0), ("sa1", 0, 1),
-    ("r", 3, 3), ("hu1", 0, 2), ("ud1", 0, 1), ("hu1", 0, 3), ("r", 3, 2), ("hu1", 0, 0),
-    ("sm1", 0, 3), ("r", 4, 3), ("hu1", 0, 1), ("wg12", 0, 0), ("r", 3, 0), ("r", 3, 1),
-    ("sm1", 0, 2), ("wg12", 0, 1), ("r", 4, 2), ("sd1", 0, 3), ("ag1", 0, 3), ("ab1", 3, 3),
-    ("sm1", 0, 1), ("wg11", 0, 0), ("r", 4, 1), ("wg11", 0, 1), ("qb1", 0, 3), ("sd1", 0, 2),
-    ("gp1", 2, 1), ("sm1", 0, 0), ("r", 4, 0), ("ag1", 0, 2), ("ab1", 3, 2), ("sd1", 0, 1),
-    ("gp1", 2, 3), ("qb1", 0, 2), ("r", 5, 3), ("ag1", 0, 1), ("ab1", 3, 1), ("gp1", 1, 0),
-    ("sd1", 0, 0), ("gp1", 2, 0), ("qb1", 0, 1), ("ag1", 0, 0), ("r", 5, 1), ("ab1", 3, 0),
-    ("sb1", 0, 3), ("gp1", 2, 2), ("r", 5, 2), ("qb1", 0, 0), ("gp1", 1, 3), ("wg10", 0, 0),
-    ("hu0", 0, 3), ("r", 5, 0), ("gp1", 1, 2), ("sb1", 0, 1), ("wg10", 0, 1), ("r", 6, 3),
-    ("sb1", 0, 2), ("hu0", 0, 2), ("gp1", 0, 1), ("hu0", 0, 1), ("sb1", 0, 0), ("gp1", 0, 0),
-    ("r", 6, 2), ("hu0", 0, 0), ("wg02", 0, 1), ("sd0", 0, 3), ("gf", 2, 1), ("r", 6, 1),
-    ("gp1", 0, 3), ("ag0", 0, 3), ("wg02", 0, 0), ("ab0", 3, 3), ("gp1", 1, 1), ("gp1", 0, 2),
-    ("qb0", 0, 3), ("gp0", 2, 2), ("gp0", 2, 3), ("sd0", 0, 2), ("wg01", 0, 1), ("r", 6, 0),
-    ("r", 7, 3), ("gp0", 2, 0), ("ag0", 0, 2), ("ab0", 3, 2), ("wg01", 0, 0), ("sd0", 0, 0),
-    ("qb0", 0, 2), ("gp0", 2, 1), ("sd0", 0, 1), ("ag0", 0, 1), ("ab0", 3, 1), ("qb0", 0, 1),
-    ("ag0", 0, 0), ("ab0", 3, 0), ("qb0", 0, 0), ("r", 7, 2), ("wg00", 0, 1), ("gp0", 1, 2),
-    ("gp0", 1, 0), ("r", 7, 1), ("gp0", 1, 1), ("r", 7, 0), ("sb0", 0, 3), ("gf", 0, 1),
-    ("gp0", 1, 3), ("wg00", 0, 0), ("sb0", 0, 0), ("gp0", 0, 2), ("sb0", 0, 1), ("sb0", 0, 2),
-    ("gg0", 0, 0), ("gg1", 0, 0), ("gf", 1, 1), ("gp0", 0, 0), ("gf", 1, 0), ("gf", 2, 0),
-    ("gp0", 0, 1), ("gp0", 0, 3), ("gg2", 0, 0), ("gg3", 0, 0), ("gf", 0, 0),
+    ("cs", 0, 0), ("wt2", 0, 0), ("wt1", 0, 0), ("wr", 0, 0), ("xp", 0, 0), ("wr", 0, 1),
+    ("wr", 0, 2), ("gw", 0, 0), ("wr", 0, 3), ("x0", 0, 0), ("x0", 0, 1), ("wr", 2, 2),
+    ("x0", 0, 2), ("wr", 2, 0), ("cp", 0, 0), ("wr", 2, 1), ("ww", 0, 0), ("nq0", 0, 1),
+    ("nq0", 0, 0), ("at0", 3, 1), ("nq0", 0, 2), ("op0", 0, 1), ("wr", 1, 2), ("x0", 0, 3),
+    ("x1", 0, 3), ("at0", 3, 2), ("wr", 1, 0), ("wr", 1, 1), ("wr", 1, 3), ("op0", 0, 2),
+    ("ws0", 0, 0), ("at0", 3, 0), ("op0", 0, 0), ("nq0", 0, 3), ("wr", 2, 3), ("r", 0, 1),
+    ("r", 0, 2), ("r", 0, 0), ("at0", 3, 3), ("ws2", 0, 0), ("op0", 0, 3), ("wr", 3, 2),
+    ("wr", 3, 0), ("ws1", 0, 0), ("sa0", 0, 1), ("sa0", 0, 0), ("x1", 0, 0), ("ww", 0, 1),
+    ("wr", 3, 1), ("r", 0, 3), ("ww", 0, 2), ("ud0", 0, 0), ("wr", 3, 3), ("ud0", 0, 1),
+    ("r", 1, 0), ("sa0", 0, 3), ("wr", 4, 2), ("ud0", 0, 3), ("r", 1, 1), ("wr", 5, 3),
+    ("sa0", 0, 2), ("x1", 0, 1), ("ud0", 0, 2), ("r", 1, 2), ("sm0", 0, 1), ("sm0", 0, 0),
+    ("ww", 1, 0), ("wr", 4, 0), ("nq1", 0, 0), ("wr", 4, 1), ("r", 1, 3), ("nq1", 0, 1),
+    ("at1", 3, 1), ("at1", 3, 0), ("op1", 0, 1), ("sm0", 0, 2), ("op1", 0, 0), ("wr", 5, 2),
+    ("nq1", 0, 2), ("r", 2, 1), ("sm0", 0, 3), ("at1", 3, 2), ("op1", 0, 2), ("x1", 0, 2),
+    ("r", 2, 0), ("wr", 4, 3), ("nq1", 0, 3), ("at1", 3, 3), ("wr", 5, 1), ("op1", 0, 3),
+    ("r", 2, 2), ("r", 2, 3), ("wr", 5, 0), ("sa1", 0, 0), ("ww", 1, 1), ("sa1", 0, 1),
+    ("sa1", 0, 2), ("ww", 1, 2), ("ud1", 0, 1), ("ud1", 0, 2), ("sa1", 0, 3), ("hu1", 0, 1),
+    ("r", 3, 1), ("ud1", 0, 3), ("hu1", 0, 2), ("r", 3, 2), ("r", 3, 3), ("ud1", 0, 0),
+    ("hu1", 0, 3), ("hu1", 0, 0), ("wg12", 0, 1), ("sm1", 0, 3), ("r", 4, 3), ("r", 3, 0),
+    ("wg12", 0, 0), ("sm1", 0, 1), ("wg11", 0, 1), ("r", 4, 1), ("sd1", 0, 3), ("gp1", 2, 2),
+    ("sm1", 0, 2), ("sm1", 0, 0), ("r", 4, 2), ("ag1", 0, 3), ("gp1", 2, 3), ("ab1", 3, 3),
+    ("gp1", 2, 0), ("qb1", 0, 3), ("sd1", 0, 2), ("r", 4, 0), ("wg11", 0, 0), ("gp1", 2, 1),
+    ("sd1", 0, 1), ("r", 5, 3), ("ag1", 0, 2), ("ab1", 3, 2), ("gp1", 1, 3), ("qb1", 0, 2),
+    ("ag1", 0, 1), ("sd1", 0, 0), ("ab1", 3, 1), ("r", 5, 2), ("qb1", 0, 1), ("sb1", 0, 3),
+    ("ag1", 0, 0), ("ab1", 3, 0), ("gp1", 1, 2), ("qb1", 0, 0), ("r", 5, 1), ("wg10", 0, 1),
+    ("gp1", 1, 0), ("hu0", 0, 3), ("wg10", 0, 0), ("gp1", 1, 1), ("sb1", 0, 2), ("r", 5, 0),
+    ("r", 6, 3), ("sb1", 0, 1), ("hu0", 0, 2), ("gp1", 0, 3), ("sb1", 0, 0), ("hu0", 0, 1),
+    ("gp1", 0, 2), ("hu0", 0, 0), ("wg02", 0, 0), ("gp1", 0, 0), ("sd0", 0, 3), ("wg02", 0, 1),
+    ("r", 6, 2), ("wg01", 0, 0), ("gp1", 0, 1), ("ag0", 0, 3), ("ab0", 3, 3), ("r", 6, 1),
+    ("sd0", 0, 2), ("qb0", 0, 3), ("gp0", 2, 0), ("r", 6, 0), ("ag0", 0, 2), ("ab0", 3, 2),
+    ("wg01", 0, 1), ("qb0", 0, 2), ("gp0", 2, 3), ("sd0", 0, 1), ("gp0", 2, 1), ("gp0", 2, 2),
+    ("gf", 2, 1), ("r", 7, 3), ("r", 7, 2), ("ag0", 0, 1), ("sd0", 0, 0), ("ab0", 3, 1),
+    ("qb0", 0, 1), ("gp0", 1, 1), ("gp0", 1, 0), ("ag0", 0, 0), ("ab0", 3, 0), ("sb0", 0, 2),
+    ("gf", 1, 1), ("qb0", 0, 0), ("gp0", 1, 3), ("wg00", 0, 0), ("gf", 0, 1), ("gp0", 1, 2),
+    ("r", 7, 0), ("wg00", 0, 1), ("r", 7, 1), ("sb0", 0, 1), ("sb0", 0, 0), ("gf", 1, 0),
+    ("sb0", 0, 3), ("gp0", 0, 1), ("gp0", 0, 0), ("gg0", 0, 0), ("gf", 2, 0), ("gp0", 0, 3),
+    ("gp0", 0, 2), ("gg1", 0, 0), ("gg2", 0, 0), ("gg3", 0, 0), ("gf", 0, 0),
 )
 
 
@@ -1081,6 +1081,65 @@
     )(*given.values())
 
 
+def pack_kernel(w_qkv, w_out, gains, own_a, gain_rows):
+    heads = w_qkv.shape[2] // HEAD
+    q, k, v = (w_qkv[i] for i in range(3))
+    columns = []
+    for h in range(heads):
+        here = slice(h * HEAD, (h + 1) * HEAD)
+        columns += [k[:, here], v[:, here]]
+    turned = w_out[...].astype(F32).T.astype(BF16)
+    own_a[...] = jnp.concatenate(columns + [q, turned], axis=1)
+    gain_rows[...] = jnp.zeros_like(gain_rows)
+    gain_rows[0:2, 0 : gains.shape[1]] = gains[...].astype(F32)
+
+
+def pack_weights(w_qkv, w_out, gains):
+    _, slab, columns = w_qkv.shape
+    in_vmem = pl.BlockSpec(memory_space=pltpu.VMEM)
+    return pl.pallas_call(
+        pack_kernel,
+        out_shape=(
+            jax.ShapeDtypeStruct((slab, 4 * columns), BF16),
+            jax.ShapeDtypeStruct((8, slab + -slab % 128), F32),
+        ),
+        in_specs=[in_vmem] * 3,
+        out_specs=(in_vmem,) * 2,
+        name="pack",
+    )(w_qkv, w_out, gains)
+
+
+def unpack_kernel(gsum, acts, igr, gain_part, *outs):
+    acts_out, igr_out, gain_out, qkv_out, out_out, up_out, down_out = outs
+    columns = qkv_out.shape[2]
+    heads = columns // HEAD
+    first = gsum[0]
+    kv = [first[:, i * HEAD : (i + 1) * HEAD] for i in range(2 * heads)]
+    qkv_out[0] = first[:, 2 * columns : 3 * columns]
+    qkv_out[1] = jnp.concatenate(kv[0::2], axis=1)
+    qkv_out[2] = jnp.concatenate(kv[1::2], axis=1)
+    out_out[0] = first[:, 3 * columns :].T
+    up_out[0] = gsum[1]
+    down_out[...] = gsum[2]
+    acts_out[0] = acts[...]
+    igr_out[0] = igr[...]
+    width, share = gain_part.shape[1], gain_out.shape[2]
+    at = lax.axis_index("tensor") * lax.axis_size("dp") + lax.axis_index("dp")
+    turned = pltpu.roll(gain_part[...], width - at * share, 1)
+    gain_out[0] = turned[0:2, 0:share]
+
+
+def unpack_results(total, acts, input_grads, gain_part, shapes):
+    in_vmem = pl.BlockSpec(memory_space=pltpu.VMEM)
+    return pl.pallas_call(
+        unpack_kernel,
+        out_shape=tuple(jax.ShapeDtypeStruct(shape, kind) for shape, kind in shapes),
+        in_specs=[in_vmem] * 4,
+        out_specs=(in_vmem,) * 7,
+        name="unpack",
+    )(total, acts, input_grads, gain_part)
+
+
 def shards(inputs, lengths, gains, w_qkv, w_out, w_up, w_down, cotangent):
     local_rows, width = inputs.shape[1:]
     slab = w_up.shape[1]
@@ -1089,24 +1148,47 @@
     y = lax.div(lax.axis_index("tensor"), 2)
     section = lax.axis_index("section")
     inside = slab % 16 == 0 and depth == 4
-    split = (slab, heads, HEAD)
-    kv = jnp.stack([w_qkv[0, :, 1].reshape(split), w_qkv[0, :, 2].reshape(split)], axis=2)
-    own = (
-        jnp.concatenate([kv.reshape(slab, -1), w_qkv[0, :, 0], w_out[0].T], axis=1),
-        w_up[0],
-        w_down[0].T,
-    )
     axes = ("section", "tensor")
     if inside:
-        gain_rows = jnp.pad(gains[0].astype(F32), ((0, 6), (0, -slab % 128)))
+        own_a, gain_rows = pack_weights(w_qkv[0].transpose(1, 0, 2), w_out[0], gains[0])
+        own = (own_a, w_up[0], w_down[0].T)
         acts, input_grads, total, gain_part = run_blocks(
             inputs, cotangent, own, gain_rows, lengths, depth, inside
         )
-        gain_part = gain_part[None, :2]
-        at = lax.axis_index("tensor") * depth + lax.axis_index("dp")
-        share = width // (depth * lax.axis_size("tensor"))
-        gain_grads = lax.dynamic_slice_in_dim(gain_part, at * share, share, 2)
+        columns = heads * HEAD
+        results = unpack_results(
+            total,
+            acts,
+            input_grads,
+            gain_part,
+            (
+                ((1,) + acts.shape, BF16),
+                ((1,) + acts.shape, BF16),
+                ((1, 2, width // (depth * lax.axis_size("tensor"))), F32),
+                ((3, slab, columns), F32),
+                (w_out.shape, F32),
+                (w_up.shape, F32),
+                ((slab, width), F32),
+            ),
+        )
+        acts, input_grads, gain_grads, qkv_grads, out_grads, up_grads, down_grads = results
+        return (
+            acts,
+            input_grads,
+            gain_grads,
+            qkv_grads.transpose(1, 0, 2)[None],
+            out_grads,
+            up_grads,
+            down_grads.T[None],
+        )
     else:
+        split = (slab, heads, HEAD)
+        kv = jnp.stack([w_qkv[0, :, 1].reshape(split), w_qkv[0, :, 2].reshape(split)], axis=2)
+        own = (
+            jnp.concatenate([kv.reshape(slab, -1), w_qkv[0, :, 0], w_out[0].T], axis=1),
+            w_up[0],
+            w_down[0].T,
+        )
         whole = lax.all_gather(jnp.stack(own), "dp", axis=1, tiled=True)
         weights = []
         for l in range(2):

time: 235 us -> 229 us (0.974)
  local copies, waits for them, and re-layouts: 9.02 us -> 0 us
  Pallas kernels: 222 us -> 228 us
    pallas_call x0 -> x2, Pallas kernels: none -> 5.91 us  [the longest x1 3.96 us: unpack_results(): pl.pallas_call(unpack_kernel, out_shape=tuple((jax.ShapeDtypeStruct(shape...]
    unnamed x14 -> x0, local copies, waits for them, and re-layouts: 3.76 us -> none
    slice x5 -> x0, local copies, waits for them, and re-layouts: 3.05 us -> none  [the longest x2 1.14 us: shards(): kv = total[0, :, :2 * columns].reshape(slab, heads, 2, HEAD)]
where the time goes in v6:
time: 229 us
  Pallas kernels  228 us (100%)
    pallas_call x1, Pallas kernels, run_blocks(): pl.pallas_call(functools.partial(block_kernel, inside, STEPS, list(given)...  222 us

profile of v6, /device:TPU:0, one launch (start us, length us, event | category | flops | bytes accessed | tf_op | source)
XLA Modules:
  0.0 228.7 jit_solution(1191676117096904470)
XLA Ops:
  0.6 1.9 pack.1
  2.6 222.2 %blocks.1 = (bf16[2,256,768]{2,1,0:T(8,128)(2,1)}, bf16[2,256,768]{2,1,0:T(8,128)(2,1)}, f32[3,192,768]{2,1,0:T(8,128)}, f32[8,768]{1,0:T(8,128)}) custom-call(bf16[2,256,768]{2,1,0:T(8,128)(2,1)} %refs_0_.1, bf16[2,256,768]{2,1,0:T(8,128)(2,1)} %refs_1_.1, bf16[192,768]{1,0:T(8,128)(2,1)} %get-tuple-element.20.refs_2_, bf16[192,768]{1,0:T(8,128)(2,1)} %bitcast.20, ...), custom_call_target="tpu_custom_call" | custom-call | flops 27000000512 | bytes 40000000 | tf_op jit(solution)/shard_map/blocks/pallas_call | solution.py:1064
  224.8 4.0 %unpack.1 = (bf16[1,2,256,768]{3,2,1,0:T(8,128)(2,1)}, bf16[1,2,256,768]{3,2,1,0:T(8,128)(2,1)}, f32[1,2,48]{2,1,0:T(2,128)}, f32[3,192,192]{2,1,0:T(8,128)}, f3...) custom-call(f32[3,192,768]{2,1,0:T(8,128)} %get-tuple-element.22.gsum, ...), custom_call_target="tpu_custom_call" | custom-call | tf_op jit(solution)/shard_map/unpack/pallas_call | solution.py:1134

commit v7 on v6

--- a/solution.py
+++ b/solution.py
@@ -119,6 +119,20 @@
     def bytes_of(count):
         return n.PART.at[0, 0:count]
 
+    if inside:
+        q, k, v = (n.w_qkv[i] for i in range(3))
+        columns = []
+        for h in range(heads):
+            here = slice(h * HEAD, (h + 1) * HEAD)
+            columns += [k[:, here], v[:, here]]
+        turned = n.w_out[...].astype(F32).T.astype(BF16)
+        n.own_a[...] = jnp.concatenate(columns + [q, turned], axis=1)
+        n.OWN_GAINS[...] = jnp.zeros_like(n.OWN_GAINS)
+        n.OWN_GAINS[0:2, 0:slab] = n.gain_rows[...].astype(F32)
+
+    n.GACC[...] = jnp.zeros_like(n.GACC)
+    n.BIAS[...] = jnp.where(n.lengths[y] == rows_all, 0.0, MASKED) + jnp.zeros_like(n.BIAS)
+
     barrier = pltpu.get_barrier_semaphore()
     greeted = 0
     for other_s in range(2):
@@ -509,7 +523,7 @@
         n.GACC[l, 1:2, :] += jnp.sum(total * unit, axis=0, keepdims=True)
         gain = n.GAINS[2 * l + 1 : 2 * l + 2, :]
         grad = source[own, :].astype(F32) + norm_back(unit, scale, gain, total)
-        n.DMID[own_of(j), :] = grad
+        n.MID[l, own_of(j), :] = grad
         n.DA[l, own, :] = grad.astype(BF16)
         pair_start(PAIR_DA[l], n.DA.at[l], j)
 
@@ -589,7 +603,7 @@
         unit, scale = unit_rows(source[own_of(j), :].astype(F32))
         n.GACC[l, 0:1, :] += jnp.sum(total * unit, axis=0, keepdims=True)
         gain = n.GAINS[2 * l : 2 * l + 1, :]
-        return n.DMID[own_of(j), :] + norm_back(unit, scale, gain, total)
+        return n.MID[l, own_of(j), :] + norm_back(unit, scale, gain, total)
 
     def attn_back_sum(l, j):
         own = half_of(j, s)
@@ -724,20 +738,15 @@
             pltpu.make_async_copy(n.FIN.at[slot], n.gsum.at[p], n.fin_send.at[p]).start()
 
     def grads_done():
+        for i in range(2):
+            grad_sent(*grad_order[-1], i)
         if not inside:
-            for late in grad_order[-2:]:
-                grad_sent(*late, 0)
-                grad_sent(*late, 1)
             return
-        for late in grad_order[-2:]:
-            grad_sent(*late, 0)
-            grad_sent(*late, 1)
-        for p in range(PARTS):
-            for far in range(depth):
-
-                @pl.when(z != far)
-                def _():
-                    done(n.ZR.at[0, p], n.z_send.at[p, far])
+        for far in range(depth):
+
+            @pl.when(z != far)
+            def _():
+                done(n.ZR.at[0, 0], n.z_send.at[0, far])
 
         done(n.FIN.at[0], n.fin_send.at[0])
         done(n.FIN.at[1], n.fin_send.at[1])
@@ -746,14 +755,14 @@
         if not inside:
             n.GAINS[...] = n.gain_rows[...]
             return
-        n.GIN[s, z] = n.gain_rows[...]
+        n.GIN[s, z] = n.OWN_GAINS[...]
         for c in range(2):
             for far in range(depth):
 
                 @pl.when((s != c) | (z != far))
                 def _():
                     remote(
-                        n.gain_rows,
+                        n.OWN_GAINS,
                         n.GIN.at[s, z],
                         n.gin_send.at[c, far],
                         n.gin_recv.at[s, z],
@@ -768,8 +777,8 @@
 
                 @pl.when((s != c) | (z != far))
                 def _():
-                    done(n.gain_rows, n.gin_recv.at[c, far])
-                    done(n.gain_rows, n.gin_send.at[c, far])
+                    done(n.OWN_GAINS, n.gin_recv.at[c, far])
+                    done(n.OWN_GAINS, n.gin_send.at[c, far])
 
                 for k in range(2):
                     n.GAINS[2 * c + k : 2 * c + k + 1, far * slab : (far + 1) * slab] = n.GIN[
@@ -823,6 +832,43 @@
             @pl.when(z != far)
             def _():
                 done(n.GC, n.gg_send.at[2 + far])
+
+    def early_sends():
+        if inside:
+            for p in range(PARTS):
+                weights_sent(p)
+                for l in range(2):
+
+                    @pl.when(hub)
+                    def _():
+                        for far in range(depth):
+                            done(n.W.at[l, p, slab_of(far)], n.relay_send.at[l, p, far])
+
+                            @pl.when((z == 1) if far >= 2 else (z == 2))
+                            def _():
+                                done(n.W.at[l, p, slab_of(far)], n.onward_send.at[l, p, far])
+
+            for p in (1, 2):
+                for far in range(depth):
+
+                    @pl.when(z != far)
+                    def _():
+                        done(n.ZR.at[0, p], n.z_send.at[p, far])
+
+        spread_done(0)
+        spread_done(1)
+
+        @pl.loop(0, CHUNKS)
+        def _(j):
+            for stage in range(7):
+                done(bytes_of(part), n.pair_send.at[stage, j])
+            for which, section in ((1, 0), (2, 0), (3, 1)):
+                given_out(which, section, j)
+
+        for which, section in ((0, 1), (2, 0), (3, 1)):
+            got_out(which, section)
+        for i in range(2):
+            grad_sent(*grad_order[-2], i)
 
     tasks = {"none": lambda h, j: None}
     for l in range(2):
@@ -850,6 +896,7 @@
     tasks["ww"] = lambda h, j: weights_wait(h, j)
     for l in range(2):
         tasks[f"gp{l}"] = lambda h, j, l=l: grad_pass(l, h, j)
+    tasks["es"] = lambda h, j: early_sends()
     tasks["gf"] = lambda h, j: grad_final(j, h)
     for step in range(4):
         tasks[f"gg{step}"] = lambda h, j, step=step: gain_grads(step)
@@ -864,12 +911,10 @@
     weights_send(0, 0)
     gains_send()
     spread(0, n.inp, n.X0)
-    n.GACC[...] = jnp.zeros_like(n.GACC)
-    n.BIAS[...] = jnp.where(n.lengths[y] == rows_all, 0.0, MASKED) + jnp.zeros_like(n.BIAS)
-
-    group = 12
+
+    group = 6
     codes = [order.index(name) * 32 + h * 4 + j for name, h, j in steps]
-    codes += [0] * (-len(codes) % group)
+    codes = [0] * (-len(codes) % group) + codes
     pairs = [codes[i] + 4096 * codes[i + 1] for i in range(0, len(codes), 2)]
     per_group = group // 2
     groups = len(pairs) // per_group
@@ -903,32 +948,7 @@
                 code & 3,
             )
 
-    if inside:
-        for p in range(PARTS):
-            weights_sent(p)
-            for l in range(2):
-
-                @pl.when(hub)
-                def _():
-                    for far in range(depth):
-                        done(n.W.at[l, p, slab_of(far)], n.relay_send.at[l, p, far])
-
-                        @pl.when((z == 1) if far >= 2 else (z == 2))
-                        def _():
-                            done(n.W.at[l, p, slab_of(far)], n.onward_send.at[l, p, far])
-
-    spread_done(0)
-    spread_done(1)
-
-    @pl.loop(0, CHUNKS)
-    def _(j):
-        for stage in range(7):
-            done(bytes_of(part), n.pair_send.at[stage, j])
-        for which, section in ((1, 0), (2, 0), (3, 1)):
-            given_out(which, section, j)
-
-    for which, section in ((0, 1), (1, 0), (2, 0), (3, 1)):
-        got_out(which, section)
+    got_out(1, 0)
     grads_done()
     gain_grads_done()
 
@@ -970,7 +990,7 @@
     ("gf", 1, 1), ("qb0", 0, 0), ("gp0", 1, 3), ("wg00", 0, 0), ("gf", 0, 1), ("gp0", 1, 2),
     ("r", 7, 0), ("wg00", 0, 1), ("r", 7, 1), ("sb0", 0, 1), ("sb0", 0, 0), ("gf", 1, 0),
     ("sb0", 0, 3), ("gp0", 0, 1), ("gp0", 0, 0), ("gg0", 0, 0), ("gf", 2, 0), ("gp0", 0, 3),
-    ("gp0", 0, 2), ("gg1", 0, 0), ("gg2", 0, 0), ("gg3", 0, 0), ("gf", 0, 0),
+    ("gp0", 0, 2), ("gg1", 0, 0), ("gg2", 0, 0), ("gg3", 0, 0), ("es", 0, 0), ("gf", 0, 0),
 )
 
 
@@ -1003,7 +1023,6 @@
         GRADT=vmem((8, chunk), F32),
         DQT=vmem((heads, HEAD, chunk), F32),
         MID=vmem((2, CHUNKS * part, width), F32),
-        DMID=vmem((CHUNKS * part, width), F32),
         PART=vmem((2, rows, width), BF16),
         RC=vmem((2, CHUNKS, part, width), BF16),
         RX=vmem((3, CHUNKS, part, width), BF16),
@@ -1033,7 +1052,9 @@
             GR=vmem((2, PARTS, width, width), BF16),
             ZR=vmem((depth - 1, PARTS, slab, width), BF16),
             FIN=vmem((2, slab, width), F32),
-            GIN=vmem((2, depth) + gain_rows.shape, F32),
+            GIN=vmem((2, depth, 8, slab + -slab % 128), F32),
+            OWN_GAINS=vmem((8, slab + -slab % 128), F32),
+            own_a=vmem((slab, width), BF16),
             GC=vmem((8, width), F32),
             GX=vmem((8, width), F32),
             GY=vmem((8, width), F32),
@@ -1050,7 +1071,7 @@
             gg_send=dma((3 + depth,)),
             gg_recv=dma((4 + depth,)),
         )
-        own = dict(own_a=weights[0], own_b=weights[1], own_c=weights[2])
+        own = dict(w_qkv=weights[0], w_out=weights[1], own_b=weights[2], own_c=weights[3])
         outs["gsum"] = jax.ShapeDtypeStruct((PARTS, slab, width), F32)
     else:
         own = dict(w_whole=weights)
@@ -1059,7 +1080,7 @@
     given = dict(inp=inputs, cot=cotangent, **own, gain_rows=gain_rows, lengths=lengths)
     hbm = pl.BlockSpec(memory_space=pl.ANY)
     in_vmem = pl.BlockSpec(memory_space=pltpu.VMEM)
-    small = ("gain_rows", "gain_out")
+    small = ("gain_rows", "gain_out", "w_qkv", "w_out")
     in_smem = pl.BlockSpec(memory_space=pltpu.SMEM)
     return pl.pallas_call(
         functools.partial(
@@ -1081,34 +1102,6 @@
     )(*given.values())
 
 
-def pack_kernel(w_qkv, w_out, gains, own_a, gain_rows):
-    heads = w_qkv.shape[2] // HEAD
-    q, k, v = (w_qkv[i] for i in range(3))
-    columns = []
-    for h in range(heads):
-        here = slice(h * HEAD, (h + 1) * HEAD)
-        columns += [k[:, here], v[:, here]]
-    turned = w_out[...].astype(F32).T.astype(BF16)
-    own_a[...] = jnp.concatenate(columns + [q, turned], axis=1)
-    gain_rows[...] = jnp.zeros_like(gain_rows)
-    gain_rows[0:2, 0 : gains.shape[1]] = gains[...].astype(F32)
-
-
-def pack_weights(w_qkv, w_out, gains):
-    _, slab, columns = w_qkv.shape
-    in_vmem = pl.BlockSpec(memory_space=pltpu.VMEM)
-    return pl.pallas_call(
-        pack_kernel,
-        out_shape=(
-            jax.ShapeDtypeStruct((slab, 4 * columns), BF16),
-            jax.ShapeDtypeStruct((8, slab + -slab % 128), F32),
-        ),
-        in_specs=[in_vmem] * 3,
-        out_specs=(in_vmem,) * 2,
-        name="pack",
-    )(w_qkv, w_out, gains)
-
-
 def unpack_kernel(gsum, acts, igr, gain_part, *outs):
     acts_out, igr_out, gain_out, qkv_out, out_out, up_out, down_out = outs
     columns = qkv_out.shape[2]
@@ -1150,10 +1143,9 @@
     inside = slab % 16 == 0 and depth == 4
     axes = ("section", "tensor")
     if inside:
-        own_a, gain_rows = pack_weights(w_qkv[0].transpose(1, 0, 2), w_out[0], gains[0])
-        own = (own_a, w_up[0], w_down[0].T)
+        own = (w_qkv[0].transpose(1, 0, 2), w_out[0], w_up[0], w_down[0].T)
         acts, input_grads, total, gain_part = run_blocks(
-            inputs, cotangent, own, gain_rows, lengths, depth, inside
+            inputs, cotangent, own, gains[0], lengths, depth, inside
         )
         columns = heads * HEAD
         results = unpack_results(

time: 229 us -> 227 us (level)
  no operation moved by 1% of the time
where the time goes in v7:
time: 227 us
  Pallas kernels  226 us (100%)
    pallas_call x1, Pallas kernels, run_blocks(): pl.pallas_call(functools.partial(block_kernel, inside, STEPS, list(given)...  222 us

profile of v7, /device:TPU:0, one launch (start us, length us, event | category | flops | bytes accessed | tf_op | source)
XLA Modules:
  0.0 227.1 jit_solution(2437295245589406321)
XLA Ops:
  0.6 222.5 %blocks.1 = (bf16[2,256,768]{2,1,0:T(8,128)(2,1)}, bf16[2,256,768]{2,1,0:T(8,128)(2,1)}, f32[3,192,768]{2,1,0:T(8,128)}, f32[8,768]{1,0:T(8,128)}) custom-call(bf16[2,256,768]{2,1,0:T(8,128)(2,1)} %refs_0_.1, bf16[2,256,768]{2,1,0:T(8,128)(2,1)} %refs_1_.1, bf16[3,192,192]{2,1,0:T(8,128)(2,1)} %bitcast.17, bf16[192,192]{1,0:T(8,128)(2,1)} %bitcast.20, ...), custom_call_target="tpu_custom_call" | custom-call | flops 27000000512 | bytes 40000000 | tf_op jit(solution)/shard_map/blocks/pallas_call | solution.py:1085
  223.1 4.0 %unpack.1 = (bf16[1,2,256,768]{3,2,1,0:T(8,128)(2,1)}, bf16[1,2,256,768]{3,2,1,0:T(8,128)(2,1)}, f32[1,2,48]{2,1,0:T(2,128)}, f32[3,192,192]{2,1,0:T(8,128)}, f3...) custom-call(f32[3,192,768]{2,1,0:T(8,128)} %get-tuple-element.18.gsum, ...), custom_call_target="tpu_custom_call" | custom-call | tf_op jit(solution)/shard_map/unpack/pallas_call | solution.py:1127

commit v8 on v7

--- a/solution.py
+++ b/solution.py
@@ -954,43 +954,228 @@
 
 
 STEPS = (
-    ("cs", 0, 0), ("wt2", 0, 0), ("wt1", 0, 0), ("wr", 0, 0), ("xp", 0, 0), ("wr", 0, 1),
-    ("wr", 0, 2), ("gw", 0, 0), ("wr", 0, 3), ("x0", 0, 0), ("x0", 0, 1), ("wr", 2, 2),
-    ("x0", 0, 2), ("wr", 2, 0), ("cp", 0, 0), ("wr", 2, 1), ("ww", 0, 0), ("nq0", 0, 1),
-    ("nq0", 0, 0), ("at0", 3, 1), ("nq0", 0, 2), ("op0", 0, 1), ("wr", 1, 2), ("x0", 0, 3),
-    ("x1", 0, 3), ("at0", 3, 2), ("wr", 1, 0), ("wr", 1, 1), ("wr", 1, 3), ("op0", 0, 2),
-    ("ws0", 0, 0), ("at0", 3, 0), ("op0", 0, 0), ("nq0", 0, 3), ("wr", 2, 3), ("r", 0, 1),
-    ("r", 0, 2), ("r", 0, 0), ("at0", 3, 3), ("ws2", 0, 0), ("op0", 0, 3), ("wr", 3, 2),
-    ("wr", 3, 0), ("ws1", 0, 0), ("sa0", 0, 1), ("sa0", 0, 0), ("x1", 0, 0), ("ww", 0, 1),
-    ("wr", 3, 1), ("r", 0, 3), ("ww", 0, 2), ("ud0", 0, 0), ("wr", 3, 3), ("ud0", 0, 1),
-    ("r", 1, 0), ("sa0", 0, 3), ("wr", 4, 2), ("ud0", 0, 3), ("r", 1, 1), ("wr", 5, 3),
-    ("sa0", 0, 2), ("x1", 0, 1), ("ud0", 0, 2), ("r", 1, 2), ("sm0", 0, 1), ("sm0", 0, 0),
-    ("ww", 1, 0), ("wr", 4, 0), ("nq1", 0, 0), ("wr", 4, 1), ("r", 1, 3), ("nq1", 0, 1),
-    ("at1", 3, 1), ("at1", 3, 0), ("op1", 0, 1), ("sm0", 0, 2), ("op1", 0, 0), ("wr", 5, 2),
-    ("nq1", 0, 2), ("r", 2, 1), ("sm0", 0, 3), ("at1", 3, 2), ("op1", 0, 2), ("x1", 0, 2),
-    ("r", 2, 0), ("wr", 4, 3), ("nq1", 0, 3), ("at1", 3, 3), ("wr", 5, 1), ("op1", 0, 3),
-    ("r", 2, 2), ("r", 2, 3), ("wr", 5, 0), ("sa1", 0, 0), ("ww", 1, 1), ("sa1", 0, 1),
-    ("sa1", 0, 2), ("ww", 1, 2), ("ud1", 0, 1), ("ud1", 0, 2), ("sa1", 0, 3), ("hu1", 0, 1),
-    ("r", 3, 1), ("ud1", 0, 3), ("hu1", 0, 2), ("r", 3, 2), ("r", 3, 3), ("ud1", 0, 0),
-    ("hu1", 0, 3), ("hu1", 0, 0), ("wg12", 0, 1), ("sm1", 0, 3), ("r", 4, 3), ("r", 3, 0),
-    ("wg12", 0, 0), ("sm1", 0, 1), ("wg11", 0, 1), ("r", 4, 1), ("sd1", 0, 3), ("gp1", 2, 2),
-    ("sm1", 0, 2), ("sm1", 0, 0), ("r", 4, 2), ("ag1", 0, 3), ("gp1", 2, 3), ("ab1", 3, 3),
-    ("gp1", 2, 0), ("qb1", 0, 3), ("sd1", 0, 2), ("r", 4, 0), ("wg11", 0, 0), ("gp1", 2, 1),
-    ("sd1", 0, 1), ("r", 5, 3), ("ag1", 0, 2), ("ab1", 3, 2), ("gp1", 1, 3), ("qb1", 0, 2),
-    ("ag1", 0, 1), ("sd1", 0, 0), ("ab1", 3, 1), ("r", 5, 2), ("qb1", 0, 1), ("sb1", 0, 3),
-    ("ag1", 0, 0), ("ab1", 3, 0), ("gp1", 1, 2), ("qb1", 0, 0), ("r", 5, 1), ("wg10", 0, 1),
-    ("gp1", 1, 0), ("hu0", 0, 3), ("wg10", 0, 0), ("gp1", 1, 1), ("sb1", 0, 2), ("r", 5, 0),
-    ("r", 6, 3), ("sb1", 0, 1), ("hu0", 0, 2), ("gp1", 0, 3), ("sb1", 0, 0), ("hu0", 0, 1),
-    ("gp1", 0, 2), ("hu0", 0, 0), ("wg02", 0, 0), ("gp1", 0, 0), ("sd0", 0, 3), ("wg02", 0, 1),
-    ("r", 6, 2), ("wg01", 0, 0), ("gp1", 0, 1), ("ag0", 0, 3), ("ab0", 3, 3), ("r", 6, 1),
-    ("sd0", 0, 2), ("qb0", 0, 3), ("gp0", 2, 0), ("r", 6, 0), ("ag0", 0, 2), ("ab0", 3, 2),
-    ("wg01", 0, 1), ("qb0", 0, 2), ("gp0", 2, 3), ("sd0", 0, 1), ("gp0", 2, 1), ("gp0", 2, 2),
-    ("gf", 2, 1), ("r", 7, 3), ("r", 7, 2), ("ag0", 0, 1), ("sd0", 0, 0), ("ab0", 3, 1),
-    ("qb0", 0, 1), ("gp0", 1, 1), ("gp0", 1, 0), ("ag0", 0, 0), ("ab0", 3, 0), ("sb0", 0, 2),
-    ("gf", 1, 1), ("qb0", 0, 0), ("gp0", 1, 3), ("wg00", 0, 0), ("gf", 0, 1), ("gp0", 1, 2),
-    ("r", 7, 0), ("wg00", 0, 1), ("r", 7, 1), ("sb0", 0, 1), ("sb0", 0, 0), ("gf", 1, 0),
-    ("sb0", 0, 3), ("gp0", 0, 1), ("gp0", 0, 0), ("gg0", 0, 0), ("gf", 2, 0), ("gp0", 0, 3),
-    ("gp0", 0, 2), ("gg1", 0, 0), ("gg2", 0, 0), ("gg3", 0, 0), ("es", 0, 0), ("gf", 0, 0),
+    ("cs", 0, 0),
+    ("wt2", 0, 0),
+    ("wt1", 0, 0),
+    ("wr", 0, 0),
+    ("xp", 0, 0),
+    ("wr", 0, 1),
+    ("wr", 0, 2),
+    ("gw", 0, 0),
+    ("wr", 0, 3),
+    ("x0", 0, 0),
+    ("x0", 0, 1),
+    ("wr", 2, 2),
+    ("x0", 0, 2),
+    ("wr", 2, 0),
+    ("cp", 0, 0),
+    ("wr", 2, 1),
+    ("ww", 0, 0),
+    ("nq0", 0, 1),
+    ("nq0", 0, 0),
+    ("at0", 3, 1),
+    ("nq0", 0, 2),
+    ("op0", 0, 1),
+    ("wr", 1, 2),
+    ("x0", 0, 3),
+    ("x1", 0, 3),
+    ("at0", 3, 2),
+    ("wr", 1, 0),
+    ("wr", 1, 1),
+    ("wr", 1, 3),
+    ("op0", 0, 2),
+    ("ws0", 0, 0),
+    ("at0", 3, 0),
+    ("op0", 0, 0),
+    ("nq0", 0, 3),
+    ("wr", 2, 3),
+    ("r", 0, 1),
+    ("r", 0, 2),
+    ("r", 0, 0),
+    ("at0", 3, 3),
+    ("ws2", 0, 0),
+    ("op0", 0, 3),
+    ("wr", 3, 2),
+    ("wr", 3, 0),
+    ("ws1", 0, 0),
+    ("sa0", 0, 1),
+    ("sa0", 0, 0),
+    ("x1", 0, 0),
+    ("ww", 0, 1),
+    ("wr", 3, 1),
+    ("r", 0, 3),
+    ("ww", 0, 2),
+    ("ud0", 0, 0),
+    ("wr", 3, 3),
+    ("ud0", 0, 1),
+    ("r", 1, 0),
+    ("sa0", 0, 3),
+    ("wr", 4, 2),
+    ("ud0", 0, 3),
+    ("r", 1, 1),
+    ("wr", 5, 3),
+    ("sa0", 0, 2),
+    ("x1", 0, 1),
+    ("ud0", 0, 2),
+    ("r", 1, 2),
+    ("sm0", 0, 1),
+    ("sm0", 0, 0),
+    ("ww", 1, 0),
+    ("wr", 4, 0),
+    ("nq1", 0, 0),
+    ("wr", 4, 1),
+    ("r", 1, 3),
+    ("nq1", 0, 1),
+    ("at1", 3, 1),
+    ("at1", 3, 0),
+    ("op1", 0, 1),
+    ("sm0", 0, 2),
+    ("op1", 0, 0),
+    ("wr", 5, 2),
+    ("nq1", 0, 2),
+    ("r", 2, 1),
+    ("sm0", 0, 3),
+    ("at1", 3, 2),
+    ("op1", 0, 2),
+    ("x1", 0, 2),
+    ("r", 2, 0),
+    ("wr", 4, 3),
+    ("nq1", 0, 3),
+    ("at1", 3, 3),
+    ("wr", 5, 1),
+    ("op1", 0, 3),
+    ("r", 2, 2),
+    ("r", 2, 3),
+    ("wr", 5, 0),
+    ("sa1", 0, 0),
+    ("ww", 1, 1),
+    ("sa1", 0, 1),
+    ("sa1", 0, 2),
+    ("ww", 1, 2),
+    ("ud1", 0, 1),
+    ("ud1", 0, 2),
+    ("sa1", 0, 3),
+    ("hu1", 0, 1),
+    ("r", 3, 1),
+    ("ud1", 0, 3),
+    ("hu1", 0, 2),
+    ("r", 3, 2),
+    ("r", 3, 3),
+    ("ud1", 0, 0),
+    ("hu1", 0, 3),
+    ("hu1", 0, 0),
+    ("wg12", 0, 1),
+    ("sm1", 0, 3),
+    ("r", 4, 3),
+    ("r", 3, 0),
+    ("wg12", 0, 0),
+    ("sm1", 0, 1),
+    ("wg11", 0, 1),
+    ("r", 4, 1),
+    ("sd1", 0, 3),
+    ("gp1", 2, 2),
+    ("sm1", 0, 2),
+    ("sm1", 0, 0),
+    ("r", 4, 2),
+    ("ag1", 0, 3),
+    ("gp1", 2, 3),
+    ("ab1", 3, 3),
+    ("gp1", 2, 0),
+    ("qb1", 0, 3),
+    ("sd1", 0, 2),
+    ("r", 4, 0),
+    ("wg11", 0, 0),
+    ("gp1", 2, 1),
+    ("sd1", 0, 1),
+    ("r", 5, 3),
+    ("ag1", 0, 2),
+    ("ab1", 3, 2),
+    ("gp1", 1, 3),
+    ("qb1", 0, 2),
+    ("ag1", 0, 1),
+    ("sd1", 0, 0),
+    ("ab1", 3, 1),
+    ("r", 5, 2),
+    ("qb1", 0, 1),
+    ("sb1", 0, 3),
+    ("ag1", 0, 0),
+    ("ab1", 3, 0),
+    ("gp1", 1, 2),
+    ("qb1", 0, 0),
+    ("r", 5, 1),
+    ("wg10", 0, 1),
+    ("gp1", 1, 0),
+    ("hu0", 0, 3),
+    ("wg10", 0, 0),
+    ("gp1", 1, 1),
+    ("sb1", 0, 2),
+    ("r", 5, 0),
+    ("r", 6, 3),
+    ("sb1", 0, 1),
+    ("hu0", 0, 2),
+    ("gp1", 0, 3),
+    ("sb1", 0, 0),
+    ("hu0", 0, 1),
+    ("gp1", 0, 2),
+    ("hu0", 0, 0),
+    ("wg02", 0, 0),
+    ("gp1", 0, 0),
+    ("sd0", 0, 3),
+    ("wg02", 0, 1),
+    ("r", 6, 2),
+    ("wg01", 0, 0),
+    ("gp1", 0, 1),
+    ("ag0", 0, 3),
+    ("ab0", 3, 3),
+    ("r", 6, 1),
+    ("sd0", 0, 2),
+    ("qb0", 0, 3),
+    ("gp0", 2, 0),
+    ("r", 6, 0),
+    ("ag0", 0, 2),
+    ("ab0", 3, 2),
+    ("wg01", 0, 1),
+    ("qb0", 0, 2),
+    ("gp0", 2, 3),
+    ("sd0", 0, 1),
+    ("gp0", 2, 1),
+    ("gp0", 2, 2),
+    ("gf", 2, 1),
+    ("r", 7, 3),
+    ("r", 7, 2),
+    ("ag0", 0, 1),
+    ("sd0", 0, 0),
+    ("ab0", 3, 1),
+    ("qb0", 0, 1),
+    ("gp0", 1, 1),
+    ("gp0", 1, 0),
+    ("ag0", 0, 0),
+    ("ab0", 3, 0),
+    ("sb0", 0, 2),
+    ("gf", 1, 1),
+    ("qb0", 0, 0),
+    ("wg00", 0, 0),
+    ("wg00", 0, 1),
+    ("r", 7, 0),
+    ("r", 7, 1),
+    ("gp0", 1, 3),
+    ("gp0", 1, 2),
+    ("sb0", 0, 1),
+    ("sb0", 0, 0),
+    ("sb0", 0, 3),
+    ("gg0", 0, 0),
+    ("gf", 0, 1),
+    ("gp0", 0, 1),
+    ("gp0", 0, 0),
+    ("gg1", 0, 0),
+    ("gp0", 0, 3),
+    ("gg2", 0, 0),
+    ("gp0", 0, 2),
+    ("gg3", 0, 0),
+    ("gf", 2, 0),
+    ("gf", 1, 0),
+    ("es", 0, 0),
+    ("gf", 0, 0),
 )
 
 

time: 227 us -> 225 us (level)
  Pallas kernels: 226 us -> 222 us
    pallas_call x1, Pallas kernels: 222 us -> 218 us  [run_blocks(): pl.pallas_call(functools.partial(block_kernel, inside, STEPS, list(given)...]
where the time goes in v8:
time: 225 us; the launch traced here: 223 us
  Pallas kernels  222 us (99%)
    pallas_call x1, Pallas kernels, run_blocks(): pl.pallas_call(functools.partial(block_kernel, inside, STEPS, list(given)...  218 us

profile of v8, /device:TPU:0, one launch (start us, length us, event | category | flops | bytes accessed | tf_op | source)
XLA Modules:
  0.0 223.0 jit_solution(16288596021525055136)
XLA Ops:
  0.6 218.4 %blocks.1 = (bf16[2,256,768]{2,1,0:T(8,128)(2,1)}, bf16[2,256,768]{2,1,0:T(8,128)(2,1)}, f32[3,192,768]{2,1,0:T(8,128)}, f32[8,768]{1,0:T(8,128)}) custom-call(bf16[2,256,768]{2,1,0:T(8,128)(2,1)} %refs_0_.1, bf16[2,256,768]{2,1,0:T(8,128)(2,1)} %refs_1_.1, bf16[3,192,192]{2,1,0:T(8,128)(2,1)} %bitcast.17, bf16[192,192]{1,0:T(8,128)(2,1)} %bitcast.20, ...), custom_call_target="tpu_custom_call" | custom-call | flops 27000000512 | bytes 40000000 | tf_op jit(solution)/shard_map/blocks/pallas_call | solution.py:1270
  219.1 4.0 %unpack.1 = (bf16[1,2,256,768]{3,2,1,0:T(8,128)(2,1)}, bf16[1,2,256,768]{3,2,1,0:T(8,128)(2,1)}, f32[1,2,48]{2,1,0:T(2,128)}, f32[3,192,192]{2,1,0:T(8,128)}, f3...) custom-call(f32[3,192,768]{2,1,0:T(8,128)} %get-tuple-element.18.gsum, ...), custom_call_target="tpu_custom_call" | custom-call | tf_op jit(solution)/shard_map/unpack/pallas_call | solution.py:1312
